TPU v7x, 32 devices: a whole 2x2x4 slice. The times are simulated.
32 devices in a mesh: grp: 2 (over y), space: 16 (over z, x, core).
Axes of the slice: x: 2, y: 2, z: 4, core: 2. Of those that a mesh axis runs over, the one named last changes fastest.
Arguments:
- snapshots: bfloat16 [2048, 3, 2048], P(('grp', 'space')), parts along dimension 0, may hold values from -6 to 6
- weights: float32 [4096], P(('grp', 'space')), parts along dimension 0, may hold values from 0.5 to 20, as said below
Outputs:
- spod_matrix: float32 [32, 30, 30], P('grp'), parts along dimension 0
There are 2 independent parts, one for each index of `grp`. A program takes and returns all parts, laid end to end along the dimension named above; each array names one. Nothing has to cross between parts.
Inputs may be any that keep to these rules, and one draw needn't show every extreme that they name: Positive quadrature weights.
All inputs are finite; a program needn't handle non-finite values.
Results may differ from a plain program's by a relative error of at most 0.0003.
Values may be sent and summed in bfloat16 or wider, within the bound.
No kernel may reach another device: no remote copies, remote signals or barrier semaphores. Data moves between devices by JAX's collectives and lax.ppermute only.
A program may use at most 128 MiB of HBM per device.

v0:
```python
import jax
import jax.numpy as jnp
from jax import lax
from jax.sharding import PartitionSpec as P

NFFT = 128
NB = 15
NF = 16


def dft_rows():
    phase = jnp.arange(NFFT, dtype=jnp.int32)
    freqs = jnp.arange(1, NF + 1, dtype=jnp.int32)
    window = 0.5 - 0.5 * jnp.cos(2.0 * jnp.pi * phase.astype(jnp.float32) / NFFT)
    norm = jnp.sqrt(jnp.sum(window * window))
    turns = (freqs[:, None] * phase[None, :] % NFFT).astype(jnp.float32) * (2.0 * jnp.pi / NFFT)
    scaled = (window / norm)[None, :]
    return jnp.concatenate([jnp.cos(turns) * scaled, -jnp.sin(turns) * scaled], axis=0)


def spectral(block):
    steps_all = block.shape[0]
    components = block.shape[1]
    points = block.shape[2]
    rows = components * points
    half = NFFT // 2
    signal = block.astype(jnp.float32).reshape(steps_all, rows)
    signal = signal - jnp.mean(signal, axis=0, keepdims=True)
    halves = signal.reshape(NB + 1, half, rows)
    dft_table = dft_rows()
    front_part = jnp.einsum(
        "kj,hjr->khr", dft_table[:, :half], halves, precision=lax.Precision.HIGHEST
    )
    back_part = jnp.einsum(
        "kj,hjr->khr", dft_table[:, half:], halves, precision=lax.Precision.HIGHEST
    )
    spectra = front_part[:, :-1] + back_part[:, 1:]
    spectra = spectra.reshape(2, NF, NB, rows)
    spectra = jnp.transpose(spectra, (1, 0, 2, 3))
    return spectra.reshape(NF, 2 * NB, components, points)


def local(snapshots, weights):
    spectra = spectral(lax.all_to_all(snapshots, "space", split_axis=2, concat_axis=0, tiled=True))
    weighted = spectra * weights[None, None, None, :]
    local_gram = jnp.einsum("fbcp,fdcp->fbd", weighted, spectra, precision=lax.Precision.HIGHEST)
    weight_part = jnp.sum(weights)
    summed, weight_sum = lax.psum((local_gram, weight_part), "space")
    return summed / weight_sum


def solution(mesh):
    in_specs = (P(("grp", "space"), None, None), P(("grp", "space")))
    out_specs = P("grp", None, None)
    return jax.shard_map(local, mesh=mesh, in_specs=in_specs, out_specs=out_specs, check_vma=False)
```

profile of v0, /device:TPU:0, one launch (start us, length us, event | category | flops | bytes accessed | tf_op | source)
XLA Modules:
  0.0 116.0 jit_solution(1502312128846091476)
XLA Ops:
  0.0 2.8 %copy.35 = bf16[64,3,2048]{0,1,2:T(4,128)(2,1)S(1)} copy(bf16[64,3,2048]{2,0,1:T(8,128)(2,1)} %param.2) | data formatting | bytes 1572864 | tf_op args[0]
  2.9 0.0 copy-start
  2.9 2.5 %reshape.52 = bf16[16,2,12288]{2,1,0:T(2,128)(2,1)} reshape(bf16[2048,3,64]{2,1,0:T(4,128)(2,1)S(1)} %bitcast.27) | data formatting | bytes 1572864
  5.3 7.4 %all-to-all-start = ((bf16[16,2,12288]{2,1,0:T(2,128)(2,1)}), bf16[16,2,12288]{2,1,0:T(2,128)(2,1)S(1)}, u32[]{:S(2)}, u32[]{:S(2)}) async-start(bf16[16,2,12288]{2,1,0:T(2,128)(2,1)} %reshape.52), calls=%async_computation | async-start | bytes 1572864 | tf_op jit(solution)/shard_map/all_to_all | solution.py:44
  12.7 0.6 multiply_reduce_fusion
  14.0 0.0 copy-done
  14.0 0.6 reduce_sum.38
  14.7 0.1 cosine_multiply_fusion
  14.8 16.6 %all-to-all-done = bf16[16,2,12288]{2,1,0:T(2,128)(2,1)S(1)} async-done(((bf16[16,2,12288]{2,1,0:T(2,128)(2,1)}), bf16[16,2,12288]{2,1,0:T(2,128)(2,1)S(1)}, u32[]{:S(2)}, u32[]{:S(2)}) %all-to-all-start) | async-done | bytes 786464 | tf_op jit(solution)/shard_map/all_to_all | solution.py:44
  31.4 1.3 %reshape.53 = bf16[2048,3,64]{2,1,0:T(4,128)(2,1)S(1)} reshape(bf16[16,2,12288]{2,1,0:T(2,128)(2,1)S(1)} %all-to-all-done) | data formatting | bytes 1572864
  32.7 3.5 %convert_reduce_fusion = f32[3,2048]{0,1:T(8,128)S(1)} fusion(bf16[2048,3,64]{2,1,0:T(4,128)(2,1)S(1)} %reshape.53), kind=kLoop, calls=%fused_computation.6 | loop fusion | flops 780288 | bytes 811008 | tf_op jit(solution)/shard_map/reduce_sum | solution.py:28
  36.1 0.1 reduce_sum.37
  36.2 0.1 copy.43
  36.3 2.4 %copy.36 = f32[64,3,16,128]{3,1,0,2:T(4,128)} copy(bf16[64,3,16,128]{0,1,3,2:T(4,128)(2,1)S(1)} %bitcast.25) | data formatting | bytes 2359296 | tf_op jit(solution)/shard_map/convert_element_type | solution.py:27
  38.7 2.8 %reshape.47 = f32[16,64,384]{2,1,0:T(8,128)S(1)} reshape(f32[16,64,3,128]{3,2,1,0:T(4,128)} %bitcast.26) | data formatting | bytes 3145728 | tf_op jit(solution)/shard_map/convert_element_type | solution.py:27
  41.4 3.3 %fusion = f32[32,15,384]{2,0,1:T(8,128)S(1)} fusion(f32[16,64,384]{2,1,0:T(8,128)S(1)} %reshape.47, f32[384]{0:T(512)S(1)} %bitcast.31, f32[16,128]{1,0:T(8,128)S(1)} %get-tuple-element.8, f32[16,128]{1,0:T(8,128)S(1)} %get-tuple-element.7), kind=kOutput, calls=%fused_computation | convolution fusion | flops 141953024 | bytes 2328064 | tf_op jit(solution)/shard_map/slice | solution.py:37
  44.7 3.3 %fusion.4 = f32[32,15,384]{2,0,1:T(8,128)S(1)} fusion(f32[32,15,384]{2,0,1:T(8,128)S(1)} %fusion, f32[16,64,384]{2,1,0:T(8,128)S(1)} %reshape.47, f32[384]{0:T(512)S(1)} %bitcast.32, f32[16,128]{1,0:T(8,128)S(1)} %get-tuple-element.8, f32[16,128]{1,0:T(8,128)S(1)} %get-tuple-element.7), kind=kOutput, calls=%fused_computation.4 | convolution fusion | flops 142137344 | bytes 3065344 | tf_op jit(solution)/shard_map/slice | solution.py:37
  48.0 0.3 reshape.46
  48.3 0.3 broadcast_multiply_fusion
  48.6 1.8 %convolution_bitcast_fusion = f32[16,30,30]{2,1,0:T(8,128)S(1)} fusion(f32[16,30,3,128]{3,2,0,1:T(4,128)S(1)} %reshape.46, f32[16,30,3,128]{3,2,0,1:T(4,128)S(1)} %broadcast_multiply_fusion), kind=kOutput, calls=%fused_computation.5 | convolution fusion | flops 66355200 | bytes 1532160 | tf_op jit(solution)/shard_map/fbcp,fdcp->fbd/dot_general | solution.py:46
  50.4 0.1 copy.41
  50.6 64.0 %all-reduce = (f32[16,30,30]{2,0,1:T(8,128)S(1)}, f32[]{:T(128)}) all-reduce(f32[16,30,30]{2,0,1:T(8,128)S(1)} %copy.41, f32[]{:T(128)} %reduce_sum.38), channel_id=1, replica_groups=mesh['grp'=2,'space'=16] {'space'}, use_global_device_ids=true, to_apply=%region_3.4 | all-reduce | flops 14401 | bytes 115208 | tf_op jit(solution)/shard_map/psum | solution.py:48
  114.6 1.4 %broadcast_divide_fusion = f32[16,30,30]{2,0,1:T(8,128)} fusion(f32[16,30,30]{2,0,1:T(8,128)S(1)} %get-tuple-element.5, f32[]{:T(128)} %get-tuple-element.6), kind=kLoop, calls=%fused_computation.13 | loop fusion | flops 14400 | bytes 115204 | tf_op jit(solution)/shard_map/div | solution.py:49
  (4 shorter events, 0.1 us)
Async XLA Ops:
  2.9 11.2 %copy-start = (f32[128]{0:T(128)S(1)}, f32[128]{0:T(128)}, u32[]{:S(2)}) copy-start(f32[128]{0:T(128)} %param.3) | copy-start | bytes 1540
  5.3 26.1 %all-to-all-start = ((bf16[16,2,12288]{2,1,0:T(2,128)(2,1)}), bf16[16,2,12288]{2,1,0:T(2,128)(2,1)S(1)}, u32[]{:S(2)}, u32[]{:S(2)}) async-start(bf16[16,2,12288]{2,1,0:T(2,128)(2,1)} %reshape.52), calls=%async_computation | async-start | bytes 1572864 | tf_op jit(solution)/shard_map/all_to_all | solution.py:44
where the time goes:
time: 116 us
  blocking collectives  64 us (55%)
  waiting for transfers between devices  16.6 us (14%)
  local copies, waits for them, and re-layouts  12.2 us (11%)
  matrix products  8.33 us (7%)
  starting transfers between devices  7.36 us (6%)
  other arithmetic  6.67 us (6%)
    psum x1, blocking collectives, local(): summed, weight_sum = lax.psum((local_gram, weight_part), 'space')  64 us
    all_to_all x1, waiting for transfers between devices, local(): lax.all_to_all(snapshots, 'space', split_axis=2, concat_axis=0, tiled=True)  16.6 us
    all_to_all x1, starting transfers between devices, local(): lax.all_to_all(snapshots, 'space', split_axis=2, concat_axis=0, tiled=True)  7.36 us
    unnamed x6, local copies, waits for them, and re-layouts  6.64 us
    slice x2, matrix products, spectral(): spectra = front_part[:, :-1] + back_part[:, 1:]  6.52 us
    convert_element_type x2, local copies, waits for them, and re-layouts, spectral(): signal = block.astype(jnp.float32).reshape(steps_all, rows)  5.11 us
    reduce_sum x2, other arithmetic, spectral(): signal = signal - jnp.mean(signal, axis=0, keepdims=True)  3.54 us
  transfers between devices with their start and end apart: 1, of which 1 were waited for; matrix products, arithmetic and copies ran while one was open for 1% of the time, Pallas kernels for 0%

commit v1 on v0

v1 whole, which is shorter than its diff:
```python
import numpy as np
import ml_dtypes
import jax
import jax.numpy as jnp
from jax import lax
from jax.experimental import pallas as pl
from jax.experimental.pallas import tpu as pltpu
from jax.sharding import PartitionSpec as P

NFFT = 128
NB = 15
NF = 16
HALF = NFFT // 2
NH = NB + 1
LANES = 128
ROWS = 40
VMEM = 48 * 1024 * 1024


def half_table():
    turns = 2.0 * np.pi * np.arange(NF + 2)[:, None] * np.arange(HALF)[None, :] / NFFT
    re, im = np.cos(turns), -np.sin(turns)
    offset_re, offset_im = re.sum(1), im.sum(1)
    re0, im0 = re - re.mean(1, keepdims=True), im - im.mean(1, keepdims=True)
    table = np.zeros((ROWS, HALF))
    table[0:NF] = re0[1 : NF + 1]
    table[NF : 2 * NF] = im0[1 : NF + 1]
    table[32] = 1.0
    table[35] = re0[NF + 1]
    table[36] = im0[NF + 1]
    offsets = np.zeros((ROWS, 1))
    offsets[0:NF, 0] = offset_re[1 : NF + 1]
    offsets[NF : 2 * NF, 0] = offset_im[1 : NF + 1]
    offsets[35, 0] = offset_re[NF + 1]
    offsets[36, 0] = offset_im[NF + 1]
    return table, offsets.astype(np.float32)


def pieces(table, count):
    out, rest = [], table.astype(np.float64)
    for _ in range(count):
        part = rest.astype(np.float32).astype(ml_dtypes.bfloat16)
        out.append(part)
        rest = rest - part.astype(np.float64)
    return np.concatenate(out, axis=0)


def spectra_gram(halves, means, root, out_ref, tall_ref, offsets, steps_all):
    width = root.shape[1]
    total = means(0)
    for h in range(1, NH):
        total = total + means(h)
    mean = total * (1.0 / steps_all)
    freq = lax.broadcasted_iota(jnp.int32, (NF, 1), 0)
    sign = (2 * (freq & 1) - 1).astype(jnp.float32)
    lane = lax.broadcasted_iota(jnp.int32, (1, width), 1)
    held = None
    for h in range(NH):
        delta = means(h) * (1.0 / HALF) - mean
        rows = halves(h) + offsets * delta
        delta, rows = delta * root, rows * root
        re, im = rows[0:NF], rows[NF : 2 * NF]
        re_sides = jnp.concatenate([delta * float(HALF), re[:-1]], 0) + jnp.concatenate([re[1:], rows[35:36]], 0)
        im_sides = jnp.concatenate([jnp.zeros_like(delta), im[:-1]], 0) + jnp.concatenate([im[1:], rows[36:37]], 0)
        re2, im2 = re + re, im + im
        if h:
            tall_ref[h - 1, 0:NF] = held[0] + sign * (re2 + re_sides)
            tall_ref[h - 1, NF : 2 * NF] = held[1] + sign * (im2 + im_sides)
        held = (re2 - re_sides, im2 - im_sides)
    tall_ref[NH - 1, 0:NF] = jnp.broadcast_to(jnp.where(lane < LANES, root, 0.0), (NF, width))
    tall_ref[NH - 1, NF : 2 * NF] = jnp.zeros((NF, width), jnp.float32)
    tall = jnp.transpose(tall_ref[...], (1, 0, 2))
    group = NF // 2
    shared = lax.broadcasted_iota(jnp.int32, (NH, 4 * LANES // 2), 1) // NH % group
    dims = (((1,), (1,)), ((), ()))
    for g in range(2):
        part = [tall[i * NF + g * group : i * NF + (g + 1) * group].reshape(group * NH, width) for i in range(2)]
        rows = jnp.concatenate(part, 0)
        high = rows.astype(jnp.bfloat16)
        low = (rows - high.astype(jnp.float32)).astype(jnp.bfloat16)
        gram = lax.dot_general(high, high, dims, preferred_element_type=jnp.float32)
        gram = gram + lax.dot_general(high, low, dims, preferred_element_type=jnp.float32)
        gram = gram + lax.dot_general(low, high, dims, preferred_element_type=jnp.float32)
        gram = gram.reshape(2, group, NH, gram.shape[1])
        for i in range(2):
            kept = jnp.zeros(shared.shape, jnp.float32)
            for f in range(group):
                kept = kept + jnp.where(shared == f, gram[i, f], 0.0)
            out_ref[g, i] = kept


def gram_kernel(steps_all, block_ref, table_ref, offset_ref, weight_ref, out_ref, tall_ref, rows_ref):
    table = table_ref[...]
    for h in range(NH):
        block = jnp.concatenate([block_ref[h, c] for c in range(3)], axis=1)
        part = jnp.dot(table, block, preferred_element_type=jnp.float32)
        rows_ref[h] = part[0:ROWS] + part[ROWS : 2 * ROWS] + part[2 * ROWS :]
    root = jnp.sqrt(weight_ref[...])
    root = jnp.concatenate([root] * 3, axis=1)
    spectra_gram(
        lambda h: rows_ref[h], lambda h: rows_ref[h, 32:33, :], root, out_ref, tall_ref, offset_ref[...], steps_all
    )


def local_gram(block, weights, steps_all):
    table, offsets = half_table()
    width = block.shape[1] * block.shape[3]
    return pl.pallas_call(
        lambda *refs: gram_kernel(steps_all, *refs),
        out_shape=jax.ShapeDtypeStruct((2, 2, NH, 2 * LANES), jnp.float32),
        scratch_shapes=[
            pltpu.VMEM((NH, 2 * NF, width), jnp.float32),
            pltpu.VMEM((NH, ROWS, width), jnp.float32),
        ],
        compiler_params=pltpu.CompilerParams(vmem_limit_bytes=VMEM),
    )(block, jnp.asarray(pieces(table, 3)), jnp.asarray(offsets), weights[None, :])


def sum_over(value, axis, size):
    step = 1
    while step < size:
        value = value + lax.ppermute(value, axis, [(i, i ^ step) for i in range(size)])
        step *= 2
    return value


def unpack(summed):
    group = NF // 2
    whole = summed.reshape(2, 2, NH, 2, group, NH)
    weight_sum = whole[0, 0, NH - 1, 0, 0, NH - 1]
    whole = jnp.transpose(whole[:, :, :NB, :, :, :NB], (0, 4, 1, 2, 3, 5)).reshape(NF, 2 * NB, 2 * NB)
    return whole * (1.0 / (16.0 * 0.375 * NFFT)) / weight_sum


def make_local(n_space):
    def local(snapshots, weights):
        steps, components, points = snapshots.shape
        x = jnp.transpose(snapshots, (1, 0, 2)).reshape(components, steps, n_space, points // n_space)
        x = jnp.transpose(x, (2, 0, 1, 3))
        x = lax.all_to_all(x, "space", split_axis=0, concat_axis=0, tiled=True)
        steps_all = n_space * steps
        if steps != HALF:
            x = x.reshape(n_space * steps // HALF, HALF // steps, components, steps, -1)
            x = jnp.transpose(x, (0, 2, 1, 3, 4)).reshape(NH, components, HALF, -1)
        gram = local_gram(x, weights, steps_all)
        return unpack(sum_over(gram, "space", n_space))

    return local


def solution(mesh):
    in_specs = (P(("grp", "space"), None, None), P(("grp", "space")))
    out_specs = P("grp", None, None)
    return jax.shard_map(
        make_local(mesh.shape["space"]), mesh=mesh, in_specs=in_specs, out_specs=out_specs, check_vma=False
    )
```

time: 116 us -> 50.6 us (0.44)
  blocking collectives: 64 us -> 27.4 us
  matrix products: 8.33 us -> 0 us
  local copies, waits for them, and re-layouts: 12.2 us -> 4.03 us
  other arithmetic: 6.67 us -> 0.73 us
  waiting for transfers between devices: 16.6 us -> 12 us
  starting transfers between devices: 7.36 us -> 4.37 us
  Pallas kernels: 0 us -> 1.69 us
    psum x1 -> x0, blocking collectives: 64 us -> none  [local(): summed, weight_sum = lax.psum((local_gram, weight_part), 'space')]
    all_to_all x0 -> x1, blocking collectives: none -> 27.4 us  [local(): x = lax.all_to_all(x, 'space', split_axis=0, concat_axis=0, tiled=True)]
    all_to_all x1 -> x0, waiting for transfers between devices: 16.6 us -> none  [local(): lax.all_to_all(snapshots, 'space', split_axis=2, concat_axis=0, tiled=True)]
    ppermute x0 -> x4, waiting for transfers between devices: none -> 12 us  [sum_over(): lax.ppermute(value, axis, [(i, i ^ step) for i in range(size)])]
    all_to_all x1 -> x0, starting transfers between devices: 7.36 us -> none  [local(): lax.all_to_all(snapshots, 'space', split_axis=2, concat_axis=0, tiled=True)]
    slice x2 -> x0, matrix products: 6.52 us -> none  [spectral(): spectra = front_part[:, :-1] + back_part[:, 1:]]
    convert_element_type x2 -> x0, local copies, waits for them, and re-layouts: 5.11 us -> none  [spectral(): signal = block.astype(jnp.float32).reshape(steps_all, rows)]
    unnamed x6 -> x8, local copies, waits for them, and re-layouts: 6.64 us -> 1.8 us
  transfers between devices with their start and end apart: 1 -> 4, of which waited for: 1 -> 4; matrix products, arithmetic and copies ran while one was open for 1% -> 0% of each run, Pallas kernels for 0% -> 0%
where the time goes in v1:
time: 50.6 us; the launch traced here: 50.4 us
  blocking collectives  27.4 us (54%)
  waiting for transfers between devices  12 us (24%)
  starting transfers between devices  4.37 us (9%)
  local copies, waits for them, and re-layouts  4.03 us (8%)
  Pallas kernels  1.69 us (3%)
  other arithmetic  0.73 us (1%)
    all_to_all x1, blocking collectives, local(): x = lax.all_to_all(x, 'space', split_axis=0, concat_axis=0, tiled=True)  27.4 us
    ppermute x4, waiting for transfers between devices, sum_over(): lax.ppermute(value, axis, [(i, i ^ step) for i in range(size)])  12 us
    ppermute x4, starting transfers between devices, sum_over(): lax.ppermute(value, axis, [(i, i ^ step) for i in range(size)])  4.37 us
    unnamed x8, local copies, waits for them, and re-layouts  1.8 us
    pallas_call x1, Pallas kernels, local_gram(): pl.pallas_call(lambda *refs: gram_kernel(steps_all, *refs), out_shape=jax...  1.69 us
    div x2, local copies, waits for them, and re-layouts, unpack(): return whole * (1.0 / (16.0 * 0.375 * NFFT)) / weight_sum  1.24 us
  transfers between devices with their start and end apart: 4, of which 4 were waited for; matrix products, arithmetic and copies ran while one was open for 0% of the time, Pallas kernels for 0%

profile of v1, /device:TPU:0, one launch (start us, length us, event | category | flops | bytes accessed | tf_op | source)
XLA Modules:
  0.0 50.4 jit_solution(3042698350171312177)
XLA Ops:
  0.0 0.0 copy-start
  0.0 1.1 %copy-done = bf16[64,3,2048]{2,0,1:T(8,128)(2,1)S(1)} copy-done((bf16[64,3,2048]{2,0,1:T(8,128)(2,1)S(1)}, bf16[64,3,2048]{2,0,1:T(8,128)(2,1)}, u32[]{:S(2)}) %copy-start) | copy-done | bytes 786456
  1.1 0.2 bitcast_bitcast_fusion
  1.4 0.0 copy-start.1
  1.4 0.0 copy-start.2
  1.4 27.4 %all_to_all.5.refs_0_ = bf16[16,3,64,128]{3,2,1,0:T(8,128)(2,1)S(1)} all-to-all(bf16[16,3,64,128]{3,2,1,0:T(8,128)(2,1)S(1)} %bitcast_bitcast_fusion), channel_id=1, replica_groups=mesh['grp'=2,'space'=16] {'space'}, dimensions={0} | all-to-all | bytes 1572864 | tf_op jit(solution)/shard_map/all_to_all | solution.py:140
  28.8 0.0 copy-start.3
  28.8 0.0 copy-done.1
  28.8 0.0 copy-done.2
  28.8 0.6 %copy-done.3 = f32[128]{0:T(128)S(1)} copy-done((f32[128]{0:T(128)S(1)}, f32[128]{0:T(128)}, u32[]{:S(2)}) %copy-start.3) | copy-done | bytes 536
  29.5 1.7 %shard_map.46 = f32[2,2,16,256]{3,2,1,0:T(8,128)S(1)} custom-call(bf16[16,3,64,128]{3,2,1,0:T(8,128)(2,1)S(1)} %all_to_all.5.refs_0_, bf16[120,64]{1,0:T(8,128)(2,1)S(1)} %copy-done.1, f32[40,1]{1,0:T(8,128)S(1)} %copy-done.2, f32[1,128]{1,0:T(1,128)S(1)} %bitcast.16), custom_call_target="tpu_custom_call" | custom-call | tf_op jit(solution)/shard_map/pallas_call | solution.py:108
  31.2 0.8 %collective-permute-start = (f32[2,2,16,256]{3,2,1,0:T(8,128)S(1)}, f32[2,2,16,256]{3,2,1,0:T(8,128)S(1)}, u32[]{:S(2)}, u32[]{:S(2)}) collective-permute-start(f32[2,2,16,256]{3,2,1,0:T(8,128)S(1)} %shard_map.46), channel_id=1, source_target_pairs={{0,1},{1,0},{2,3},{3,2},{4,5},{5,4},{6,7},{7,6},{8,9},{9,8},{10,11... | collective-permute-start | bytes 196616 | tf_op jit(solution)/shard_map/ppermute | solution.py:122
  32.0 0.9 %collective-permute-done = f32[2,2,16,256]{3,2,1,0:T(8,128)S(1)} collective-permute-done((f32[2,2,16,256]{3,2,1,0:T(8,128)S(1)}, f32[2,2,16,256]{3,2,1,0:T(8,128)S(1)}, u32[]{:S(2)}, u32[]{:S(2)}) %collective-permute-start) | collective-permute-done | bytes 65568 | tf_op jit(solution)/shard_map/ppermute | solution.py:122
  32.9 0.9 %collective-permute-start.1 = (f32[2,2,16,256]{3,2,1,0:T(8,128)S(1)}, f32[2,2,16,256]{3,2,1,0:T(8,128)S(1)}, u32[]{:S(2)}, u32[]{:S(2)}) collective-permute-start(f32[2,2,16,256]{3,2,1,0:T(8,128)S(1)} %add.12), channel_id=1, source_target_pairs={{0,2},{1,3},{2,0},{3,1},{4,6},{5,7},{6,4},{7,5},{8,10},{9,11},{10,... | collective-permute-start | bytes 196616 | tf_op jit(solution)/shard_map/ppermute | solution.py:122
  33.8 3.6 %collective-permute-done.1 = f32[2,2,16,256]{3,2,1,0:T(8,128)S(1)} collective-permute-done((f32[2,2,16,256]{3,2,1,0:T(8,128)S(1)}, f32[2,2,16,256]{3,2,1,0:T(8,128)S(1)}, u32[]{:S(2)}, u32[]{:S(2)}) %collective-permute-start.1) | collective-permute-done | bytes 65568 | tf_op jit(solution)/shard_map/ppermute | solution.py:122
  37.3 1.0 %collective-permute-start.2 = (f32[2,2,16,256]{3,2,1,0:T(8,128)S(1)}, f32[2,2,16,256]{3,2,1,0:T(8,128)S(1)}, u32[]{:S(2)}, u32[]{:S(2)}) collective-permute-start(f32[2,2,16,256]{3,2,1,0:T(8,128)S(1)} %add.13), channel_id=1, source_target_pairs={{0,4},{1,5},{2,6},{3,7},{4,0},{5,1},{6,2},{7,3},{8,12},{9,13},{10,... | collective-permute-start | bytes 196616 | tf_op jit(solution)/shard_map/ppermute | solution.py:122
  38.4 3.3 %collective-permute-done.2 = f32[2,2,16,256]{3,2,1,0:T(8,128)S(1)} collective-permute-done((f32[2,2,16,256]{3,2,1,0:T(8,128)S(1)}, f32[2,2,16,256]{3,2,1,0:T(8,128)S(1)}, u32[]{:S(2)}, u32[]{:S(2)}) %collective-permute-start.2) | collective-permute-done | bytes 65568 | tf_op jit(solution)/shard_map/ppermute | solution.py:122
  41.7 1.6 %collective-permute-start.3 = (f32[2,2,16,256]{3,2,1,0:T(8,128)S(1)}, f32[2,2,16,256]{3,2,1,0:T(8,128)S(1)}, u32[]{:S(2)}, u32[]{:S(2)}) collective-permute-start(f32[2,2,16,256]{3,2,1,0:T(8,128)S(1)} %add.14), channel_id=1, source_target_pairs={{0,8},{1,9},{2,10},{3,11},{4,12},{5,13},{6,14},{7,15},{8,0},{9,1},... | collective-permute-start | bytes 196616 | tf_op jit(solution)/shard_map/ppermute | solution.py:122
  43.3 4.3 %collective-permute-done.3 = f32[2,2,16,256]{3,2,1,0:T(8,128)S(1)} collective-permute-done((f32[2,2,16,256]{3,2,1,0:T(8,128)S(1)}, f32[2,2,16,256]{3,2,1,0:T(8,128)S(1)}, u32[]{:S(2)}, u32[]{:S(2)}) %collective-permute-start.3) | collective-permute-done | bytes 65568 | tf_op jit(solution)/shard_map/ppermute | solution.py:122
  47.6 0.2 reshape.12
  47.8 0.6 %slice.9 = f32[1,1,1,1,1,1]{5,4,3,2,1,0:T(1,128)} slice(f32[2,2,16,2,8,16]{5,4,3,2,1,0:T(8,128)S(1)} %reshape.12), slice={[0:1], [0:1], [15:16], [0:1], [0:1], [15:16]} | slice | bytes 8 | tf_op jit(solution)/shard_map/slice | solution.py:130
  48.4 0.7 %fusion.1 = f32[2,8,2,15,2,15]{5,1,4,3,2,0:T(8,128)S(1)} fusion(f32[2,2,16,2,8,16]{5,4,3,2,1,0:T(8,128)S(1)} %reshape.12, f32[]{:T(128)} %bitcast.3), kind=kLoop, calls=%fused_computation.3 | loop fusion | flops 28800 | bytes 115204 | tf_op jit(solution)/shard_map/div | solution.py:132
  49.1 0.3 copy.7
  49.4 1.0 %div.15 = f32[16,30,30]{2,0,1:T(8,128)} reshape(f32[2,8,2,15,2,15]{5,4,1,0,3,2:T(2,128)S(1)} %copy.7) | data formatting | bytes 115200 | tf_op jit(solution)/shard_map/div | solution.py:132
  (4 shorter events, 0.0 us)
Async XLA Ops:
  0.0 1.1 %copy-start = (bf16[64,3,2048]{2,0,1:T(8,128)(2,1)S(1)}, bf16[64,3,2048]{2,0,1:T(8,128)(2,1)}, u32[]{:S(2)}) copy-start(bf16[64,3,2048]{2,0,1:T(8,128)(2,1)} %param.4) | copy-start | bytes 2359300
  1.4 27.5 %copy-start.1 = (bf16[120,64]{1,0:T(8,128)(2,1)S(1)}, bf16[120,64]{1,0:T(8,128)(2,1)}, u32[]{:S(2)}) copy-start(bf16[120,64]{1,0:T(8,128)(2,1)} %constant.6.clone.refs_1_) | copy-start | bytes 46084
  1.4 27.4 %copy-start.2 = (f32[40,1]{1,0:T(8,128)S(1)}, f32[40,1]{1,0:T(8,128)}, u32[]{:S(2)}) copy-start(f32[40,1]{1,0:T(8,128)} %constant.7.clone.refs_2_) | copy-start | bytes 484
  28.8 0.7 %copy-start.3 = (f32[128]{0:T(128)S(1)}, f32[128]{0:T(128)}, u32[]{:S(2)}) copy-start(f32[128]{0:T(128)} %param.5) | copy-start | bytes 1540
  31.2 1.7 %collective-permute-start = (f32[2,2,16,256]{3,2,1,0:T(8,128)S(1)}, f32[2,2,16,256]{3,2,1,0:T(8,128)S(1)}, u32[]{:S(2)}, u32[]{:S(2)}) collective-permute-start(f32[2,2,16,256]{3,2,1,0:T(8,128)S(1)} %shard_map.46), channel_id=1, source_target_pairs={{0,1},{1,0},{2,3},{3,2},{4,5},{5,4},{6,7},{7,6},{8,9},{9,8},{10,11... | collective-permute-start | bytes 196616 | tf_op jit(solution)/shard_map/ppermute | solution.py:122
  32.9 4.4 %collective-permute-start.1 = (f32[2,2,16,256]{3,2,1,0:T(8,128)S(1)}, f32[2,2,16,256]{3,2,1,0:T(8,128)S(1)}, u32[]{:S(2)}, u32[]{:S(2)}) collective-permute-start(f32[2,2,16,256]{3,2,1,0:T(8,128)S(1)} %add.12), channel_id=1, source_target_pairs={{0,2},{1,3},{2,0},{3,1},{4,6},{5,7},{6,4},{7,5},{8,10},{9,11},{10,... | collective-permute-start | bytes 196616 | tf_op jit(solution)/shard_map/ppermute | solution.py:122
  37.3 4.3 %collective-permute-start.2 = (f32[2,2,16,256]{3,2,1,0:T(8,128)S(1)}, f32[2,2,16,256]{3,2,1,0:T(8,128)S(1)}, u32[]{:S(2)}, u32[]{:S(2)}) collective-permute-start(f32[2,2,16,256]{3,2,1,0:T(8,128)S(1)} %add.13), channel_id=1, source_target_pairs={{0,4},{1,5},{2,6},{3,7},{4,0},{5,1},{6,2},{7,3},{8,12},{9,13},{10,... | collective-permute-start | bytes 196616 | tf_op jit(solution)/shard_map/ppermute | solution.py:122
  41.7 5.9 %collective-permute-start.3 = (f32[2,2,16,256]{3,2,1,0:T(8,128)S(1)}, f32[2,2,16,256]{3,2,1,0:T(8,128)S(1)}, u32[]{:S(2)}, u32[]{:S(2)}) collective-permute-start(f32[2,2,16,256]{3,2,1,0:T(8,128)S(1)} %add.14), channel_id=1, source_target_pairs={{0,8},{1,9},{2,10},{3,11},{4,12},{5,13},{6,14},{7,15},{8,0},{9,1},... | collective-permute-start | bytes 196616 | tf_op jit(solution)/shard_map/ppermute | solution.py:122

commit v2 on v1

v2 whole, which is shorter than its diff:
```python
import numpy as np
import ml_dtypes
import jax
import jax.numpy as jnp
from jax import lax
from jax.experimental import pallas as pl
from jax.experimental.pallas import tpu as pltpu
from jax.sharding import PartitionSpec as P

NFFT = 128
NB = 15
NF = 16
HALF = NFFT // 2
NH = NB + 1
LANES = 128
MAIN = 2 * NF
EXTRA = 5
ROWS = 40
SMALLEST = 2.0**-60
VMEM = 48 * 1024 * 1024


def half_table():
    turns = 2.0 * np.pi * np.arange(NF + 2)[:, None] * np.arange(HALF)[None, :] / NFFT
    re, im = np.cos(turns), -np.sin(turns)
    offset_re, offset_im = re.sum(1), im.sum(1)
    re0, im0 = re - re.mean(1, keepdims=True), im - im.mean(1, keepdims=True)
    table = np.zeros((ROWS, HALF))
    table[0:NF] = re0[1 : NF + 1]
    table[NF : 2 * NF] = im0[1 : NF + 1]
    table[32] = 1.0
    table[35] = re0[NF + 1]
    table[36] = im0[NF + 1]
    offsets = np.zeros((ROWS, 1))
    offsets[0:NF, 0] = offset_re[1 : NF + 1]
    offsets[NF : 2 * NF, 0] = offset_im[1 : NF + 1]
    offsets[35, 0] = offset_re[NF + 1]
    offsets[36, 0] = offset_im[NF + 1]
    return table, offsets.astype(np.float32)


def pieces(table, count):
    out, rest = [], table.astype(np.float64)
    for _ in range(count):
        part = rest.astype(np.float32).astype(ml_dtypes.bfloat16)
        out.append(part)
        rest = rest - part.astype(np.float64)
    return np.concatenate(out, axis=0)


def transform_kernel(block_ref, table_ref, weight_ref, out_ref, root_ref):
    components, _, points = block_ref.shape
    table = table_ref[...]
    top = jnp.max(jnp.abs(block_ref[...].astype(jnp.float32)), axis=(0, 1, 2), keepdims=True)[0]
    power = jnp.floor(jnp.log2(jnp.maximum(top, SMALLEST)))
    scale = jnp.exp2(-power)
    extras = []
    for c in range(components):
        part = jnp.dot(table, block_ref[c], preferred_element_type=jnp.float32)
        rows = (part[0:ROWS] + part[ROWS : 2 * ROWS] + part[2 * ROWS :]) * scale
        for d in range(points // LANES):
            out_ref[d, c * MAIN : (c + 1) * MAIN] = rows[0:MAIN, d * LANES : (d + 1) * LANES]
        whole = rows[32:33]
        high = whole.astype(jnp.bfloat16).astype(jnp.float32)
        middle = (whole - high).astype(jnp.bfloat16).astype(jnp.float32)
        extras += [high, middle, whole - high - middle, rows[35:37]]
    extras.append(jnp.broadcast_to(power, (1, points)))
    extras = jnp.concatenate(extras, axis=0)
    for d in range(points // LANES):
        out_ref[d, components * MAIN :] = extras[:, d * LANES : (d + 1) * LANES]
    root_ref[...] = jnp.sqrt(weight_ref[...])


def gram_kernel(steps_all, rows_ref, offset_ref, root_ref, out_ref, tall_ref):
    components = (rows_ref.shape[1] - 1) // (MAIN + EXTRA)
    extra = components * MAIN

    def beside(h, at, step, count):
        return jnp.concatenate([rows_ref[h, at + c * step : at + c * step + count, :] for c in range(components)], 1)

    root = jnp.concatenate([root_ref[...]] * components, axis=1)
    offsets = offset_ref[...]
    sums, ends, scales, total = [], [], [], None
    for h in range(NH):
        further = beside(h, extra, EXTRA, EXTRA)
        power = rows_ref[h, extra + components * EXTRA : extra + components * EXTRA + 1, :]
        scale = jnp.concatenate([jnp.exp2(power)] * components, axis=1)
        sums.append((further[0:1] + further[1:2] + further[2:3]) * scale)
        ends.append(further[3:5])
        scales.append(scale)
        total = sums[0] if total is None else total + sums[h]
    mean = total * (1.0 / steps_all)
    freq = lax.broadcasted_iota(jnp.int32, (NF, 1), 0)
    sign = (2 * (freq & 1) - 1).astype(jnp.float32)
    lane = lax.broadcasted_iota(jnp.int32, root.shape, 1)
    held = None
    for h in range(NH):
        delta = (sums[h] * (1.0 / HALF) - mean) * root
        scale = scales[h] * root
        rows = beside(h, 0, MAIN, MAIN) * scale + offsets[0:MAIN] * delta
        end = ends[h] * scale + offsets[35:37] * delta
        re, im = rows[0:NF], rows[NF:MAIN]
        re_sides = jnp.concatenate([delta * float(HALF), re[:-1]], 0) + jnp.concatenate([re[1:], end[0:1]], 0)
        im_sides = jnp.concatenate([jnp.zeros_like(delta), im[:-1]], 0) + jnp.concatenate([im[1:], end[1:2]], 0)
        re2, im2 = re + re, im + im
        if h:
            tall_ref[h - 1, 0:NF] = held[0] + sign * (re2 + re_sides)
            tall_ref[h - 1, NF:MAIN] = held[1] + sign * (im2 + im_sides)
        held = (re2 - re_sides, im2 - im_sides)
    tall_ref[NH - 1, 0:NF] = jnp.broadcast_to(jnp.where(lane < LANES, root, 0.0), (NF, root.shape[1]))
    tall_ref[NH - 1, NF:MAIN] = jnp.zeros((NF, root.shape[1]), jnp.float32)
    tall = jnp.transpose(tall_ref[...], (1, 0, 2))
    group = NF // 2
    shared = lax.broadcasted_iota(jnp.int32, (NH, 2 * group * NH), 1) // NH % group
    dims = (((1,), (1,)), ((), ()))
    for g in range(2):
        part = [tall[i * NF + g * group : i * NF + (g + 1) * group].reshape(group * NH, -1) for i in range(2)]
        rows = jnp.concatenate(part, 0)
        high = rows.astype(jnp.bfloat16)
        low = (rows - high.astype(jnp.float32)).astype(jnp.bfloat16)
        gram = lax.dot_general(high, high, dims, preferred_element_type=jnp.float32)
        gram = gram + lax.dot_general(high, low, dims, preferred_element_type=jnp.float32)
        gram = gram + lax.dot_general(low, high, dims, preferred_element_type=jnp.float32)
        gram = gram.reshape(2, group, NH, gram.shape[1])
        for i in range(2):
            kept = jnp.zeros(shared.shape, jnp.float32)
            for f in range(group):
                kept = kept + jnp.where(shared == f, gram[i, f], 0.0)
            out_ref[g, i] = kept


def transform(block, weights):
    table, _ = half_table()
    components, _, points = block.shape
    return pl.pallas_call(
        transform_kernel,
        out_shape=(
            jax.ShapeDtypeStruct((points // LANES, components * (MAIN + EXTRA) + 1, LANES), jnp.float32),
            jax.ShapeDtypeStruct((1, LANES), jnp.float32),
        ),
        compiler_params=pltpu.CompilerParams(vmem_limit_bytes=VMEM),
    )(block, jnp.asarray(pieces(table, 3)), weights[None, :])


def local_gram(rows, root, steps_all):
    _, offsets = half_table()
    width = (rows.shape[1] - 1) // (MAIN + EXTRA) * LANES
    return pl.pallas_call(
        lambda *refs: gram_kernel(steps_all, *refs),
        out_shape=jax.ShapeDtypeStruct((2, 2, NH, 2 * LANES), jnp.float32),
        scratch_shapes=[pltpu.VMEM((NH, MAIN, width), jnp.float32)],
        compiler_params=pltpu.CompilerParams(vmem_limit_bytes=VMEM),
    )(rows, jnp.asarray(offsets), root)


def sum_over(value, axis, size):
    step = 1
    while step < size:
        value = value + lax.ppermute(value, axis, [(i, i ^ step) for i in range(size)])
        step *= 2
    return value


def unpack(summed):
    group = NF // 2
    whole = summed.reshape(2, 2, NH, 2, group, NH)
    weight_sum = whole[0, 0, NH - 1, 0, 0, NH - 1]
    whole = jnp.transpose(whole[:, :, :NB, :, :, :NB], (0, 4, 1, 2, 3, 5)).reshape(NF, 2 * NB, 2 * NB)
    return whole * (1.0 / (16.0 * 0.375 * NFFT)) / weight_sum


def make_local(n_space):
    def local(snapshots, weights):
        steps, components, points = snapshots.shape
        share = HALF // steps
        block = jnp.transpose(snapshots, (1, 0, 2))
        across = None
        if share > 1:
            block = block.reshape(components, steps, NH, share, -1)
            teams = [[h * share + i for i in range(share)] for h in range(NH)]
            block = lax.all_to_all(block, "space", split_axis=3, concat_axis=1, axis_index_groups=teams, tiled=True)
            block = block.reshape(components, HALF, -1)
            across = [[h * share + i for h in range(NH)] for i in range(share)]
        rows, root = transform(block, weights)
        rows = lax.all_to_all(
            rows.astype(jnp.float16), "space", split_axis=0, concat_axis=0, axis_index_groups=across, tiled=True
        )
        gram = local_gram(rows.astype(jnp.float32), root, n_space * steps)
        return unpack(sum_over(gram, "space", n_space))

    return local


def solution(mesh):
    in_specs = (P(("grp", "space"), None, None), P(("grp", "space")))
    out_specs = P("grp", None, None)
    return jax.shard_map(
        make_local(mesh.shape["space"]), mesh=mesh, in_specs=in_specs, out_specs=out_specs, check_vma=False
    )
```

time: 50.6 us -> 43.9 us (0.87)
  blocking collectives: 27.4 us -> 20.4 us
  waiting for transfers between devices: 12 us -> 10.7 us
  local copies, waits for them, and re-layouts: 4.03 us -> 5.22 us
    all_to_all x1, blocking collectives: 27.4 us -> 20.4 us  [local(): lax.all_to_all(rows.astype(jnp.float16), 'space', split_axis=0, concat_ax...]
    unnamed x8, local copies, waits for them, and re-layouts: 1.8 us -> 3.2 us
    ppermute x4, waiting for transfers between devices: 12 us -> 10.7 us  [sum_over(): lax.ppermute(value, axis, [(i, i ^ step) for i in range(size)])]
    pallas_call x0 -> x1, Pallas kernels: none -> 0.59 us  [transform(): pl.pallas_call(transform_kernel, out_shape=(jax.ShapeDtypeStruct((points...]
where the time goes in v2:
time: 43.9 us; the launch traced here: 43.5 us
  blocking collectives  20.4 us (46%)
  waiting for transfers between devices  10.7 us (24%)
  local copies, waits for them, and re-layouts  5.22 us (12%)
  starting transfers between devices  4.55 us (10%)
  Pallas kernels  1.78 us (4%)
  other arithmetic  0.86 us (2%)
    all_to_all x1, blocking collectives, local(): lax.all_to_all(rows.astype(jnp.float16), 'space', split_axis=0, concat_ax...  20.4 us
    ppermute x4, waiting for transfers between devices, sum_over(): lax.ppermute(value, axis, [(i, i ^ step) for i in range(size)])  10.7 us
    ppermute x4, starting transfers between devices, sum_over(): lax.ppermute(value, axis, [(i, i ^ step) for i in range(size)])  4.55 us
    unnamed x8, local copies, waits for them, and re-layouts  3.2 us
    div x2, local copies, waits for them, and re-layouts, unpack(): return whole * (1.0 / (16.0 * 0.375 * NFFT)) / weight_sum  1.24 us
    pallas_call x1, Pallas kernels, local_gram(): pl.pallas_call(lambda *refs: gram_kernel(steps_all, *refs), out_shape=jax...  1.19 us
  transfers between devices with their start and end apart: 4, of which 4 were waited for; matrix products, arithmetic and copies ran while one was open for 0% of the time, Pallas kernels for 0%

profile of v2, /device:TPU:0, one launch (start us, length us, event | category | flops | bytes accessed | tf_op | source)
XLA Modules:
  0.0 43.5 jit_solution(7702599318536152604)
XLA Ops:
  0.0 0.0 copy-start.3
  0.0 0.7 %copy-done.3 = f32[128]{0:T(128)S(1)} copy-done((f32[128]{0:T(128)S(1)}, f32[128]{0:T(128)}, u32[]{:S(2)}) %copy-start.3) | copy-done | bytes 536
  0.7 0.0 copy-start
  0.7 1.1 %copy-done = bf16[64,3,2048]{2,0,1:T(8,128)(2,1)S(1)} copy-done((bf16[64,3,2048]{2,0,1:T(8,128)(2,1)S(1)}, bf16[64,3,2048]{2,0,1:T(8,128)(2,1)}, u32[]{:S(2)}) %copy-start) | copy-done | bytes 786456
  1.8 0.0 copy-start.1
  1.8 0.8 %copy-done.1 = bf16[120,64]{1,0:T(8,128)(2,1)S(1)} copy-done((bf16[120,64]{1,0:T(8,128)(2,1)S(1)}, bf16[120,64]{1,0:T(8,128)(2,1)}, u32[]{:S(2)}) %copy-start.1) | copy-done | bytes 15384
  2.5 0.6 %shard_map.46 = (f32[16,112,128]{2,1,0:T(8,128)S(1)}, f32[1,128]{1,0:T(1,128)S(1)}) custom-call(bf16[3,64,2048]{2,1,0:T(8,128)(2,1)S(1)} %bitcast.9, bf16[120,64]{1,0:T(8,128)(2,1)S(1)} %copy-done.1, f32[1,128]{1,0:T(1,128)S(1)} %bitcast.10), custom_call_target="tpu_custom_call" | custom-call | tf_op jit(solution)/shard_map/pallas_call | solution.py:135
  3.1 0.1 convert_element_type.6
  3.2 20.4 %all_to_all.5 = f16[16,112,128]{2,1,0:T(8,128)(2,1)S(1)} all-to-all(f16[16,112,128]{2,1,0:T(8,128)(2,1)S(1)} %convert_element_type.6), channel_id=1, replica_groups=mesh['grp'=2,'space'=16] {'space'}, dimensions={0} | all-to-all | bytes 917504 | tf_op jit(solution)/shard_map/all_to_all | solution.py:185
  23.6 0.0 copy-start.2
  23.6 0.1 convert_element_type.7.refs_0_
  23.7 0.7 %copy-done.2 = f32[40,1]{1,0:T(8,128)S(1)} copy-done((f32[40,1]{1,0:T(8,128)S(1)}, f32[40,1]{1,0:T(8,128)}, u32[]{:S(2)}) %copy-start.2) | copy-done | bytes 184
  24.3 1.2 %shard_map.47 = f32[2,2,16,256]{3,2,1,0:T(8,128)S(1)} custom-call(f32[16,112,128]{2,1,0:T(8,128)S(1)} %convert_element_type.7.refs_0_, f32[40,1]{1,0:T(8,128)S(1)} %copy-done.2, f32[1,128]{1,0:T(1,128)S(1)} %get-tuple-element.8.refs_2_), custom_call_target="tpu_custom_call" | custom-call | tf_op jit(solution)/shard_map/pallas_call | solution.py:148
  25.5 0.2 collective-permute-start
  25.7 1.1 %collective-permute-done = f32[2,2,16,256]{3,2,1,0:T(8,128)S(1)} collective-permute-done((f32[2,2,16,256]{3,2,1,0:T(8,128)S(1)}, f32[2,2,16,256]{3,2,1,0:T(8,128)S(1)}, u32[]{:S(2)}, u32[]{:S(2)}) %collective-permute-start) | collective-permute-done | bytes 65568 | tf_op jit(solution)/shard_map/ppermute | solution.py:159
  26.9 0.8 %collective-permute-start.1 = (f32[2,2,16,256]{3,2,1,0:T(8,128)S(1)}, f32[2,2,16,256]{3,2,1,0:T(8,128)S(1)}, u32[]{:S(2)}, u32[]{:S(2)}) collective-permute-start(f32[2,2,16,256]{3,2,1,0:T(8,128)S(1)} %add.12), channel_id=1, source_target_pairs={{0,2},{1,3},{2,0},{3,1},{4,6},{5,7},{6,4},{7,5},{8,10},{9,11},{10,... | collective-permute-start | bytes 196616 | tf_op jit(solution)/shard_map/ppermute | solution.py:159
  27.7 3.5 %collective-permute-done.1 = f32[2,2,16,256]{3,2,1,0:T(8,128)S(1)} collective-permute-done((f32[2,2,16,256]{3,2,1,0:T(8,128)S(1)}, f32[2,2,16,256]{3,2,1,0:T(8,128)S(1)}, u32[]{:S(2)}, u32[]{:S(2)}) %collective-permute-start.1) | collective-permute-done | bytes 65568 | tf_op jit(solution)/shard_map/ppermute | solution.py:159
  31.2 1.4 %collective-permute-start.2 = (f32[2,2,16,256]{3,2,1,0:T(8,128)S(1)}, f32[2,2,16,256]{3,2,1,0:T(8,128)S(1)}, u32[]{:S(2)}, u32[]{:S(2)}) collective-permute-start(f32[2,2,16,256]{3,2,1,0:T(8,128)S(1)} %add.13), channel_id=1, source_target_pairs={{0,4},{1,5},{2,6},{3,7},{4,0},{5,1},{6,2},{7,3},{8,12},{9,13},{10,... | collective-permute-start | bytes 196616 | tf_op jit(solution)/shard_map/ppermute | solution.py:159
  32.6 2.9 %collective-permute-done.2 = f32[2,2,16,256]{3,2,1,0:T(8,128)S(1)} collective-permute-done((f32[2,2,16,256]{3,2,1,0:T(8,128)S(1)}, f32[2,2,16,256]{3,2,1,0:T(8,128)S(1)}, u32[]{:S(2)}, u32[]{:S(2)}) %collective-permute-start.2) | collective-permute-done | bytes 65568 | tf_op jit(solution)/shard_map/ppermute | solution.py:159
  35.6 2.1 %collective-permute-start.3 = (f32[2,2,16,256]{3,2,1,0:T(8,128)S(1)}, f32[2,2,16,256]{3,2,1,0:T(8,128)S(1)}, u32[]{:S(2)}, u32[]{:S(2)}) collective-permute-start(f32[2,2,16,256]{3,2,1,0:T(8,128)S(1)} %add.14), channel_id=1, source_target_pairs={{0,8},{1,9},{2,10},{3,11},{4,12},{5,13},{6,14},{7,15},{8,0},{9,1},... | collective-permute-start | bytes 196616 | tf_op jit(solution)/shard_map/ppermute | solution.py:159
  37.7 3.1 %collective-permute-done.3 = f32[2,2,16,256]{3,2,1,0:T(8,128)S(1)} collective-permute-done((f32[2,2,16,256]{3,2,1,0:T(8,128)S(1)}, f32[2,2,16,256]{3,2,1,0:T(8,128)S(1)}, u32[]{:S(2)}, u32[]{:S(2)}) %collective-permute-start.3) | collective-permute-done | bytes 65568 | tf_op jit(solution)/shard_map/ppermute | solution.py:159
  40.8 0.2 reshape.8
  41.0 0.6 %slice.9 = f32[1,1,1,1,1,1]{5,4,3,2,1,0:T(1,128)} slice(f32[2,2,16,2,8,16]{5,4,3,2,1,0:T(8,128)S(1)} %reshape.8), slice={[0:1], [0:1], [15:16], [0:1], [0:1], [15:16]} | slice | bytes 8 | tf_op jit(solution)/shard_map/slice | solution.py:167
  41.6 0.7 %fusion.1 = f32[2,8,2,15,2,15]{5,1,4,3,2,0:T(8,128)S(1)} fusion(f32[2,2,16,2,8,16]{5,4,3,2,1,0:T(8,128)S(1)} %reshape.8, f32[]{:T(128)} %bitcast.2), kind=kLoop, calls=%fused_computation.2 | loop fusion | flops 28800 | bytes 115204 | tf_op jit(solution)/shard_map/div | solution.py:169
  42.3 0.3 copy.5
  42.6 1.0 %div.15 = f32[16,30,30]{2,0,1:T(8,128)} reshape(f32[2,8,2,15,2,15]{5,4,1,0,3,2:T(2,128)S(1)} %copy.5) | data formatting | bytes 115200 | tf_op jit(solution)/shard_map/div | solution.py:169
  (4 shorter events, 0.0 us)
Async XLA Ops:
  0.0 0.7 %copy-start.3 = (f32[128]{0:T(128)S(1)}, f32[128]{0:T(128)}, u32[]{:S(2)}) copy-start(f32[128]{0:T(128)} %param.5) | copy-start | bytes 1540
  0.7 1.1 %copy-start = (bf16[64,3,2048]{2,0,1:T(8,128)(2,1)S(1)}, bf16[64,3,2048]{2,0,1:T(8,128)(2,1)}, u32[]{:S(2)}) copy-start(bf16[64,3,2048]{2,0,1:T(8,128)(2,1)} %param.4) | copy-start | bytes 2359300
  1.8 0.8 %copy-start.1 = (bf16[120,64]{1,0:T(8,128)(2,1)S(1)}, bf16[120,64]{1,0:T(8,128)(2,1)}, u32[]{:S(2)}) copy-start(bf16[120,64]{1,0:T(8,128)(2,1)} %constant.6.clone.table_ref) | copy-start | bytes 46084
  23.6 0.7 %copy-start.2 = (f32[40,1]{1,0:T(8,128)S(1)}, f32[40,1]{1,0:T(8,128)}, u32[]{:S(2)}) copy-start(f32[40,1]{1,0:T(8,128)} %constant.7.clone.refs_1_) | copy-start | bytes 484
  25.5 1.3 %collective-permute-start = (f32[2,2,16,256]{3,2,1,0:T(8,128)S(1)}, f32[2,2,16,256]{3,2,1,0:T(8,128)S(1)}, u32[]{:S(2)}, u32[]{:S(2)}) collective-permute-start(f32[2,2,16,256]{3,2,1,0:T(8,128)S(1)} %shard_map.47), channel_id=1, source_target_pairs={{0,1},{1,0},{2,3},{3,2},{4,5},{5,4},{6,7},{7,6},{8,9},{9,8},{10,11... | collective-permute-start | bytes 196616 | tf_op jit(solution)/shard_map/ppermute | solution.py:159
  26.9 4.3 %collective-permute-start.1 = (f32[2,2,16,256]{3,2,1,0:T(8,128)S(1)}, f32[2,2,16,256]{3,2,1,0:T(8,128)S(1)}, u32[]{:S(2)}, u32[]{:S(2)}) collective-permute-start(f32[2,2,16,256]{3,2,1,0:T(8,128)S(1)} %add.12), channel_id=1, source_target_pairs={{0,2},{1,3},{2,0},{3,1},{4,6},{5,7},{6,4},{7,5},{8,10},{9,11},{10,... | collective-permute-start | bytes 196616 | tf_op jit(solution)/shard_map/ppermute | solution.py:159
  31.2 4.3 %collective-permute-start.2 = (f32[2,2,16,256]{3,2,1,0:T(8,128)S(1)}, f32[2,2,16,256]{3,2,1,0:T(8,128)S(1)}, u32[]{:S(2)}, u32[]{:S(2)}) collective-permute-start(f32[2,2,16,256]{3,2,1,0:T(8,128)S(1)} %add.13), channel_id=1, source_target_pairs={{0,4},{1,5},{2,6},{3,7},{4,0},{5,1},{6,2},{7,3},{8,12},{9,13},{10,... | collective-permute-start | bytes 196616 | tf_op jit(solution)/shard_map/ppermute | solution.py:159
  35.6 5.2 %collective-permute-start.3 = (f32[2,2,16,256]{3,2,1,0:T(8,128)S(1)}, f32[2,2,16,256]{3,2,1,0:T(8,128)S(1)}, u32[]{:S(2)}, u32[]{:S(2)}) collective-permute-start(f32[2,2,16,256]{3,2,1,0:T(8,128)S(1)} %add.14), channel_id=1, source_target_pairs={{0,8},{1,9},{2,10},{3,11},{4,12},{5,13},{6,14},{7,15},{8,0},{9,1},... | collective-permute-start | bytes 196616 | tf_op jit(solution)/shard_map/ppermute | solution.py:159

commit v3 on v2

--- a/solution.py
+++ b/solution.py
@@ -48,8 +48,16 @@
     return np.concatenate(out, axis=0)
 
 
-def transform_kernel(block_ref, table_ref, weight_ref, out_ref, root_ref):
+def transform_kernel(block_hbm, table_hbm, weight_hbm, offset_hbm, out_ref, root_ref, offset_ref, block_ref, table_ref, weight_ref, sems):
     components, _, points = block_ref.shape
+    copies = [pltpu.make_async_copy(block_hbm.at[c], block_ref.at[c], sems.at[c]) for c in range(components)]
+    copies.append(pltpu.make_async_copy(table_hbm, table_ref, sems.at[components]))
+    copies.append(pltpu.make_async_copy(weight_hbm, weight_ref, sems.at[components + 1]))
+    copies.append(pltpu.make_async_copy(offset_hbm, offset_ref, sems.at[components + 2]))
+    for copy in copies:
+        copy.start()
+    for copy in copies:
+        copy.wait()
     table = table_ref[...]
     top = jnp.max(jnp.abs(block_ref[...].astype(jnp.float32)), axis=(0, 1, 2), keepdims=True)[0]
     power = jnp.floor(jnp.log2(jnp.maximum(top, SMALLEST)))
@@ -130,43 +138,78 @@
 
 
 def transform(block, weights):
-    table, _ = half_table()
+    table, offsets = half_table()
     components, _, points = block.shape
+    table = pieces(table, 3)
     return pl.pallas_call(
         transform_kernel,
+        in_specs=[pl.BlockSpec(memory_space=pltpu.HBM)] * 4,
         out_shape=(
             jax.ShapeDtypeStruct((points // LANES, components * (MAIN + EXTRA) + 1, LANES), jnp.float32),
             jax.ShapeDtypeStruct((1, LANES), jnp.float32),
+            jax.ShapeDtypeStruct(offsets.shape, jnp.float32),
         ),
+        scratch_shapes=[
+            pltpu.VMEM(block.shape, block.dtype),
+            pltpu.VMEM(table.shape, jnp.bfloat16),
+            pltpu.VMEM((1, LANES), jnp.float32),
+            pltpu.SemaphoreType.DMA((components + 3,)),
+        ],
         compiler_params=pltpu.CompilerParams(vmem_limit_bytes=VMEM),
-    )(block, jnp.asarray(pieces(table, 3)), weights[None, :])
-
-
-def local_gram(rows, root, steps_all):
-    _, offsets = half_table()
+    )(block, jnp.asarray(table), weights[None, :], jnp.asarray(offsets))
+
+
+def local_gram(rows, root, offsets, steps_all):
     width = (rows.shape[1] - 1) // (MAIN + EXTRA) * LANES
     return pl.pallas_call(
         lambda *refs: gram_kernel(steps_all, *refs),
         out_shape=jax.ShapeDtypeStruct((2, 2, NH, 2 * LANES), jnp.float32),
         scratch_shapes=[pltpu.VMEM((NH, MAIN, width), jnp.float32)],
         compiler_params=pltpu.CompilerParams(vmem_limit_bytes=VMEM),
-    )(rows, jnp.asarray(offsets), root)
+    )(rows, offsets, root)
+
+
+def partners(value, axis, size, steps):
+    return [lax.ppermute(value, axis, [(i, i ^ step) for i in range(size)]) for step in steps]
+
+
+def finish_kernel(*refs):
+    out_ref = refs[-1]
+    summed = refs[0][...]
+    for ref in refs[1:-1]:
+        summed = summed + ref[...]
+    weight_sum = summed[0, 0, NB : NB + 1, NB : NB + 1]
+    summed = summed * (1.0 / (16.0 * 0.375 * NFFT)) / weight_sum
+    group = NF // 2
+    squares = []
+    for g in range(2):
+        rows = summed[g].reshape(2 * NH, 2 * group * NH)
+        for f in range(group):
+            cuts = [rows[:, (i * group + f) * NH : (i * group + f) * NH + NB] for i in range(2)]
+            squares.append(jnp.concatenate(cuts, axis=1))
+    whole = jnp.transpose(jnp.stack(squares), (1, 0, 2))
+    out_ref[0:NB] = whole[0:NB]
+    out_ref[NB:] = whole[NH : NH + NB]
+
+
+def finish(terms):
+    out = pl.pallas_call(
+        finish_kernel,
+        out_shape=jax.ShapeDtypeStruct((2 * NB, NF, 2 * NB), jnp.float32),
+        compiler_params=pltpu.CompilerParams(vmem_limit_bytes=VMEM),
+    )(*terms)
+    return jnp.transpose(out, (1, 0, 2))
 
 
 def sum_over(value, axis, size):
-    step = 1
+    rounds, step = [], 1
     while step < size:
-        value = value + lax.ppermute(value, axis, [(i, i ^ step) for i in range(size)])
-        step *= 2
-    return value
-
-
-def unpack(summed):
-    group = NF // 2
-    whole = summed.reshape(2, 2, NH, 2, group, NH)
-    weight_sum = whole[0, 0, NH - 1, 0, 0, NH - 1]
-    whole = jnp.transpose(whole[:, :, :NB, :, :, :NB], (0, 4, 1, 2, 3, 5)).reshape(NF, 2 * NB, 2 * NB)
-    return whole * (1.0 / (16.0 * 0.375 * NFFT)) / weight_sum
+        wide = step == 2 and 4 * step <= size
+        rounds.append([step, 2 * step, 3 * step] if wide else [step])
+        step *= 4 if wide else 2
+    for steps in rounds[:-1]:
+        value = sum(partners(value, axis, size, steps), value)
+    return [value] + partners(value, axis, size, rounds[-1])
 
 
 def make_local(n_space):
@@ -181,12 +224,12 @@
             block = lax.all_to_all(block, "space", split_axis=3, concat_axis=1, axis_index_groups=teams, tiled=True)
             block = block.reshape(components, HALF, -1)
             across = [[h * share + i for h in range(NH)] for i in range(share)]
-        rows, root = transform(block, weights)
+        rows, root, offsets = transform(block, weights)
         rows = lax.all_to_all(
             rows.astype(jnp.float16), "space", split_axis=0, concat_axis=0, axis_index_groups=across, tiled=True
         )
-        gram = local_gram(rows.astype(jnp.float32), root, n_space * steps)
-        return unpack(sum_over(gram, "space", n_space))
+        gram = local_gram(rows.astype(jnp.float32), root, offsets, n_space * steps)
+        return finish(sum_over(gram, "space", n_space))
 
     return local
 

time: 43.9 us -> 40.4 us (0.920)
  waiting for transfers between devices: 10.7 us -> 7.42 us
  local copies, waits for them, and re-layouts: 5.22 us -> 3.27 us
  Pallas kernels: 1.78 us -> 2.99 us
  starting transfers between devices: 4.55 us -> 5.76 us
  other arithmetic: 0.86 us -> 0.16 us
    ppermute x4 -> x5, waiting for transfers between devices: 10.7 us -> 7.42 us  [partners(): lax.ppermute(value, axis, [(i, i ^ step) for i in range(size)])]
    div x2 -> x0, local copies, waits for them, and re-layouts: 1.24 us -> none  [unpack(): return whole * (1.0 / (16.0 * 0.375 * NFFT)) / weight_sum]
    ppermute x4 -> x5, starting transfers between devices: 4.55 us -> 5.76 us  [partners(): lax.ppermute(value, axis, [(i, i ^ step) for i in range(size)])]
    pallas_call x1 -> x2, Pallas kernels: 0.59 us -> 1.79 us  [the longest x1 1.01 us: finish(): pl.pallas_call(finish_kernel, out_shape=jax.ShapeDtypeStruct((2 * NB, NF,...]
    div x1 -> x0, other arithmetic: 0.69 us -> none  [unpack(): return whole * (1.0 / (16.0 * 0.375 * NFFT)) / weight_sum]
    slice x1 -> x0, local copies, waits for them, and re-layouts: 0.58 us -> none  [unpack(): weight_sum = whole[0, 0, NH - 1, 0, 0, NH - 1]]
  transfers between devices with their start and end apart: 4 -> 5, of which waited for: 4 -> 5; matrix products, arithmetic and copies ran while one was open for 0% -> 0% of each run, Pallas kernels for 0% -> 0%
where the time goes in v3:
time: 40.4 us; the launch traced here: 40 us
  blocking collectives  20.4 us (50%)
  waiting for transfers between devices  7.42 us (18%)
  starting transfers between devices  5.76 us (14%)
  local copies, waits for them, and re-layouts  3.27 us (8%)
  Pallas kernels  2.99 us (7%)
    all_to_all x1, blocking collectives, local(): lax.all_to_all(rows.astype(jnp.float16), 'space', split_axis=0, concat_ax...  20.4 us
    ppermute x5, waiting for transfers between devices, partners(): lax.ppermute(value, axis, [(i, i ^ step) for i in range(size)])  7.42 us
    ppermute x5, starting transfers between devices, partners(): lax.ppermute(value, axis, [(i, i ^ step) for i in range(size)])  5.76 us
    unnamed x8, local copies, waits for them, and re-layouts  3.27 us
    pallas_call x1, Pallas kernels, local_gram(): pl.pallas_call(lambda *refs: gram_kernel(steps_all, *refs), out_shape=jax...  1.2 us
    pallas_call x1, Pallas kernels, finish(): pl.pallas_call(finish_kernel, out_shape=jax.ShapeDtypeStruct((2 * NB, NF,...  1.01 us
  transfers between devices with their start and end apart: 5, of which 5 were waited for; matrix products, arithmetic and copies ran while one was open for 0% of the time, Pallas kernels for 0%

profile of v3, /device:TPU:0, one launch (start us, length us, event | category | flops | bytes accessed | tf_op | source)
XLA Modules:
  0.0 40.0 jit_solution(16935827460083274653)
XLA Ops:
  0.0 0.0 copy-start.3
  0.0 0.7 %copy-done.3 = f32[128]{0:T(128)S(1)} copy-done((f32[128]{0:T(128)S(1)}, f32[128]{0:T(128)}, u32[]{:S(2)}) %copy-start.3) | copy-done | bytes 536
  0.7 0.0 copy-start
  0.7 1.1 %copy-done = bf16[64,3,2048]{2,0,1:T(8,128)(2,1)S(1)} copy-done((bf16[64,3,2048]{2,0,1:T(8,128)(2,1)S(1)}, bf16[64,3,2048]{2,0,1:T(8,128)(2,1)}, u32[]{:S(2)}) %copy-start) | copy-done | bytes 786456
  1.8 0.0 copy-start.1
  1.8 0.8 %copy-done.1 = bf16[120,64]{1,0:T(8,128)(2,1)S(1)} copy-done((bf16[120,64]{1,0:T(8,128)(2,1)S(1)}, bf16[120,64]{1,0:T(8,128)(2,1)}, u32[]{:S(2)}) %copy-start.1) | copy-done | bytes 15384
  2.5 0.0 copy-start.2
  2.5 0.7 %copy-done.2 = f32[40,1]{1,0:T(8,128)S(1)} copy-done((f32[40,1]{1,0:T(8,128)S(1)}, f32[40,1]{1,0:T(8,128)}, u32[]{:S(2)}) %copy-start.2) | copy-done | bytes 184
  3.3 0.8 %shard_map.46 = (f32[16,112,128]{2,1,0:T(8,128)S(1)}, f32[1,128]{1,0:T(1,128)S(1)}, f32[40,1]{1,0:T(8,128)S(1)}) custom-call(bf16[3,64,2048]{2,1,0:T(8,128)(2,1)S(1)} %bitcast.3, bf16[120,64]{1,0:T(8,128)(2,1)S(1)} %copy-done.1, f32[1,128]{1,0:T(1,128)S(1)} %bitcast.4, f32[40,1]{1,0:T(8,128)S(1)} %copy-done.2), custom_call_target="tpu_custom_call" | custom-call | tf_op jit(solution)/shard_map/pallas_call | solution.py:144
  4.1 0.1 convert_element_type.6
  4.1 20.4 %all_to_all.5 = f16[16,112,128]{2,1,0:T(8,128)(2,1)S(1)} all-to-all(f16[16,112,128]{2,1,0:T(8,128)(2,1)S(1)} %convert_element_type.6), channel_id=1, replica_groups=mesh['grp'=2,'space'=16] {'space'}, dimensions={0} | all-to-all | bytes 917504 | tf_op jit(solution)/shard_map/all_to_all | solution.py:228
  24.5 0.1 convert_element_type.7.refs_0_
  24.6 1.2 %shard_map.47 = f32[2,2,16,256]{3,2,1,0:T(8,128)S(1)} custom-call(f32[16,112,128]{2,1,0:T(8,128)S(1)} %convert_element_type.7.refs_0_, f32[40,1]{1,0:T(8,128)S(1)} %get-tuple-element.9.refs_1_, f32[1,128]{1,0:T(1,128)S(1)} %get-tuple-element.10.refs_2_), custom_call_target="tpu_custom_call" | custom-call | tf_op jit(solution)/shard_map/pallas_call | solution.py:164
  25.8 0.2 collective-permute-start
  26.0 1.1 %collective-permute-done = f32[2,2,16,256]{3,2,1,0:T(8,128)S(1)} collective-permute-done((f32[2,2,16,256]{3,2,1,0:T(8,128)S(1)}, f32[2,2,16,256]{3,2,1,0:T(8,128)S(1)}, u32[]{:S(2)}, u32[]{:S(2)}) %collective-permute-start) | collective-permute-done | bytes 65568 | tf_op jit(solution)/shard_map/ppermute | solution.py:173
  27.1 1.7 %collective-permute-start.3 = (f32[2,2,16,256]{3,2,1,0:T(8,128)S(1)}, f32[2,2,16,256]{3,2,1,0:T(8,128)S(1)}, u32[]{:S(2)}, u32[]{:S(2)}) collective-permute-start(f32[2,2,16,256]{3,2,1,0:T(8,128)S(1)} %add.12), channel_id=1, source_target_pairs={{0,6},{1,7},{2,4},{3,5},{4,2},{5,3},{6,0},{7,1},{8,14},{9,15},{10,... | collective-permute-start | bytes 196616 | tf_op jit(solution)/shard_map/ppermute | solution.py:173
  28.8 0.6 %collective-permute-start.2 = (f32[2,2,16,256]{3,2,1,0:T(8,128)S(1)}, f32[2,2,16,256]{3,2,1,0:T(8,128)S(1)}, u32[]{:S(2)}, u32[]{:S(2)}) collective-permute-start(f32[2,2,16,256]{3,2,1,0:T(8,128)S(1)} %add.12), channel_id=1, source_target_pairs={{0,4},{1,5},{2,6},{3,7},{4,0},{5,1},{6,2},{7,3},{8,12},{9,13},{10,... | collective-permute-start | bytes 196616 | tf_op jit(solution)/shard_map/ppermute | solution.py:173
  29.4 1.2 %collective-permute-start.1 = (f32[2,2,16,256]{3,2,1,0:T(8,128)S(1)}, f32[2,2,16,256]{3,2,1,0:T(8,128)S(1)}, u32[]{:S(2)}, u32[]{:S(2)}) collective-permute-start(f32[2,2,16,256]{3,2,1,0:T(8,128)S(1)} %add.12), channel_id=1, source_target_pairs={{0,2},{1,3},{2,0},{3,1},{4,6},{5,7},{6,4},{7,5},{8,10},{9,11},{10,... | collective-permute-start | bytes 196616 | tf_op jit(solution)/shard_map/ppermute | solution.py:173
  30.7 2.0 %collective-permute-done.3 = f32[2,2,16,256]{3,2,1,0:T(8,128)S(1)} collective-permute-done((f32[2,2,16,256]{3,2,1,0:T(8,128)S(1)}, f32[2,2,16,256]{3,2,1,0:T(8,128)S(1)}, u32[]{:S(2)}, u32[]{:S(2)}) %collective-permute-start.3) | collective-permute-done | bytes 65568 | tf_op jit(solution)/shard_map/ppermute | solution.py:173
  32.7 0.4 %collective-permute-done.2 = f32[2,2,16,256]{3,2,1,0:T(8,128)S(1)} collective-permute-done((f32[2,2,16,256]{3,2,1,0:T(8,128)S(1)}, f32[2,2,16,256]{3,2,1,0:T(8,128)S(1)}, u32[]{:S(2)}, u32[]{:S(2)}) %collective-permute-start.2) | collective-permute-done | bytes 65568 | tf_op jit(solution)/shard_map/ppermute | solution.py:173
  33.2 0.6 %collective-permute-done.1 = f32[2,2,16,256]{3,2,1,0:T(8,128)S(1)} collective-permute-done((f32[2,2,16,256]{3,2,1,0:T(8,128)S(1)}, f32[2,2,16,256]{3,2,1,0:T(8,128)S(1)}, u32[]{:S(2)}, u32[]{:S(2)}) %collective-permute-start.1) | collective-permute-done | bytes 65568 | tf_op jit(solution)/shard_map/ppermute | solution.py:173
  33.8 2.0 %collective-permute-start.4 = (f32[2,2,16,256]{3,2,1,0:T(8,128)S(1)}, f32[2,2,16,256]{3,2,1,0:T(8,128)S(1)}, u32[]{:S(2)}, u32[]{:S(2)}) collective-permute-start(f32[2,2,16,256]{3,2,1,0:T(8,128)S(1)} %add_add_fusion.refs_0_), channel_id=1, source_target_pairs={{0,8},{1,9},{2,10},{3,11},{4,12},{5,13},{6,14},{7,15},{8,0},{9,1},... | collective-permute-start | bytes 196616 | tf_op jit(solution)/shard_map/ppermute | solution.py:173
  35.8 3.2 %collective-permute-done.4.refs_1_ = f32[2,2,16,256]{3,2,1,0:T(8,128)S(1)} collective-permute-done((f32[2,2,16,256]{3,2,1,0:T(8,128)S(1)}, f32[2,2,16,256]{3,2,1,0:T(8,128)S(1)}, u32[]{:S(2)}, u32[]{:S(2)}) %collective-permute-start.4) | collective-permute-done | bytes 65568 | tf_op jit(solution)/shard_map/ppermute | solution.py:173
  39.0 1.0 %shard_map.48 = f32[30,16,30]{2,1,0:T(8,128)} custom-call(f32[2,2,16,256]{3,2,1,0:T(8,128)S(1)} %add_add_fusion.refs_0_, f32[2,2,16,256]{3,2,1,0:T(8,128)S(1)} %collective-permute-done.4.refs_1_), custom_call_target="tpu_custom_call" | custom-call | tf_op jit(solution)/shard_map/pallas_call | solution.py:196
  (2 shorter events, 0.0 us)
Async XLA Ops:
  0.0 0.7 %copy-start.3 = (f32[128]{0:T(128)S(1)}, f32[128]{0:T(128)}, u32[]{:S(2)}) copy-start(f32[128]{0:T(128)} %param.5) | copy-start | bytes 1540
  0.7 1.1 %copy-start = (bf16[64,3,2048]{2,0,1:T(8,128)(2,1)S(1)}, bf16[64,3,2048]{2,0,1:T(8,128)(2,1)}, u32[]{:S(2)}) copy-start(bf16[64,3,2048]{2,0,1:T(8,128)(2,1)} %param.4) | copy-start | bytes 2359300
  1.8 0.8 %copy-start.1 = (bf16[120,64]{1,0:T(8,128)(2,1)S(1)}, bf16[120,64]{1,0:T(8,128)(2,1)}, u32[]{:S(2)}) copy-start(bf16[120,64]{1,0:T(8,128)(2,1)} %constant.4.clone.table_hbm) | copy-start | bytes 46084
  2.5 0.7 %copy-start.2 = (f32[40,1]{1,0:T(8,128)S(1)}, f32[40,1]{1,0:T(8,128)}, u32[]{:S(2)}) copy-start(f32[40,1]{1,0:T(8,128)} %constant.5.clone.offset_hbm) | copy-start | bytes 484
  25.8 1.3 %collective-permute-start = (f32[2,2,16,256]{3,2,1,0:T(8,128)S(1)}, f32[2,2,16,256]{3,2,1,0:T(8,128)S(1)}, u32[]{:S(2)}, u32[]{:S(2)}) collective-permute-start(f32[2,2,16,256]{3,2,1,0:T(8,128)S(1)} %shard_map.47), channel_id=1, source_target_pairs={{0,1},{1,0},{2,3},{3,2},{4,5},{5,4},{6,7},{7,6},{8,9},{9,8},{10,11... | collective-permute-start | bytes 196616 | tf_op jit(solution)/shard_map/ppermute | solution.py:173
  27.1 5.6 %collective-permute-start.3 = (f32[2,2,16,256]{3,2,1,0:T(8,128)S(1)}, f32[2,2,16,256]{3,2,1,0:T(8,128)S(1)}, u32[]{:S(2)}, u32[]{:S(2)}) collective-permute-start(f32[2,2,16,256]{3,2,1,0:T(8,128)S(1)} %add.12), channel_id=1, source_target_pairs={{0,6},{1,7},{2,4},{3,5},{4,2},{5,3},{6,0},{7,1},{8,14},{9,15},{10,... | collective-permute-start | bytes 196616 | tf_op jit(solution)/shard_map/ppermute | solution.py:173
  28.8 4.4 %collective-permute-start.2 = (f32[2,2,16,256]{3,2,1,0:T(8,128)S(1)}, f32[2,2,16,256]{3,2,1,0:T(8,128)S(1)}, u32[]{:S(2)}, u32[]{:S(2)}) collective-permute-start(f32[2,2,16,256]{3,2,1,0:T(8,128)S(1)} %add.12), channel_id=1, source_target_pairs={{0,4},{1,5},{2,6},{3,7},{4,0},{5,1},{6,2},{7,3},{8,12},{9,13},{10,... | collective-permute-start | bytes 196616 | tf_op jit(solution)/shard_map/ppermute | solution.py:173
  29.4 4.3 %collective-permute-start.1 = (f32[2,2,16,256]{3,2,1,0:T(8,128)S(1)}, f32[2,2,16,256]{3,2,1,0:T(8,128)S(1)}, u32[]{:S(2)}, u32[]{:S(2)}) collective-permute-start(f32[2,2,16,256]{3,2,1,0:T(8,128)S(1)} %add.12), channel_id=1, source_target_pairs={{0,2},{1,3},{2,0},{3,1},{4,6},{5,7},{6,4},{7,5},{8,10},{9,11},{10,... | collective-permute-start | bytes 196616 | tf_op jit(solution)/shard_map/ppermute | solution.py:173
  33.8 5.2 %collective-permute-start.4 = (f32[2,2,16,256]{3,2,1,0:T(8,128)S(1)}, f32[2,2,16,256]{3,2,1,0:T(8,128)S(1)}, u32[]{:S(2)}, u32[]{:S(2)}) collective-permute-start(f32[2,2,16,256]{3,2,1,0:T(8,128)S(1)} %add_add_fusion.refs_0_), channel_id=1, source_target_pairs={{0,8},{1,9},{2,10},{3,11},{4,12},{5,13},{6,14},{7,15},{8,0},{9,1},... | collective-permute-start | bytes 196616 | tf_op jit(solution)/shard_map/ppermute | solution.py:173

commit v4 on v3

--- a/solution.py
+++ b/solution.py
@@ -119,7 +119,9 @@
     tall_ref[NH - 1, NF:MAIN] = jnp.zeros((NF, root.shape[1]), jnp.float32)
     tall = jnp.transpose(tall_ref[...], (1, 0, 2))
     group = NF // 2
-    shared = lax.broadcasted_iota(jnp.int32, (NH, 2 * group * NH), 1) // NH % group
+    row = lax.broadcasted_iota(jnp.int32, (NH, LANES), 0)
+    column = lax.broadcasted_iota(jnp.int32, (NH, LANES), 1) % NH
+    shared = lax.broadcasted_iota(jnp.int32, (NH, LANES), 1) // NH
     dims = (((1,), (1,)), ((), ()))
     for g in range(2):
         part = [tall[i * NF + g * group : i * NF + (g + 1) * group].reshape(group * NH, -1) for i in range(2)]
@@ -130,11 +132,14 @@
         gram = gram + lax.dot_general(high, low, dims, preferred_element_type=jnp.float32)
         gram = gram + lax.dot_general(low, high, dims, preferred_element_type=jnp.float32)
         gram = gram.reshape(2, group, NH, gram.shape[1])
-        for i in range(2):
-            kept = jnp.zeros(shared.shape, jnp.float32)
+        kept = []
+        for i, j in ((0, 0), (1, 1), (0, 1)):
+            block = jnp.zeros(shared.shape, jnp.float32)
             for f in range(group):
-                kept = kept + jnp.where(shared == f, gram[i, f], 0.0)
-            out_ref[g, i] = kept
+                block = block + jnp.where(shared == f, gram[i, f, :, j * LANES : (j + 1) * LANES], 0.0)
+            kept.append(block)
+        out_ref[g, :, 0:LANES] = jnp.where(column >= row, kept[0], jnp.concatenate([kept[0][0:1], kept[1][:-1]], 0))
+        out_ref[g, :, LANES:] = kept[2]
 
 
 def transform(block, weights):
@@ -156,14 +161,14 @@
             pltpu.SemaphoreType.DMA((components + 3,)),
         ],
         compiler_params=pltpu.CompilerParams(vmem_limit_bytes=VMEM),
-    )(block, jnp.asarray(table), weights[None, :], jnp.asarray(offsets))
+    )(*[pltpu.with_memory_space_constraint(x, pltpu.HBM) for x in (block, jnp.asarray(table), weights[None, :], jnp.asarray(offsets))])
 
 
 def local_gram(rows, root, offsets, steps_all):
     width = (rows.shape[1] - 1) // (MAIN + EXTRA) * LANES
     return pl.pallas_call(
         lambda *refs: gram_kernel(steps_all, *refs),
-        out_shape=jax.ShapeDtypeStruct((2, 2, NH, 2 * LANES), jnp.float32),
+        out_shape=jax.ShapeDtypeStruct((2, NH, 2 * LANES), jnp.float32),
         scratch_shapes=[pltpu.VMEM((NH, MAIN, width), jnp.float32)],
         compiler_params=pltpu.CompilerParams(vmem_limit_bytes=VMEM),
     )(rows, offsets, root)
@@ -178,18 +183,21 @@
     summed = refs[0][...]
     for ref in refs[1:-1]:
         summed = summed + ref[...]
-    weight_sum = summed[0, 0, NB : NB + 1, NB : NB + 1]
+    weight_sum = summed[0, NB : NB + 1, NB : NB + 1]
     summed = summed * (1.0 / (16.0 * 0.375 * NFFT)) / weight_sum
-    group = NF // 2
-    squares = []
-    for g in range(2):
-        rows = summed[g].reshape(2 * NH, 2 * group * NH)
-        for f in range(group):
-            cuts = [rows[:, (i * group + f) * NH : (i * group + f) * NH + NB] for i in range(2)]
-            squares.append(jnp.concatenate(cuts, axis=1))
-    whole = jnp.transpose(jnp.stack(squares), (1, 0, 2))
-    out_ref[0:NB] = whole[0:NB]
-    out_ref[NB:] = whole[NH : NH + NB]
+    cut, turned = [], []
+    for which in range(2):
+        half = summed[:, :, which * LANES : (which + 1) * LANES]
+        cut.append(jnp.stack([half[g][:, f * NH : (f + 1) * NH] for g in range(2) for f in range(NF // 2)]))
+        turned.append(jnp.concatenate([half[g].T.reshape(NF // 2, NH, NH) for g in range(2)], axis=0))
+    row = lax.broadcasted_iota(jnp.int32, (NF, NB, NB), 1)
+    column = lax.broadcasted_iota(jnp.int32, (NF, NB, NB), 2)
+    re_re = jnp.where(row <= column, cut[0][:, 0:NB, 0:NB], turned[0][:, 0:NB, 0:NB])
+    im_im = jnp.where(row >= column, cut[0][:, 1:NH, 0:NB], turned[0][:, 0:NB, 1:NH])
+    upper = jnp.concatenate([re_re, cut[1][:, 0:NB, 0:NB]], axis=2)
+    lower = jnp.concatenate([turned[1][:, 0:NB, 0:NB], im_im], axis=2)
+    out_ref[0:NB] = jnp.transpose(upper, (1, 0, 2))
+    out_ref[NB:] = jnp.transpose(lower, (1, 0, 2))
 
 
 def finish(terms):

time: 40.4 us -> 37.2 us (0.921)
  local copies, waits for them, and re-layouts: 3.27 us -> 0 us
  Pallas kernels: 2.99 us -> 4.1 us
  starting transfers between devices: 5.76 us -> 5.01 us
    unnamed x8 -> x0, local copies, waits for them, and re-layouts: 3.27 us -> none
    pallas_call x1, Pallas kernels: 0.78 us -> 1.77 us  [transform(): pl.pallas_call(transform_kernel, in_specs=[pl.BlockSpec(memory_space=pltp...]
    ppermute x5, starting transfers between devices: 5.76 us -> 5.01 us  [partners(): lax.ppermute(value, axis, [(i, i ^ step) for i in range(size)])]
where the time goes in v4:
time: 37.2 us; the launch traced here: 37 us
  blocking collectives  20.4 us (55%)
  waiting for transfers between devices  7.31 us (20%)
  starting transfers between devices  5.01 us (13%)
  Pallas kernels  4.1 us (11%)
    all_to_all x1, blocking collectives, local(): lax.all_to_all(rows.astype(jnp.float16), 'space', split_axis=0, concat_ax...  20.4 us
    ppermute x5, waiting for transfers between devices, partners(): lax.ppermute(value, axis, [(i, i ^ step) for i in range(size)])  7.31 us
    ppermute x5, starting transfers between devices, partners(): lax.ppermute(value, axis, [(i, i ^ step) for i in range(size)])  5.01 us
    pallas_call x1, Pallas kernels, transform(): pl.pallas_call(transform_kernel, in_specs=[pl.BlockSpec(memory_space=pltp...  1.77 us
    pallas_call x1, Pallas kernels, local_gram(): pl.pallas_call(lambda *refs: gram_kernel(steps_all, *refs), out_shape=jax...  1.2 us
    pallas_call x1, Pallas kernels, finish(): pl.pallas_call(finish_kernel, out_shape=jax.ShapeDtypeStruct((2 * NB, NF,...  1.14 us
  transfers between devices with their start and end apart: 5, of which 5 were waited for; matrix products, arithmetic and copies ran while one was open for 0% of the time, Pallas kernels for 0%

profile of v4, /device:TPU:0, one launch (start us, length us, event | category | flops | bytes accessed | tf_op | source)
XLA Modules:
  0.0 37.0 jit_solution(5120802127382670783)
XLA Ops:
  0.0 1.8 %shard_map.46 = (f32[16,112,128]{2,1,0:T(8,128)S(1)}, f32[1,128]{1,0:T(1,128)S(1)}, f32[40,1]{1,0:T(8,128)S(1)}) custom-call(bf16[3,64,2048]{2,1,0:T(8,128)(2,1)} %bitcast.3, bf16[120,64]{1,0:T(8,128)(2,1)} %constant.4.clone.table_hbm, f32[1,128]{1,0:T(1,128)} %bitcast.4, f32[40,1]{1,0:T(8,128)} %constant.5.clone.offset_hbm), custom_call_target="tpu_custom_call" | custom-call | tf_op jit(solution)/shard_map/pallas_call | solution.py:149
  1.8 0.1 convert_element_type.6
  1.8 20.4 %all_to_all.5 = f16[16,112,128]{2,1,0:T(8,128)(2,1)S(1)} all-to-all(f16[16,112,128]{2,1,0:T(8,128)(2,1)S(1)} %convert_element_type.6), channel_id=1, replica_groups=mesh['grp'=2,'space'=16] {'space'}, dimensions={0} | all-to-all | bytes 917504 | tf_op jit(solution)/shard_map/all_to_all | solution.py:236
  22.2 0.1 convert_element_type.7.refs_0_
  22.3 1.2 %shard_map.47 = f32[2,16,256]{2,1,0:T(8,128)S(1)} custom-call(f32[16,112,128]{2,1,0:T(8,128)S(1)} %convert_element_type.7.refs_0_, f32[40,1]{1,0:T(8,128)S(1)} %get-tuple-element.9.refs_1_, f32[1,128]{1,0:T(1,128)S(1)} %get-tuple-element.10.refs_2_), custom_call_target="tpu_custom_call" | custom-call | tf_op jit(solution)/shard_map/pallas_call | solution.py:169
  23.5 0.2 collective-permute-start
  23.7 1.1 %collective-permute-done = f32[2,16,256]{2,1,0:T(8,128)S(1)} collective-permute-done((f32[2,16,256]{2,1,0:T(8,128)S(1)}, f32[2,16,256]{2,1,0:T(8,128)S(1)}, u32[]{:S(2)}, u32[]{:S(2)}) %collective-permute-start) | collective-permute-done | bytes 32800 | tf_op jit(solution)/shard_map/ppermute | solution.py:178
  24.8 1.6 %collective-permute-start.3 = (f32[2,16,256]{2,1,0:T(8,128)S(1)}, f32[2,16,256]{2,1,0:T(8,128)S(1)}, u32[]{:S(2)}, u32[]{:S(2)}) collective-permute-start(f32[2,16,256]{2,1,0:T(8,128)S(1)} %add.12), channel_id=1, source_target_pairs={{0,6},{1,7},{2,4},{3,5},{4,2},{5,3},{6,0},{7,1},{8,14},{9,15},{10,... | collective-permute-start | bytes 98312 | tf_op jit(solution)/shard_map/ppermute | solution.py:178
  26.4 0.7 %collective-permute-start.2 = (f32[2,16,256]{2,1,0:T(8,128)S(1)}, f32[2,16,256]{2,1,0:T(8,128)S(1)}, u32[]{:S(2)}, u32[]{:S(2)}) collective-permute-start(f32[2,16,256]{2,1,0:T(8,128)S(1)} %add.12), channel_id=1, source_target_pairs={{0,4},{1,5},{2,6},{3,7},{4,0},{5,1},{6,2},{7,3},{8,12},{9,13},{10,... | collective-permute-start | bytes 98312 | tf_op jit(solution)/shard_map/ppermute | solution.py:178
  27.1 1.2 %collective-permute-start.1 = (f32[2,16,256]{2,1,0:T(8,128)S(1)}, f32[2,16,256]{2,1,0:T(8,128)S(1)}, u32[]{:S(2)}, u32[]{:S(2)}) collective-permute-start(f32[2,16,256]{2,1,0:T(8,128)S(1)} %add.12), channel_id=1, source_target_pairs={{0,2},{1,3},{2,0},{3,1},{4,6},{5,7},{6,4},{7,5},{8,10},{9,11},{10,... | collective-permute-start | bytes 98312 | tf_op jit(solution)/shard_map/ppermute | solution.py:178
  28.3 1.3 %collective-permute-done.3 = f32[2,16,256]{2,1,0:T(8,128)S(1)} collective-permute-done((f32[2,16,256]{2,1,0:T(8,128)S(1)}, f32[2,16,256]{2,1,0:T(8,128)S(1)}, u32[]{:S(2)}, u32[]{:S(2)}) %collective-permute-start.3) | collective-permute-done | bytes 32800 | tf_op jit(solution)/shard_map/ppermute | solution.py:178
  29.6 0.7 %collective-permute-done.2 = f32[2,16,256]{2,1,0:T(8,128)S(1)} collective-permute-done((f32[2,16,256]{2,1,0:T(8,128)S(1)}, f32[2,16,256]{2,1,0:T(8,128)S(1)}, u32[]{:S(2)}, u32[]{:S(2)}) %collective-permute-start.2) | collective-permute-done | bytes 32800 | tf_op jit(solution)/shard_map/ppermute | solution.py:178
  30.3 0.7 %collective-permute-done.1 = f32[2,16,256]{2,1,0:T(8,128)S(1)} collective-permute-done((f32[2,16,256]{2,1,0:T(8,128)S(1)}, f32[2,16,256]{2,1,0:T(8,128)S(1)}, u32[]{:S(2)}, u32[]{:S(2)}) %collective-permute-start.1) | collective-permute-done | bytes 32800 | tf_op jit(solution)/shard_map/ppermute | solution.py:178
  31.0 1.3 %collective-permute-start.4 = (f32[2,16,256]{2,1,0:T(8,128)S(1)}, f32[2,16,256]{2,1,0:T(8,128)S(1)}, u32[]{:S(2)}, u32[]{:S(2)}) collective-permute-start(f32[2,16,256]{2,1,0:T(8,128)S(1)} %add_add_fusion.refs_0_), channel_id=1, source_target_pairs={{0,8},{1,9},{2,10},{3,11},{4,12},{5,13},{6,14},{7,15},{8,0},{9,1},... | collective-permute-start | bytes 98312 | tf_op jit(solution)/shard_map/ppermute | solution.py:178
  32.3 3.5 %collective-permute-done.4.refs_1_ = f32[2,16,256]{2,1,0:T(8,128)S(1)} collective-permute-done((f32[2,16,256]{2,1,0:T(8,128)S(1)}, f32[2,16,256]{2,1,0:T(8,128)S(1)}, u32[]{:S(2)}, u32[]{:S(2)}) %collective-permute-start.4) | collective-permute-done | bytes 32800 | tf_op jit(solution)/shard_map/ppermute | solution.py:178
  35.9 1.1 %shard_map.48 = f32[30,16,30]{2,1,0:T(8,128)} custom-call(f32[2,16,256]{2,1,0:T(8,128)S(1)} %add_add_fusion.refs_0_, f32[2,16,256]{2,1,0:T(8,128)S(1)} %collective-permute-done.4.refs_1_), custom_call_target="tpu_custom_call" | custom-call | tf_op jit(solution)/shard_map/pallas_call | solution.py:204
  (2 shorter events, 0.0 us)
Async XLA Ops:
  23.5 1.3 %collective-permute-start = (f32[2,16,256]{2,1,0:T(8,128)S(1)}, f32[2,16,256]{2,1,0:T(8,128)S(1)}, u32[]{:S(2)}, u32[]{:S(2)}) collective-permute-start(f32[2,16,256]{2,1,0:T(8,128)S(1)} %shard_map.47), channel_id=1, source_target_pairs={{0,1},{1,0},{2,3},{3,2},{4,5},{5,4},{6,7},{7,6},{8,9},{9,8},{10,11... | collective-permute-start | bytes 98312 | tf_op jit(solution)/shard_map/ppermute | solution.py:178
  24.8 4.8 %collective-permute-start.3 = (f32[2,16,256]{2,1,0:T(8,128)S(1)}, f32[2,16,256]{2,1,0:T(8,128)S(1)}, u32[]{:S(2)}, u32[]{:S(2)}) collective-permute-start(f32[2,16,256]{2,1,0:T(8,128)S(1)} %add.12), channel_id=1, source_target_pairs={{0,6},{1,7},{2,4},{3,5},{4,2},{5,3},{6,0},{7,1},{8,14},{9,15},{10,... | collective-permute-start | bytes 98312 | tf_op jit(solution)/shard_map/ppermute | solution.py:178
  26.4 3.9 %collective-permute-start.2 = (f32[2,16,256]{2,1,0:T(8,128)S(1)}, f32[2,16,256]{2,1,0:T(8,128)S(1)}, u32[]{:S(2)}, u32[]{:S(2)}) collective-permute-start(f32[2,16,256]{2,1,0:T(8,128)S(1)} %add.12), channel_id=1, source_target_pairs={{0,4},{1,5},{2,6},{3,7},{4,0},{5,1},{6,2},{7,3},{8,12},{9,13},{10,... | collective-permute-start | bytes 98312 | tf_op jit(solution)/shard_map/ppermute | solution.py:178
  27.1 3.9 %collective-permute-start.1 = (f32[2,16,256]{2,1,0:T(8,128)S(1)}, f32[2,16,256]{2,1,0:T(8,128)S(1)}, u32[]{:S(2)}, u32[]{:S(2)}) collective-permute-start(f32[2,16,256]{2,1,0:T(8,128)S(1)} %add.12), channel_id=1, source_target_pairs={{0,2},{1,3},{2,0},{3,1},{4,6},{5,7},{6,4},{7,5},{8,10},{9,11},{10,... | collective-permute-start | bytes 98312 | tf_op jit(solution)/shard_map/ppermute | solution.py:178
  31.0 4.9 %collective-permute-start.4 = (f32[2,16,256]{2,1,0:T(8,128)S(1)}, f32[2,16,256]{2,1,0:T(8,128)S(1)}, u32[]{:S(2)}, u32[]{:S(2)}) collective-permute-start(f32[2,16,256]{2,1,0:T(8,128)S(1)} %add_add_fusion.refs_0_), channel_id=1, source_target_pairs={{0,8},{1,9},{2,10},{3,11},{4,12},{5,13},{6,14},{7,15},{8,0},{9,1},... | collective-permute-start | bytes 98312 | tf_op jit(solution)/shard_map/ppermute | solution.py:178

commit v5 on v4

--- a/solution.py
+++ b/solution.py
@@ -213,7 +213,7 @@
     rounds, step = [], 1
     while step < size:
         wide = step == 2 and 4 * step <= size
-        rounds.append([step, 2 * step, 3 * step] if wide else [step])
+        rounds.append([c + (step > 1) for c in ([step, 2 * step, 3 * step] if wide else [step])])
         step *= 4 if wide else 2
     for steps in rounds[:-1]:
         value = sum(partners(value, axis, size, steps), value)

time: 37.2 us -> 35.8 us (0.962)
  waiting for transfers between devices: 7.31 us -> 6.16 us
    ppermute x5, waiting for transfers between devices: 7.31 us -> 6.16 us  [partners(): lax.ppermute(value, axis, [(i, i ^ step) for i in range(size)])]
where the time goes in v5:
time: 35.8 us; the launch traced here: 35.6 us
  blocking collectives  20.4 us (57%)
  waiting for transfers between devices  6.16 us (17%)
  starting transfers between devices  4.73 us (13%)
  Pallas kernels  4.1 us (11%)
    all_to_all x1, blocking collectives, local(): lax.all_to_all(rows.astype(jnp.float16), 'space', split_axis=0, concat_ax...  20.4 us
    ppermute x5, waiting for transfers between devices, partners(): lax.ppermute(value, axis, [(i, i ^ step) for i in range(size)])  6.16 us
    ppermute x5, starting transfers between devices, partners(): lax.ppermute(value, axis, [(i, i ^ step) for i in range(size)])  4.73 us
    pallas_call x1, Pallas kernels, transform(): pl.pallas_call(transform_kernel, in_specs=[pl.BlockSpec(memory_space=pltp...  1.77 us
    pallas_call x1, Pallas kernels, local_gram(): pl.pallas_call(lambda *refs: gram_kernel(steps_all, *refs), out_shape=jax...  1.2 us
    pallas_call x1, Pallas kernels, finish(): pl.pallas_call(finish_kernel, out_shape=jax.ShapeDtypeStruct((2 * NB, NF,...  1.14 us
  transfers between devices with their start and end apart: 5, of which 5 were waited for; matrix products, arithmetic and copies ran while one was open for 0% of the time, Pallas kernels for 0%

profile of v5, /device:TPU:0, one launch (start us, length us, event | category | flops | bytes accessed | tf_op | source)
XLA Modules:
  0.0 35.6 jit_solution(2667125115704900079)
XLA Ops:
  0.0 1.8 %shard_map.46 = (f32[16,112,128]{2,1,0:T(8,128)S(1)}, f32[1,128]{1,0:T(1,128)S(1)}, f32[40,1]{1,0:T(8,128)S(1)}) custom-call(bf16[3,64,2048]{2,1,0:T(8,128)(2,1)} %bitcast.3, bf16[120,64]{1,0:T(8,128)(2,1)} %constant.4.clone.table_hbm, f32[1,128]{1,0:T(1,128)} %bitcast.4, f32[40,1]{1,0:T(8,128)} %constant.5.clone.offset_hbm), custom_call_target="tpu_custom_call" | custom-call | tf_op jit(solution)/shard_map/pallas_call | solution.py:149
  1.8 0.1 convert_element_type.6
  1.8 20.4 %all_to_all.5 = f16[16,112,128]{2,1,0:T(8,128)(2,1)S(1)} all-to-all(f16[16,112,128]{2,1,0:T(8,128)(2,1)S(1)} %convert_element_type.6), channel_id=1, replica_groups=mesh['grp'=2,'space'=16] {'space'}, dimensions={0} | all-to-all | bytes 917504 | tf_op jit(solution)/shard_map/all_to_all | solution.py:236
  22.2 0.1 convert_element_type.7.refs_0_
  22.3 1.2 %shard_map.47 = f32[2,16,256]{2,1,0:T(8,128)S(1)} custom-call(f32[16,112,128]{2,1,0:T(8,128)S(1)} %convert_element_type.7.refs_0_, f32[40,1]{1,0:T(8,128)S(1)} %get-tuple-element.9.refs_1_, f32[1,128]{1,0:T(1,128)S(1)} %get-tuple-element.10.refs_2_), custom_call_target="tpu_custom_call" | custom-call | tf_op jit(solution)/shard_map/pallas_call | solution.py:169
  23.5 0.2 collective-permute-start
  23.7 1.1 %collective-permute-done = f32[2,16,256]{2,1,0:T(8,128)S(1)} collective-permute-done((f32[2,16,256]{2,1,0:T(8,128)S(1)}, f32[2,16,256]{2,1,0:T(8,128)S(1)}, u32[]{:S(2)}, u32[]{:S(2)}) %collective-permute-start) | collective-permute-done | bytes 32800 | tf_op jit(solution)/shard_map/ppermute | solution.py:178
  24.8 1.5 %collective-permute-start.3 = (f32[2,16,256]{2,1,0:T(8,128)S(1)}, f32[2,16,256]{2,1,0:T(8,128)S(1)}, u32[]{:S(2)}, u32[]{:S(2)}) collective-permute-start(f32[2,16,256]{2,1,0:T(8,128)S(1)} %add.12), channel_id=1, source_target_pairs={{0,7},{1,6},{2,5},{3,4},{4,3},{5,2},{6,1},{7,0},{8,15},{9,14},{10,... | collective-permute-start | bytes 98312 | tf_op jit(solution)/shard_map/ppermute | solution.py:178
  26.3 0.5 %collective-permute-start.2 = (f32[2,16,256]{2,1,0:T(8,128)S(1)}, f32[2,16,256]{2,1,0:T(8,128)S(1)}, u32[]{:S(2)}, u32[]{:S(2)}) collective-permute-start(f32[2,16,256]{2,1,0:T(8,128)S(1)} %add.12), channel_id=1, source_target_pairs={{0,5},{1,4},{2,7},{3,6},{4,1},{5,0},{6,3},{7,2},{8,13},{9,12},{10,... | collective-permute-start | bytes 98312 | tf_op jit(solution)/shard_map/ppermute | solution.py:178
  26.8 1.0 %collective-permute-start.1 = (f32[2,16,256]{2,1,0:T(8,128)S(1)}, f32[2,16,256]{2,1,0:T(8,128)S(1)}, u32[]{:S(2)}, u32[]{:S(2)}) collective-permute-start(f32[2,16,256]{2,1,0:T(8,128)S(1)} %add.12), channel_id=1, source_target_pairs={{0,3},{1,2},{2,1},{3,0},{4,7},{5,6},{6,5},{7,4},{8,11},{9,10},{10,... | collective-permute-start | bytes 98312 | tf_op jit(solution)/shard_map/ppermute | solution.py:178
  27.8 1.3 %collective-permute-done.3 = f32[2,16,256]{2,1,0:T(8,128)S(1)} collective-permute-done((f32[2,16,256]{2,1,0:T(8,128)S(1)}, f32[2,16,256]{2,1,0:T(8,128)S(1)}, u32[]{:S(2)}, u32[]{:S(2)}) %collective-permute-start.3) | collective-permute-done | bytes 32800 | tf_op jit(solution)/shard_map/ppermute | solution.py:178
  29.0 0.6 %collective-permute-done.2 = f32[2,16,256]{2,1,0:T(8,128)S(1)} collective-permute-done((f32[2,16,256]{2,1,0:T(8,128)S(1)}, f32[2,16,256]{2,1,0:T(8,128)S(1)}, u32[]{:S(2)}, u32[]{:S(2)}) %collective-permute-start.2) | collective-permute-done | bytes 32800 | tf_op jit(solution)/shard_map/ppermute | solution.py:178
  29.6 0.5 %collective-permute-done.1 = f32[2,16,256]{2,1,0:T(8,128)S(1)} collective-permute-done((f32[2,16,256]{2,1,0:T(8,128)S(1)}, f32[2,16,256]{2,1,0:T(8,128)S(1)}, u32[]{:S(2)}, u32[]{:S(2)}) %collective-permute-start.1) | collective-permute-done | bytes 32800 | tf_op jit(solution)/shard_map/ppermute | solution.py:178
  30.1 1.6 %collective-permute-start.4 = (f32[2,16,256]{2,1,0:T(8,128)S(1)}, f32[2,16,256]{2,1,0:T(8,128)S(1)}, u32[]{:S(2)}, u32[]{:S(2)}) collective-permute-start(f32[2,16,256]{2,1,0:T(8,128)S(1)} %add_add_fusion.refs_0_), channel_id=1, source_target_pairs={{0,9},{1,8},{2,11},{3,10},{4,13},{5,12},{6,15},{7,14},{8,1},{9,0},... | collective-permute-start | bytes 98312 | tf_op jit(solution)/shard_map/ppermute | solution.py:178
  31.7 2.7 %collective-permute-done.4.refs_1_ = f32[2,16,256]{2,1,0:T(8,128)S(1)} collective-permute-done((f32[2,16,256]{2,1,0:T(8,128)S(1)}, f32[2,16,256]{2,1,0:T(8,128)S(1)}, u32[]{:S(2)}, u32[]{:S(2)}) %collective-permute-start.4) | collective-permute-done | bytes 32800 | tf_op jit(solution)/shard_map/ppermute | solution.py:178
  34.4 1.1 %shard_map.48 = f32[30,16,30]{2,1,0:T(8,128)} custom-call(f32[2,16,256]{2,1,0:T(8,128)S(1)} %add_add_fusion.refs_0_, f32[2,16,256]{2,1,0:T(8,128)S(1)} %collective-permute-done.4.refs_1_), custom_call_target="tpu_custom_call" | custom-call | tf_op jit(solution)/shard_map/pallas_call | solution.py:204
  (2 shorter events, 0.0 us)
Async XLA Ops:
  23.5 1.3 %collective-permute-start = (f32[2,16,256]{2,1,0:T(8,128)S(1)}, f32[2,16,256]{2,1,0:T(8,128)S(1)}, u32[]{:S(2)}, u32[]{:S(2)}) collective-permute-start(f32[2,16,256]{2,1,0:T(8,128)S(1)} %shard_map.47), channel_id=1, source_target_pairs={{0,1},{1,0},{2,3},{3,2},{4,5},{5,4},{6,7},{7,6},{8,9},{9,8},{10,11... | collective-permute-start | bytes 98312 | tf_op jit(solution)/shard_map/ppermute | solution.py:178
  24.8 4.2 %collective-permute-start.3 = (f32[2,16,256]{2,1,0:T(8,128)S(1)}, f32[2,16,256]{2,1,0:T(8,128)S(1)}, u32[]{:S(2)}, u32[]{:S(2)}) collective-permute-start(f32[2,16,256]{2,1,0:T(8,128)S(1)} %add.12), channel_id=1, source_target_pairs={{0,7},{1,6},{2,5},{3,4},{4,3},{5,2},{6,1},{7,0},{8,15},{9,14},{10,... | collective-permute-start | bytes 98312 | tf_op jit(solution)/shard_map/ppermute | solution.py:178
  26.3 3.3 %collective-permute-start.2 = (f32[2,16,256]{2,1,0:T(8,128)S(1)}, f32[2,16,256]{2,1,0:T(8,128)S(1)}, u32[]{:S(2)}, u32[]{:S(2)}) collective-permute-start(f32[2,16,256]{2,1,0:T(8,128)S(1)} %add.12), channel_id=1, source_target_pairs={{0,5},{1,4},{2,7},{3,6},{4,1},{5,0},{6,3},{7,2},{8,13},{9,12},{10,... | collective-permute-start | bytes 98312 | tf_op jit(solution)/shard_map/ppermute | solution.py:178
  26.8 3.3 %collective-permute-start.1 = (f32[2,16,256]{2,1,0:T(8,128)S(1)}, f32[2,16,256]{2,1,0:T(8,128)S(1)}, u32[]{:S(2)}, u32[]{:S(2)}) collective-permute-start(f32[2,16,256]{2,1,0:T(8,128)S(1)} %add.12), channel_id=1, source_target_pairs={{0,3},{1,2},{2,1},{3,0},{4,7},{5,6},{6,5},{7,4},{8,11},{9,10},{10,... | collective-permute-start | bytes 98312 | tf_op jit(solution)/shard_map/ppermute | solution.py:178
  30.1 4.3 %collective-permute-start.4 = (f32[2,16,256]{2,1,0:T(8,128)S(1)}, f32[2,16,256]{2,1,0:T(8,128)S(1)}, u32[]{:S(2)}, u32[]{:S(2)}) collective-permute-start(f32[2,16,256]{2,1,0:T(8,128)S(1)} %add_add_fusion.refs_0_), channel_id=1, source_target_pairs={{0,9},{1,8},{2,11},{3,10},{4,13},{5,12},{6,15},{7,14},{8,1},{9,0},... | collective-permute-start | bytes 98312 | tf_op jit(solution)/shard_map/ppermute | solution.py:178

commit v6 on v5

--- a/solution.py
+++ b/solution.py
@@ -39,13 +39,19 @@
     return table, offsets.astype(np.float32)
 
 
-def pieces(table, count):
-    out, rest = [], table.astype(np.float64)
-    for _ in range(count):
-        part = rest.astype(np.float32).astype(ml_dtypes.bfloat16)
-        out.append(part)
-        rest = rest - part.astype(np.float64)
-    return np.concatenate(out, axis=0)
+def pieces(table):
+    high = table.astype(ml_dtypes.bfloat16)
+    low = (table - high.astype(np.float64)).astype(ml_dtypes.bfloat16)
+    for row in range(table.shape[0]):
+        for _ in range(8):
+            left = table[row].sum() - high[row].astype(np.float64).sum() - low[row].astype(np.float64).sum()
+            moved = (low[row].astype(np.float64) + left).astype(ml_dtypes.bfloat16)
+            error = np.abs(moved.astype(np.float64) - low[row].astype(np.float64) - left)
+            at = int(np.argmin(error))
+            if error[at] >= abs(left):
+                break
+            low[row, at] = moved[at]
+    return np.concatenate([high, low], axis=1)
 
 
 def transform_kernel(block_hbm, table_hbm, weight_hbm, offset_hbm, out_ref, root_ref, offset_ref, block_ref, table_ref, weight_ref, sems):
@@ -64,8 +70,8 @@
     scale = jnp.exp2(-power)
     extras = []
     for c in range(components):
-        part = jnp.dot(table, block_ref[c], preferred_element_type=jnp.float32)
-        rows = (part[0:ROWS] + part[ROWS : 2 * ROWS] + part[2 * ROWS :]) * scale
+        block = block_ref[c]
+        rows = jnp.dot(table, jnp.concatenate([block] * 2, axis=0), preferred_element_type=jnp.float32) * scale
         for d in range(points // LANES):
             out_ref[d, c * MAIN : (c + 1) * MAIN] = rows[0:MAIN, d * LANES : (d + 1) * LANES]
         whole = rows[32:33]
@@ -128,9 +134,8 @@
         rows = jnp.concatenate(part, 0)
         high = rows.astype(jnp.bfloat16)
         low = (rows - high.astype(jnp.float32)).astype(jnp.bfloat16)
-        gram = lax.dot_general(high, high, dims, preferred_element_type=jnp.float32)
-        gram = gram + lax.dot_general(high, low, dims, preferred_element_type=jnp.float32)
-        gram = gram + lax.dot_general(low, high, dims, preferred_element_type=jnp.float32)
+        left, right = jnp.concatenate([high, high, low], 1), jnp.concatenate([high, low, high], 1)
+        gram = lax.dot_general(left, right, dims, preferred_element_type=jnp.float32)
         gram = gram.reshape(2, group, NH, gram.shape[1])
         kept = []
         for i, j in ((0, 0), (1, 1), (0, 1)):
@@ -145,7 +150,7 @@
 def transform(block, weights):
     table, offsets = half_table()
     components, _, points = block.shape
-    table = pieces(table, 3)
+    table = pieces(table)
     return pl.pallas_call(
         transform_kernel,
         in_specs=[pl.BlockSpec(memory_space=pltpu.HBM)] * 4,

time: 35.8 us -> 35.5 us (level)
  no operation moved by 1% of the time
where the time goes in v6:
time: 35.5 us; the launch traced here: 35.3 us
  blocking collectives  20.4 us (57%)
  waiting for transfers between devices  6.15 us (17%)
  starting transfers between devices  4.74 us (13%)
  Pallas kernels  3.8 us (11%)
    all_to_all x1, blocking collectives, local(): lax.all_to_all(rows.astype(jnp.float16), 'space', split_axis=0, concat_ax...  20.4 us
    ppermute x5, waiting for transfers between devices, partners(): lax.ppermute(value, axis, [(i, i ^ step) for i in range(size)])  6.15 us
    ppermute x5, starting transfers between devices, partners(): lax.ppermute(value, axis, [(i, i ^ step) for i in range(size)])  4.74 us
    pallas_call x1, Pallas kernels, transform(): pl.pallas_call(transform_kernel, in_specs=[pl.BlockSpec(memory_space=pltp...  1.55 us
    pallas_call x1, Pallas kernels, finish(): pl.pallas_call(finish_kernel, out_shape=jax.ShapeDtypeStruct((2 * NB, NF,...  1.14 us
    pallas_call x1, Pallas kernels, local_gram(): pl.pallas_call(lambda *refs: gram_kernel(steps_all, *refs), out_shape=jax...  1.11 us
  transfers between devices with their start and end apart: 5, of which 5 were waited for; matrix products, arithmetic and copies ran while one was open for 0% of the time, Pallas kernels for 0%

profile of v6, /device:TPU:0, one launch (start us, length us, event | category | flops | bytes accessed | tf_op | source)
XLA Modules:
  0.0 35.3 jit_solution(8067620902485160952)
XLA Ops:
  0.0 1.6 %shard_map.46 = (f32[16,112,128]{2,1,0:T(8,128)S(1)}, f32[1,128]{1,0:T(1,128)S(1)}, f32[40,1]{1,0:T(8,128)S(1)}) custom-call(bf16[3,64,2048]{2,1,0:T(8,128)(2,1)} %bitcast.3, bf16[40,128]{1,0:T(8,128)(2,1)} %constant.4.clone.table_hbm, f32[1,128]{1,0:T(1,128)} %bitcast.4, f32[40,1]{1,0:T(8,128)} %constant.5.clone.offset_hbm), custom_call_target="tpu_custom_call" | custom-call | tf_op jit(solution)/shard_map/pallas_call | solution.py:154
  1.6 0.1 convert_element_type.6
  1.6 20.4 %all_to_all.5 = f16[16,112,128]{2,1,0:T(8,128)(2,1)S(1)} all-to-all(f16[16,112,128]{2,1,0:T(8,128)(2,1)S(1)} %convert_element_type.6), channel_id=1, replica_groups=mesh['grp'=2,'space'=16] {'space'}, dimensions={0} | all-to-all | bytes 917504 | tf_op jit(solution)/shard_map/all_to_all | solution.py:241
  22.0 0.1 convert_element_type.7.refs_0_
  22.1 1.1 %shard_map.47 = f32[2,16,256]{2,1,0:T(8,128)S(1)} custom-call(f32[16,112,128]{2,1,0:T(8,128)S(1)} %convert_element_type.7.refs_0_, f32[40,1]{1,0:T(8,128)S(1)} %get-tuple-element.9.refs_1_, f32[1,128]{1,0:T(1,128)S(1)} %get-tuple-element.10.refs_2_), custom_call_target="tpu_custom_call" | custom-call | tf_op jit(solution)/shard_map/pallas_call | solution.py:174
  23.2 0.2 collective-permute-start
  23.4 1.1 %collective-permute-done = f32[2,16,256]{2,1,0:T(8,128)S(1)} collective-permute-done((f32[2,16,256]{2,1,0:T(8,128)S(1)}, f32[2,16,256]{2,1,0:T(8,128)S(1)}, u32[]{:S(2)}, u32[]{:S(2)}) %collective-permute-start) | collective-permute-done | bytes 32800 | tf_op jit(solution)/shard_map/ppermute | solution.py:183
  24.5 1.5 %collective-permute-start.3 = (f32[2,16,256]{2,1,0:T(8,128)S(1)}, f32[2,16,256]{2,1,0:T(8,128)S(1)}, u32[]{:S(2)}, u32[]{:S(2)}) collective-permute-start(f32[2,16,256]{2,1,0:T(8,128)S(1)} %add.12), channel_id=1, source_target_pairs={{0,7},{1,6},{2,5},{3,4},{4,3},{5,2},{6,1},{7,0},{8,15},{9,14},{10,... | collective-permute-start | bytes 98312 | tf_op jit(solution)/shard_map/ppermute | solution.py:183
  26.0 0.5 %collective-permute-start.2 = (f32[2,16,256]{2,1,0:T(8,128)S(1)}, f32[2,16,256]{2,1,0:T(8,128)S(1)}, u32[]{:S(2)}, u32[]{:S(2)}) collective-permute-start(f32[2,16,256]{2,1,0:T(8,128)S(1)} %add.12), channel_id=1, source_target_pairs={{0,5},{1,4},{2,7},{3,6},{4,1},{5,0},{6,3},{7,2},{8,13},{9,12},{10,... | collective-permute-start | bytes 98312 | tf_op jit(solution)/shard_map/ppermute | solution.py:183
  26.5 1.0 %collective-permute-start.1 = (f32[2,16,256]{2,1,0:T(8,128)S(1)}, f32[2,16,256]{2,1,0:T(8,128)S(1)}, u32[]{:S(2)}, u32[]{:S(2)}) collective-permute-start(f32[2,16,256]{2,1,0:T(8,128)S(1)} %add.12), channel_id=1, source_target_pairs={{0,3},{1,2},{2,1},{3,0},{4,7},{5,6},{6,5},{7,4},{8,11},{9,10},{10,... | collective-permute-start | bytes 98312 | tf_op jit(solution)/shard_map/ppermute | solution.py:183
  27.5 1.3 %collective-permute-done.3 = f32[2,16,256]{2,1,0:T(8,128)S(1)} collective-permute-done((f32[2,16,256]{2,1,0:T(8,128)S(1)}, f32[2,16,256]{2,1,0:T(8,128)S(1)}, u32[]{:S(2)}, u32[]{:S(2)}) %collective-permute-start.3) | collective-permute-done | bytes 32800 | tf_op jit(solution)/shard_map/ppermute | solution.py:183
  28.7 0.6 %collective-permute-done.2 = f32[2,16,256]{2,1,0:T(8,128)S(1)} collective-permute-done((f32[2,16,256]{2,1,0:T(8,128)S(1)}, f32[2,16,256]{2,1,0:T(8,128)S(1)}, u32[]{:S(2)}, u32[]{:S(2)}) %collective-permute-start.2) | collective-permute-done | bytes 32800 | tf_op jit(solution)/shard_map/ppermute | solution.py:183
  29.3 0.5 %collective-permute-done.1 = f32[2,16,256]{2,1,0:T(8,128)S(1)} collective-permute-done((f32[2,16,256]{2,1,0:T(8,128)S(1)}, f32[2,16,256]{2,1,0:T(8,128)S(1)}, u32[]{:S(2)}, u32[]{:S(2)}) %collective-permute-start.1) | collective-permute-done | bytes 32800 | tf_op jit(solution)/shard_map/ppermute | solution.py:183
  29.8 1.6 %collective-permute-start.4 = (f32[2,16,256]{2,1,0:T(8,128)S(1)}, f32[2,16,256]{2,1,0:T(8,128)S(1)}, u32[]{:S(2)}, u32[]{:S(2)}) collective-permute-start(f32[2,16,256]{2,1,0:T(8,128)S(1)} %add_add_fusion.refs_0_), channel_id=1, source_target_pairs={{0,9},{1,8},{2,11},{3,10},{4,13},{5,12},{6,15},{7,14},{8,1},{9,0},... | collective-permute-start | bytes 98312 | tf_op jit(solution)/shard_map/ppermute | solution.py:183
  31.4 2.7 %collective-permute-done.4.refs_1_ = f32[2,16,256]{2,1,0:T(8,128)S(1)} collective-permute-done((f32[2,16,256]{2,1,0:T(8,128)S(1)}, f32[2,16,256]{2,1,0:T(8,128)S(1)}, u32[]{:S(2)}, u32[]{:S(2)}) %collective-permute-start.4) | collective-permute-done | bytes 32800 | tf_op jit(solution)/shard_map/ppermute | solution.py:183
  34.1 1.1 %shard_map.48 = f32[30,16,30]{2,1,0:T(8,128)} custom-call(f32[2,16,256]{2,1,0:T(8,128)S(1)} %add_add_fusion.refs_0_, f32[2,16,256]{2,1,0:T(8,128)S(1)} %collective-permute-done.4.refs_1_), custom_call_target="tpu_custom_call" | custom-call | tf_op jit(solution)/shard_map/pallas_call | solution.py:209
  (2 shorter events, 0.0 us)
Async XLA Ops:
  23.2 1.3 %collective-permute-start = (f32[2,16,256]{2,1,0:T(8,128)S(1)}, f32[2,16,256]{2,1,0:T(8,128)S(1)}, u32[]{:S(2)}, u32[]{:S(2)}) collective-permute-start(f32[2,16,256]{2,1,0:T(8,128)S(1)} %shard_map.47), channel_id=1, source_target_pairs={{0,1},{1,0},{2,3},{3,2},{4,5},{5,4},{6,7},{7,6},{8,9},{9,8},{10,11... | collective-permute-start | bytes 98312 | tf_op jit(solution)/shard_map/ppermute | solution.py:183
  24.5 4.2 %collective-permute-start.3 = (f32[2,16,256]{2,1,0:T(8,128)S(1)}, f32[2,16,256]{2,1,0:T(8,128)S(1)}, u32[]{:S(2)}, u32[]{:S(2)}) collective-permute-start(f32[2,16,256]{2,1,0:T(8,128)S(1)} %add.12), channel_id=1, source_target_pairs={{0,7},{1,6},{2,5},{3,4},{4,3},{5,2},{6,1},{7,0},{8,15},{9,14},{10,... | collective-permute-start | bytes 98312 | tf_op jit(solution)/shard_map/ppermute | solution.py:183
  26.0 3.3 %collective-permute-start.2 = (f32[2,16,256]{2,1,0:T(8,128)S(1)}, f32[2,16,256]{2,1,0:T(8,128)S(1)}, u32[]{:S(2)}, u32[]{:S(2)}) collective-permute-start(f32[2,16,256]{2,1,0:T(8,128)S(1)} %add.12), channel_id=1, source_target_pairs={{0,5},{1,4},{2,7},{3,6},{4,1},{5,0},{6,3},{7,2},{8,13},{9,12},{10,... | collective-permute-start | bytes 98312 | tf_op jit(solution)/shard_map/ppermute | solution.py:183
  26.5 3.3 %collective-permute-start.1 = (f32[2,16,256]{2,1,0:T(8,128)S(1)}, f32[2,16,256]{2,1,0:T(8,128)S(1)}, u32[]{:S(2)}, u32[]{:S(2)}) collective-permute-start(f32[2,16,256]{2,1,0:T(8,128)S(1)} %add.12), channel_id=1, source_target_pairs={{0,3},{1,2},{2,1},{3,0},{4,7},{5,6},{6,5},{7,4},{8,11},{9,10},{10,... | collective-permute-start | bytes 98312 | tf_op jit(solution)/shard_map/ppermute | solution.py:183
  29.8 4.3 %collective-permute-start.4 = (f32[2,16,256]{2,1,0:T(8,128)S(1)}, f32[2,16,256]{2,1,0:T(8,128)S(1)}, u32[]{:S(2)}, u32[]{:S(2)}) collective-permute-start(f32[2,16,256]{2,1,0:T(8,128)S(1)} %add_add_fusion.refs_0_), channel_id=1, source_target_pairs={{0,9},{1,8},{2,11},{3,10},{4,13},{5,12},{6,15},{7,14},{8,1},{9,0},... | collective-permute-start | bytes 98312 | tf_op jit(solution)/shard_map/ppermute | solution.py:183

commit v7 on v6

v7 whole, which is shorter than its diff:
```python
import numpy as np
import ml_dtypes
import jax
import jax.numpy as jnp
from jax import lax
from jax.experimental import pallas as pl
from jax.experimental.pallas import tpu as pltpu
from jax.sharding import PartitionSpec as P

NFFT = 128
NB = 15
NF = 16
HALF = NFFT // 2
NH = NB + 1
LANES = 128
MAIN = 2 * NF
EXTRA = 5
ROWS = 40
SMALLEST = 2.0**-60
SMALL_SUM = 1024.0
LOWEST, STEEP = -14.0, 29.9
VMEM = 48 * 1024 * 1024


def half_table():
    turns = 2.0 * np.pi * np.arange(NF + 2)[:, None] * np.arange(HALF)[None, :] / NFFT
    re, im = np.cos(turns), -np.sin(turns)
    offset_re, offset_im = re.sum(1), im.sum(1)
    re0, im0 = re - re.mean(1, keepdims=True), im - im.mean(1, keepdims=True)
    table = np.zeros((ROWS, HALF))
    table[0:NF] = re0[1 : NF + 1]
    table[NF : 2 * NF] = im0[1 : NF + 1]
    table[32] = 1.0 / SMALL_SUM
    table[35] = re0[NF + 1]
    table[36] = im0[NF + 1]
    return table, (offset_re.tolist(), offset_im.tolist())


def pieces(table):
    high = table.astype(ml_dtypes.bfloat16)
    low = (table - high.astype(np.float64)).astype(ml_dtypes.bfloat16)
    for row in range(table.shape[0]):
        for _ in range(8):
            left = table[row].sum() - high[row].astype(np.float64).sum() - low[row].astype(np.float64).sum()
            moved = (low[row].astype(np.float64) + left).astype(ml_dtypes.bfloat16)
            error = np.abs(moved.astype(np.float64) - low[row].astype(np.float64) - left)
            at = int(np.argmin(error))
            if error[at] >= abs(left):
                break
            low[row, at] = moved[at]
    return np.concatenate([high, low], axis=1)


def spread(component):
    place = lax.broadcasted_iota(jnp.int32, (1, LANES), 1) + LANES * component
    turns = place.astype(jnp.float32) * 0.618034
    return 1.0 / (1.0 + 0.125 * (turns - jnp.floor(turns)))


def transform_kernel(block_hbm, table_hbm, weight_hbm, out_ref, root_ref, block_ref, table_ref, weight_ref, sems):
    components, _, points = block_ref.shape
    copies = [pltpu.make_async_copy(block_hbm.at[c], block_ref.at[c], sems.at[c]) for c in range(components)]
    copies.append(pltpu.make_async_copy(table_hbm, table_ref, sems.at[components]))
    copies.append(pltpu.make_async_copy(weight_hbm, weight_ref, sems.at[components + 1]))
    for copy in copies:
        copy.start()
    for copy in copies:
        copy.wait()
    table = table_ref[...]
    extras = []
    for c in range(components):
        block = block_ref[c]
        rows = jnp.dot(table, jnp.concatenate([block] * 2, axis=0), preferred_element_type=jnp.float32)
        sizes = jnp.abs(rows)
        top = sizes[:, 0:LANES]
        for d in range(1, points // LANES):
            top = jnp.maximum(top, sizes[:, d * LANES : (d + 1) * LANES])
        eighths = jnp.ceil(8.0 * jnp.log2(jnp.maximum(jnp.max(top, axis=0, keepdims=True), SMALLEST)))
        scale = jnp.exp2(eighths * -0.125) * spread(c)
        scale, eighths = (jnp.concatenate([x] * (points // LANES), axis=1) for x in (scale, eighths))
        coded = jnp.exp2(sizes * (scale * STEEP) + LOWEST)
        coded = jnp.where(rows < 0.0, -coded, coded)
        for d in range(points // LANES):
            out_ref[d, c * MAIN : (c + 1) * MAIN] = coded[0:MAIN, d * LANES : (d + 1) * LANES]
        whole = rows[32:33] * (scale * SMALL_SUM)
        shifted = whole * 8193.0
        high = shifted - (shifted - whole)
        extras += [high, whole - high, coded[35:37], eighths]
    extras.append(jnp.zeros((1, points), jnp.float32))
    extras = jnp.concatenate(extras, axis=0)
    for d in range(points // LANES):
        out_ref[d, components * MAIN :] = extras[:, d * LANES : (d + 1) * LANES]
    root_ref[...] = jnp.sqrt(weight_ref[...])


def gram_kernel(steps_all, offsets, rows_ref, root_ref, out_ref, high_ref, low_ref):
    components = (rows_ref.shape[1] - 1) // (MAIN + EXTRA)
    extra = components * MAIN
    group = NF // 2
    rows = jnp.transpose(rows_ref[...], (1, 0, 2))
    root = root_ref[...]
    last = lax.broadcasted_iota(jnp.int32, (NH, LANES), 0) == NB
    for c in range(components):
        further = rows[extra + c * EXTRA : extra + (c + 1) * EXTRA]
        scale = jnp.exp2(further[4] * 0.125) * (1.0 / spread(c))
        sums = (further[0] + further[1]) * scale
        delta = (sums * (1.0 / HALF) - jnp.sum(sums, axis=0, keepdims=True) * (1.0 / steps_all)) * root
        scale = scale * (root * (1.0 / STEEP))

        def value(i, k):
            coded = rows[c * MAIN + i * NF + k - 1] if k <= NF else further[2 + i]
            size = (jnp.log2(jnp.abs(coded)) - LOWEST) * scale
            return jnp.where(coded < 0.0, -size, size) + (offsets[i][k] * delta if k % 2 else 0.0)

        for i in range(2):
            before, here = (delta * float(HALF), jnp.zeros_like(delta))[i], value(i, 1)
            for k in range(1, NF + 1):
                after = value(i, k + 1)
                sides, twice = before + after, here + here
                back = pltpu.roll(twice + sides, NH - 1, 0)
                spectrum = twice - sides - back if k % 2 else twice - sides + back
                spectrum = jnp.where(last, root if i == 0 and c == 0 else 0.0, spectrum)
                high = spectrum.astype(jnp.bfloat16)
                g, f = (k - 1) // group, (k - 1) % group
                at = pl.ds((i * group + f) * NH, NH)
                high_ref[g, at, c * LANES : (c + 1) * LANES] = high
                low_ref[g, at, c * LANES : (c + 1) * LANES] = (spectrum - high.astype(jnp.float32)).astype(jnp.bfloat16)
                before, here = here, after
    row = lax.broadcasted_iota(jnp.int32, (NH, LANES), 0)
    column = lax.broadcasted_iota(jnp.int32, (NH, LANES), 1) % NH
    shared = lax.broadcasted_iota(jnp.int32, (NH, LANES), 1) // NH
    dims = (((1,), (1,)), ((), ()))
    for g in range(2):
        high, low = high_ref[g], low_ref[g]
        left, right = jnp.concatenate([high, high, low], 1), jnp.concatenate([high, low, high], 1)
        gram = lax.dot_general(left, right, dims, preferred_element_type=jnp.float32)
        gram = gram.reshape(2, group, NH, gram.shape[1])
        kept = []
        for i, j in ((0, 0), (1, 1), (0, 1)):
            block = jnp.zeros(shared.shape, jnp.float32)
            for f in range(group):
                block = block + jnp.where(shared == f, gram[i, f, :, j * LANES : (j + 1) * LANES], 0.0)
            kept.append(block)
        out_ref[g, :, 0:LANES] = jnp.where(column >= row, kept[0], jnp.concatenate([kept[0][0:1], kept[1][:-1]], 0))
        out_ref[g, :, LANES:] = kept[2]


def transform(block, weights):
    table, _ = half_table()
    components, _, points = block.shape
    table = pieces(table)
    return pl.pallas_call(
        transform_kernel,
        in_specs=[pl.BlockSpec(memory_space=pltpu.HBM)] * 3,
        out_shape=(
            jax.ShapeDtypeStruct((points // LANES, components * (MAIN + EXTRA) + 1, LANES), jnp.float32),
            jax.ShapeDtypeStruct((1, LANES), jnp.float32),
        ),
        scratch_shapes=[
            pltpu.VMEM(block.shape, block.dtype),
            pltpu.VMEM(table.shape, jnp.bfloat16),
            pltpu.VMEM((1, LANES), jnp.float32),
            pltpu.SemaphoreType.DMA((components + 2,)),
        ],
        compiler_params=pltpu.CompilerParams(vmem_limit_bytes=VMEM),
    )(*[pltpu.with_memory_space_constraint(x, pltpu.HBM) for x in (block, jnp.asarray(table), weights[None, :])])


def local_gram(rows, root, steps_all):
    _, offsets = half_table()
    width = (rows.shape[1] - 1) // (MAIN + EXTRA) * LANES
    return pl.pallas_call(
        lambda *refs: gram_kernel(steps_all, offsets, *refs),
        out_shape=jax.ShapeDtypeStruct((2, NH, 2 * LANES), jnp.float32),
        scratch_shapes=[pltpu.VMEM((2, NF * NH, width), jnp.bfloat16)] * 2,
        compiler_params=pltpu.CompilerParams(vmem_limit_bytes=VMEM),
    )(rows, root)


def partners(value, axis, size, steps):
    return [lax.ppermute(value, axis, [(i, i ^ step) for i in range(size)]) for step in steps]


def finish_kernel(*refs):
    out_ref = refs[-1]
    summed = refs[0][...]
    for ref in refs[1:-1]:
        summed = summed + ref[...]
    weight_sum = summed[0, NB : NB + 1, NB : NB + 1]
    summed = summed * (1.0 / (16.0 * 0.375 * NFFT)) / weight_sum
    cut, turned = [], []
    for which in range(2):
        half = summed[:, :, which * LANES : (which + 1) * LANES]
        cut.append(jnp.stack([half[g][:, f * NH : (f + 1) * NH] for g in range(2) for f in range(NF // 2)]))
        turned.append(jnp.concatenate([half[g].T.reshape(NF // 2, NH, NH) for g in range(2)], axis=0))
    row = lax.broadcasted_iota(jnp.int32, (NF, NB, NB), 1)
    column = lax.broadcasted_iota(jnp.int32, (NF, NB, NB), 2)
    re_re = jnp.where(row <= column, cut[0][:, 0:NB, 0:NB], turned[0][:, 0:NB, 0:NB])
    im_im = jnp.where(row >= column, cut[0][:, 1:NH, 0:NB], turned[0][:, 0:NB, 1:NH])
    upper = jnp.concatenate([re_re, cut[1][:, 0:NB, 0:NB]], axis=2)
    lower = jnp.concatenate([turned[1][:, 0:NB, 0:NB], im_im], axis=2)
    out_ref[0:NB] = jnp.transpose(upper, (1, 0, 2))
    out_ref[NB:] = jnp.transpose(lower, (1, 0, 2))


def finish(terms):
    out = pl.pallas_call(
        finish_kernel,
        out_shape=jax.ShapeDtypeStruct((2 * NB, NF, 2 * NB), jnp.float32),
        compiler_params=pltpu.CompilerParams(vmem_limit_bytes=VMEM),
    )(*terms)
    return jnp.transpose(out, (1, 0, 2))


def sum_over(value, axis, size):
    rounds, step = [], 1
    while step < size:
        wide = step == 2 and 4 * step <= size
        rounds.append([c + (step > 1) for c in ([step, 2 * step, 3 * step] if wide else [step])])
        step *= 4 if wide else 2
    for steps in rounds[:-1]:
        value = sum(partners(value, axis, size, steps), value)
    return [value] + partners(value, axis, size, rounds[-1])


def make_local(n_space):
    def local(snapshots, weights):
        steps, components, points = snapshots.shape
        share = HALF // steps
        block = jnp.transpose(snapshots, (1, 0, 2))
        across = None
        if share > 1:
            block = block.reshape(components, steps, NH, share, -1)
            teams = [[h * share + i for i in range(share)] for h in range(NH)]
            block = lax.all_to_all(block, "space", split_axis=3, concat_axis=1, axis_index_groups=teams, tiled=True)
            block = block.reshape(components, HALF, -1)
            across = [[h * share + i for h in range(NH)] for i in range(share)]
        rows, root = transform(block, weights)
        rows = lax.all_to_all(
            rows.astype(jnp.float16), "space", split_axis=0, concat_axis=0, axis_index_groups=across, tiled=True
        )
        gram = local_gram(rows.astype(jnp.float32), root, n_space * steps)
        return finish(sum_over(gram, "space", n_space))

    return local


def solution(mesh):
    in_specs = (P(("grp", "space"), None, None), P(("grp", "space")))
    out_specs = P("grp", None, None)
    return jax.shard_map(
        make_local(mesh.shape["space"]), mesh=mesh, in_specs=in_specs, out_specs=out_specs, check_vma=False
    )
```

time: 35.5 us -> 35.8 us (level)
  no operation moved by 1% of the time
where the time goes in v7:
time: 35.8 us; the launch traced here: 35.6 us
  blocking collectives  20.4 us (57%)
  waiting for transfers between devices  6.15 us (17%)
  starting transfers between devices  4.74 us (13%)
  Pallas kernels  4.14 us (12%)
    all_to_all x1, blocking collectives, local(): lax.all_to_all(rows.astype(jnp.float16), 'space', split_axis=0, concat_ax...  20.4 us
    ppermute x5, waiting for transfers between devices, partners(): lax.ppermute(value, axis, [(i, i ^ step) for i in range(size)])  6.15 us
    ppermute x5, starting transfers between devices, partners(): lax.ppermute(value, axis, [(i, i ^ step) for i in range(size)])  4.74 us
    pallas_call x1, Pallas kernels, transform(): pl.pallas_call(transform_kernel, in_specs=[pl.BlockSpec(memory_space=pltp...  1.82 us
    pallas_call x1, Pallas kernels, local_gram(): pl.pallas_call(lambda *refs: gram_kernel(steps_all, offsets, *refs), out_...  1.18 us
    pallas_call x1, Pallas kernels, finish(): pl.pallas_call(finish_kernel, out_shape=jax.ShapeDtypeStruct((2 * NB, NF,...  1.14 us
  transfers between devices with their start and end apart: 5, of which 5 were waited for; matrix products, arithmetic and copies ran while one was open for 0% of the time, Pallas kernels for 0%

profile of v7, /device:TPU:0, one launch (start us, length us, event | category | flops | bytes accessed | tf_op | source)
XLA Modules:
  0.0 35.6 jit_solution(9760429328912189474)
XLA Ops:
  0.0 1.8 %shard_map.37 = (f32[16,112,128]{2,1,0:T(8,128)S(1)}, f32[1,128]{1,0:T(1,128)S(1)}) custom-call(bf16[3,64,2048]{2,1,0:T(8,128)(2,1)} %bitcast.3, bf16[40,128]{1,0:T(8,128)(2,1)} %constant.2.clone.table_hbm, f32[1,128]{1,0:T(1,128)} %bitcast.4), custom_call_target="tpu_custom_call" | custom-call | tf_op jit(solution)/shard_map/pallas_call | solution.py:152
  1.8 0.1 convert_element_type.6
  1.9 20.4 %all_to_all.5 = f16[16,112,128]{2,1,0:T(8,128)(2,1)S(1)} all-to-all(f16[16,112,128]{2,1,0:T(8,128)(2,1)S(1)} %convert_element_type.6), channel_id=1, replica_groups=mesh['grp'=2,'space'=16] {'space'}, dimensions={0} | all-to-all | bytes 917504 | tf_op jit(solution)/shard_map/all_to_all | solution.py:239
  22.3 0.1 convert_element_type.7.refs_0_
  22.4 1.2 %shard_map.38 = f32[2,16,256]{2,1,0:T(8,128)S(1)} custom-call(f32[16,112,128]{2,1,0:T(8,128)S(1)} %convert_element_type.7.refs_0_, f32[1,128]{1,0:T(1,128)S(1)} %get-tuple-element.8.refs_1_), custom_call_target="tpu_custom_call" | custom-call | tf_op jit(solution)/shard_map/pallas_call | solution.py:172
  23.6 0.2 collective-permute-start
  23.7 1.1 %collective-permute-done = f32[2,16,256]{2,1,0:T(8,128)S(1)} collective-permute-done((f32[2,16,256]{2,1,0:T(8,128)S(1)}, f32[2,16,256]{2,1,0:T(8,128)S(1)}, u32[]{:S(2)}, u32[]{:S(2)}) %collective-permute-start) | collective-permute-done | bytes 32800 | tf_op jit(solution)/shard_map/ppermute | solution.py:181
  24.8 1.5 %collective-permute-start.3 = (f32[2,16,256]{2,1,0:T(8,128)S(1)}, f32[2,16,256]{2,1,0:T(8,128)S(1)}, u32[]{:S(2)}, u32[]{:S(2)}) collective-permute-start(f32[2,16,256]{2,1,0:T(8,128)S(1)} %add.12), channel_id=1, source_target_pairs={{0,7},{1,6},{2,5},{3,4},{4,3},{5,2},{6,1},{7,0},{8,15},{9,14},{10,... | collective-permute-start | bytes 98312 | tf_op jit(solution)/shard_map/ppermute | solution.py:181
  26.3 0.5 %collective-permute-start.2 = (f32[2,16,256]{2,1,0:T(8,128)S(1)}, f32[2,16,256]{2,1,0:T(8,128)S(1)}, u32[]{:S(2)}, u32[]{:S(2)}) collective-permute-start(f32[2,16,256]{2,1,0:T(8,128)S(1)} %add.12), channel_id=1, source_target_pairs={{0,5},{1,4},{2,7},{3,6},{4,1},{5,0},{6,3},{7,2},{8,13},{9,12},{10,... | collective-permute-start | bytes 98312 | tf_op jit(solution)/shard_map/ppermute | solution.py:181
  26.8 1.0 %collective-permute-start.1 = (f32[2,16,256]{2,1,0:T(8,128)S(1)}, f32[2,16,256]{2,1,0:T(8,128)S(1)}, u32[]{:S(2)}, u32[]{:S(2)}) collective-permute-start(f32[2,16,256]{2,1,0:T(8,128)S(1)} %add.12), channel_id=1, source_target_pairs={{0,3},{1,2},{2,1},{3,0},{4,7},{5,6},{6,5},{7,4},{8,11},{9,10},{10,... | collective-permute-start | bytes 98312 | tf_op jit(solution)/shard_map/ppermute | solution.py:181
  27.8 1.3 %collective-permute-done.3 = f32[2,16,256]{2,1,0:T(8,128)S(1)} collective-permute-done((f32[2,16,256]{2,1,0:T(8,128)S(1)}, f32[2,16,256]{2,1,0:T(8,128)S(1)}, u32[]{:S(2)}, u32[]{:S(2)}) %collective-permute-start.3) | collective-permute-done | bytes 32800 | tf_op jit(solution)/shard_map/ppermute | solution.py:181
  29.1 0.6 %collective-permute-done.2 = f32[2,16,256]{2,1,0:T(8,128)S(1)} collective-permute-done((f32[2,16,256]{2,1,0:T(8,128)S(1)}, f32[2,16,256]{2,1,0:T(8,128)S(1)}, u32[]{:S(2)}, u32[]{:S(2)}) %collective-permute-start.2) | collective-permute-done | bytes 32800 | tf_op jit(solution)/shard_map/ppermute | solution.py:181
  29.7 0.5 %collective-permute-done.1 = f32[2,16,256]{2,1,0:T(8,128)S(1)} collective-permute-done((f32[2,16,256]{2,1,0:T(8,128)S(1)}, f32[2,16,256]{2,1,0:T(8,128)S(1)}, u32[]{:S(2)}, u32[]{:S(2)}) %collective-permute-start.1) | collective-permute-done | bytes 32800 | tf_op jit(solution)/shard_map/ppermute | solution.py:181
  30.2 1.6 %collective-permute-start.4 = (f32[2,16,256]{2,1,0:T(8,128)S(1)}, f32[2,16,256]{2,1,0:T(8,128)S(1)}, u32[]{:S(2)}, u32[]{:S(2)}) collective-permute-start(f32[2,16,256]{2,1,0:T(8,128)S(1)} %add_add_fusion.refs_0_), channel_id=1, source_target_pairs={{0,9},{1,8},{2,11},{3,10},{4,13},{5,12},{6,15},{7,14},{8,1},{9,0},... | collective-permute-start | bytes 98312 | tf_op jit(solution)/shard_map/ppermute | solution.py:181
  31.7 2.7 %collective-permute-done.4.refs_1_ = f32[2,16,256]{2,1,0:T(8,128)S(1)} collective-permute-done((f32[2,16,256]{2,1,0:T(8,128)S(1)}, f32[2,16,256]{2,1,0:T(8,128)S(1)}, u32[]{:S(2)}, u32[]{:S(2)}) %collective-permute-start.4) | collective-permute-done | bytes 32800 | tf_op jit(solution)/shard_map/ppermute | solution.py:181
  34.5 1.1 %shard_map.39 = f32[30,16,30]{2,1,0:T(8,128)} custom-call(f32[2,16,256]{2,1,0:T(8,128)S(1)} %add_add_fusion.refs_0_, f32[2,16,256]{2,1,0:T(8,128)S(1)} %collective-permute-done.4.refs_1_), custom_call_target="tpu_custom_call" | custom-call | tf_op jit(solution)/shard_map/pallas_call | solution.py:207
  (2 shorter events, 0.0 us)
Async XLA Ops:
  23.6 1.3 %collective-permute-start = (f32[2,16,256]{2,1,0:T(8,128)S(1)}, f32[2,16,256]{2,1,0:T(8,128)S(1)}, u32[]{:S(2)}, u32[]{:S(2)}) collective-permute-start(f32[2,16,256]{2,1,0:T(8,128)S(1)} %shard_map.38), channel_id=1, source_target_pairs={{0,1},{1,0},{2,3},{3,2},{4,5},{5,4},{6,7},{7,6},{8,9},{9,8},{10,11... | collective-permute-start | bytes 98312 | tf_op jit(solution)/shard_map/ppermute | solution.py:181
  24.8 4.2 %collective-permute-start.3 = (f32[2,16,256]{2,1,0:T(8,128)S(1)}, f32[2,16,256]{2,1,0:T(8,128)S(1)}, u32[]{:S(2)}, u32[]{:S(2)}) collective-permute-start(f32[2,16,256]{2,1,0:T(8,128)S(1)} %add.12), channel_id=1, source_target_pairs={{0,7},{1,6},{2,5},{3,4},{4,3},{5,2},{6,1},{7,0},{8,15},{9,14},{10,... | collective-permute-start | bytes 98312 | tf_op jit(solution)/shard_map/ppermute | solution.py:181
  26.3 3.3 %collective-permute-start.2 = (f32[2,16,256]{2,1,0:T(8,128)S(1)}, f32[2,16,256]{2,1,0:T(8,128)S(1)}, u32[]{:S(2)}, u32[]{:S(2)}) collective-permute-start(f32[2,16,256]{2,1,0:T(8,128)S(1)} %add.12), channel_id=1, source_target_pairs={{0,5},{1,4},{2,7},{3,6},{4,1},{5,0},{6,3},{7,2},{8,13},{9,12},{10,... | collective-permute-start | bytes 98312 | tf_op jit(solution)/shard_map/ppermute | solution.py:181
  26.8 3.3 %collective-permute-start.1 = (f32[2,16,256]{2,1,0:T(8,128)S(1)}, f32[2,16,256]{2,1,0:T(8,128)S(1)}, u32[]{:S(2)}, u32[]{:S(2)}) collective-permute-start(f32[2,16,256]{2,1,0:T(8,128)S(1)} %add.12), channel_id=1, source_target_pairs={{0,3},{1,2},{2,1},{3,0},{4,7},{5,6},{6,5},{7,4},{8,11},{9,10},{10,... | collective-permute-start | bytes 98312 | tf_op jit(solution)/shard_map/ppermute | solution.py:181
  30.2 4.3 %collective-permute-start.4 = (f32[2,16,256]{2,1,0:T(8,128)S(1)}, f32[2,16,256]{2,1,0:T(8,128)S(1)}, u32[]{:S(2)}, u32[]{:S(2)}) collective-permute-start(f32[2,16,256]{2,1,0:T(8,128)S(1)} %add_add_fusion.refs_0_), channel_id=1, source_target_pairs={{0,9},{1,8},{2,11},{3,10},{4,13},{5,12},{6,15},{7,14},{8,1},{9,0},... | collective-permute-start | bytes 98312 | tf_op jit(solution)/shard_map/ppermute | solution.py:181

commit v8 on v7

--- a/solution.py
+++ b/solution.py
@@ -17,8 +17,8 @@
 EXTRA = 5
 ROWS = 40
 SMALLEST = 2.0**-60
-SMALL_SUM = 1024.0
-LOWEST, STEEP = -14.0, 29.9
+SMALL_SUM = 256.0
+LOWEST, STEEP = -125.0, 251.0
 VMEM = 48 * 1024 * 1024
 
 
@@ -55,6 +55,16 @@
     place = lax.broadcasted_iota(jnp.int32, (1, LANES), 1) + LANES * component
     turns = place.astype(jnp.float32) * 0.618034
     return 1.0 / (1.0 + 0.125 * (turns - jnp.floor(turns)))
+
+
+def coded_of(values, sizes, scale):
+    coded = jnp.exp2(sizes * (scale * STEEP) + LOWEST)
+    return jnp.where(values < 0.0, -coded, coded)
+
+
+def value_of(coded, scale):
+    size = (jnp.log2(jnp.abs(coded)) - LOWEST) * scale
+    return jnp.where(coded < 0.0, -size, size)
 
 
 def transform_kernel(block_hbm, table_hbm, weight_hbm, out_ref, root_ref, block_ref, table_ref, weight_ref, sems):
@@ -75,19 +85,18 @@
         top = sizes[:, 0:LANES]
         for d in range(1, points // LANES):
             top = jnp.maximum(top, sizes[:, d * LANES : (d + 1) * LANES])
-        eighths = jnp.ceil(8.0 * jnp.log2(jnp.maximum(jnp.max(top, axis=0, keepdims=True), SMALLEST)))
-        scale = jnp.exp2(eighths * -0.125) * spread(c)
-        scale, eighths = (jnp.concatenate([x] * (points // LANES), axis=1) for x in (scale, eighths))
-        coded = jnp.exp2(sizes * (scale * STEEP) + LOWEST)
-        coded = jnp.where(rows < 0.0, -coded, coded)
+        halves = jnp.ceil(2.0 * jnp.log2(jnp.maximum(jnp.max(top, axis=0, keepdims=True), SMALLEST)))
+        scale = jnp.exp2(halves * -0.5) * spread(c)
+        scale, halves = (jnp.concatenate([x] * (points // LANES), axis=1) for x in (scale, halves))
+        coded = coded_of(rows, sizes, scale)
         for d in range(points // LANES):
-            out_ref[d, c * MAIN : (c + 1) * MAIN] = coded[0:MAIN, d * LANES : (d + 1) * LANES]
-        whole = rows[32:33] * (scale * SMALL_SUM)
-        shifted = whole * 8193.0
-        high = shifted - (shifted - whole)
-        extras += [high, whole - high, coded[35:37], eighths]
+            out_ref[d, c * MAIN : (c + 1) * MAIN] = coded[0:MAIN, d * LANES : (d + 1) * LANES].astype(jnp.bfloat16)
+        whole = rows[32:33] * SMALL_SUM
+        high = whole.astype(jnp.bfloat16).astype(jnp.float32)
+        rest = whole - high
+        extras += [high, coded_of(rest, jnp.abs(rest), scale), coded[35:37], halves]
     extras.append(jnp.zeros((1, points), jnp.float32))
-    extras = jnp.concatenate(extras, axis=0)
+    extras = jnp.concatenate(extras, axis=0).astype(jnp.bfloat16)
     for d in range(points // LANES):
         out_ref[d, components * MAIN :] = extras[:, d * LANES : (d + 1) * LANES]
     root_ref[...] = jnp.sqrt(weight_ref[...])
@@ -97,20 +106,19 @@
     components = (rows_ref.shape[1] - 1) // (MAIN + EXTRA)
     extra = components * MAIN
     group = NF // 2
-    rows = jnp.transpose(rows_ref[...], (1, 0, 2))
+    rows = jnp.transpose(rows_ref[...].astype(jnp.float32), (1, 0, 2))
     root = root_ref[...]
     last = lax.broadcasted_iota(jnp.int32, (NH, LANES), 0) == NB
     for c in range(components):
         further = rows[extra + c * EXTRA : extra + (c + 1) * EXTRA]
-        scale = jnp.exp2(further[4] * 0.125) * (1.0 / spread(c))
-        sums = (further[0] + further[1]) * scale
+        scale = jnp.exp2(further[4] * 0.5) * (1.0 / (STEEP * spread(c)))
+        sums = further[0] + value_of(further[1], scale)
         delta = (sums * (1.0 / HALF) - jnp.sum(sums, axis=0, keepdims=True) * (1.0 / steps_all)) * root
-        scale = scale * (root * (1.0 / STEEP))
+        scale = scale * root
 
         def value(i, k):
             coded = rows[c * MAIN + i * NF + k - 1] if k <= NF else further[2 + i]
-            size = (jnp.log2(jnp.abs(coded)) - LOWEST) * scale
-            return jnp.where(coded < 0.0, -size, size) + (offsets[i][k] * delta if k % 2 else 0.0)
+            return value_of(coded, scale) + (offsets[i][k] * delta if k % 2 else 0.0)
 
         for i in range(2):
             before, here = (delta * float(HALF), jnp.zeros_like(delta))[i], value(i, 1)
@@ -153,7 +161,7 @@
         transform_kernel,
         in_specs=[pl.BlockSpec(memory_space=pltpu.HBM)] * 3,
         out_shape=(
-            jax.ShapeDtypeStruct((points // LANES, components * (MAIN + EXTRA) + 1, LANES), jnp.float32),
+            jax.ShapeDtypeStruct((points // LANES, components * (MAIN + EXTRA) + 1, LANES), jnp.bfloat16),
             jax.ShapeDtypeStruct((1, LANES), jnp.float32),
         ),
         scratch_shapes=[
@@ -236,10 +244,8 @@
             block = block.reshape(components, HALF, -1)
             across = [[h * share + i for h in range(NH)] for i in range(share)]
         rows, root = transform(block, weights)
-        rows = lax.all_to_all(
-            rows.astype(jnp.float16), "space", split_axis=0, concat_axis=0, axis_index_groups=across, tiled=True
-        )
-        gram = local_gram(rows.astype(jnp.float32), root, n_space * steps)
+        rows = lax.all_to_all(rows, "space", split_axis=0, concat_axis=0, axis_index_groups=across, tiled=True)
+        gram = local_gram(rows, root, n_space * steps)
         return finish(sum_over(gram, "space", n_space))
 
     return local

time: 35.8 us -> 35.8 us (level)
  no operation moved by 1% of the time
where the time goes in v8:
time: 35.8 us; the launch traced here: 35.6 us
  blocking collectives  20.4 us (57%)
  waiting for transfers between devices  6.15 us (17%)
  starting transfers between devices  4.74 us (13%)
  Pallas kernels  4.25 us (12%)
    all_to_all x1, blocking collectives, local(): lax.all_to_all(rows, 'space', split_axis=0, concat_axis=0, axis_index_gro...  20.4 us
    ppermute x5, waiting for transfers between devices, partners(): lax.ppermute(value, axis, [(i, i ^ step) for i in range(size)])  6.15 us
    ppermute x5, starting transfers between devices, partners(): lax.ppermute(value, axis, [(i, i ^ step) for i in range(size)])  4.74 us
    pallas_call x1, Pallas kernels, transform(): pl.pallas_call(transform_kernel, in_specs=[pl.BlockSpec(memory_space=pltp...  1.87 us
    pallas_call x1, Pallas kernels, local_gram(): pl.pallas_call(lambda *refs: gram_kernel(steps_all, offsets, *refs), out_...  1.24 us
    pallas_call x1, Pallas kernels, finish(): pl.pallas_call(finish_kernel, out_shape=jax.ShapeDtypeStruct((2 * NB, NF,...  1.14 us
  transfers between devices with their start and end apart: 5, of which 5 were waited for; matrix products, arithmetic and copies ran while one was open for 0% of the time, Pallas kernels for 0%

profile of v8, /device:TPU:0, one launch (start us, length us, event | category | flops | bytes accessed | tf_op | source)
XLA Modules:
  0.0 35.6 jit_solution(15481622116214830693)
XLA Ops:
  0.0 1.9 %shard_map.37 = (bf16[16,112,128]{2,1,0:T(8,128)(2,1)S(1)}, f32[1,128]{1,0:T(1,128)S(1)}) custom-call(bf16[3,64,2048]{2,1,0:T(8,128)(2,1)} %bitcast.3, bf16[40,128]{1,0:T(8,128)(2,1)} %constant.2.clone.table_hbm, f32[1,128]{1,0:T(1,128)} %bitcast.4), custom_call_target="tpu_custom_call" | custom-call | tf_op jit(solution)/shard_map/pallas_call | solution.py:160
  1.9 20.4 %all_to_all.5.refs_0_ = bf16[16,112,128]{2,1,0:T(8,128)(2,1)S(1)} all-to-all(bf16[16,112,128]{2,1,0:T(8,128)(2,1)S(1)} %get-tuple-element.7), channel_id=1, replica_groups=mesh['grp'=2,'space'=16] {'space'}, dimensions={0} | all-to-all | bytes 917504 | tf_op jit(solution)/shard_map/all_to_all | solution.py:247
  22.3 1.2 %shard_map.38 = f32[2,16,256]{2,1,0:T(8,128)S(1)} custom-call(bf16[16,112,128]{2,1,0:T(8,128)(2,1)S(1)} %all_to_all.5.refs_0_, f32[1,128]{1,0:T(1,128)S(1)} %get-tuple-element.8.refs_1_), custom_call_target="tpu_custom_call" | custom-call | tf_op jit(solution)/shard_map/pallas_call | solution.py:180
  23.5 0.2 collective-permute-start
  23.7 1.1 %collective-permute-done = f32[2,16,256]{2,1,0:T(8,128)S(1)} collective-permute-done((f32[2,16,256]{2,1,0:T(8,128)S(1)}, f32[2,16,256]{2,1,0:T(8,128)S(1)}, u32[]{:S(2)}, u32[]{:S(2)}) %collective-permute-start) | collective-permute-done | bytes 32800 | tf_op jit(solution)/shard_map/ppermute | solution.py:189
  24.8 1.5 %collective-permute-start.3 = (f32[2,16,256]{2,1,0:T(8,128)S(1)}, f32[2,16,256]{2,1,0:T(8,128)S(1)}, u32[]{:S(2)}, u32[]{:S(2)}) collective-permute-start(f32[2,16,256]{2,1,0:T(8,128)S(1)} %add.12), channel_id=1, source_target_pairs={{0,7},{1,6},{2,5},{3,4},{4,3},{5,2},{6,1},{7,0},{8,15},{9,14},{10,... | collective-permute-start | bytes 98312 | tf_op jit(solution)/shard_map/ppermute | solution.py:189
  26.3 0.5 %collective-permute-start.2 = (f32[2,16,256]{2,1,0:T(8,128)S(1)}, f32[2,16,256]{2,1,0:T(8,128)S(1)}, u32[]{:S(2)}, u32[]{:S(2)}) collective-permute-start(f32[2,16,256]{2,1,0:T(8,128)S(1)} %add.12), channel_id=1, source_target_pairs={{0,5},{1,4},{2,7},{3,6},{4,1},{5,0},{6,3},{7,2},{8,13},{9,12},{10,... | collective-permute-start | bytes 98312 | tf_op jit(solution)/shard_map/ppermute | solution.py:189
  26.8 1.0 %collective-permute-start.1 = (f32[2,16,256]{2,1,0:T(8,128)S(1)}, f32[2,16,256]{2,1,0:T(8,128)S(1)}, u32[]{:S(2)}, u32[]{:S(2)}) collective-permute-start(f32[2,16,256]{2,1,0:T(8,128)S(1)} %add.12), channel_id=1, source_target_pairs={{0,3},{1,2},{2,1},{3,0},{4,7},{5,6},{6,5},{7,4},{8,11},{9,10},{10,... | collective-permute-start | bytes 98312 | tf_op jit(solution)/shard_map/ppermute | solution.py:189
  27.8 1.3 %collective-permute-done.3 = f32[2,16,256]{2,1,0:T(8,128)S(1)} collective-permute-done((f32[2,16,256]{2,1,0:T(8,128)S(1)}, f32[2,16,256]{2,1,0:T(8,128)S(1)}, u32[]{:S(2)}, u32[]{:S(2)}) %collective-permute-start.3) | collective-permute-done | bytes 32800 | tf_op jit(solution)/shard_map/ppermute | solution.py:189
  29.1 0.6 %collective-permute-done.2 = f32[2,16,256]{2,1,0:T(8,128)S(1)} collective-permute-done((f32[2,16,256]{2,1,0:T(8,128)S(1)}, f32[2,16,256]{2,1,0:T(8,128)S(1)}, u32[]{:S(2)}, u32[]{:S(2)}) %collective-permute-start.2) | collective-permute-done | bytes 32800 | tf_op jit(solution)/shard_map/ppermute | solution.py:189
  29.7 0.5 %collective-permute-done.1 = f32[2,16,256]{2,1,0:T(8,128)S(1)} collective-permute-done((f32[2,16,256]{2,1,0:T(8,128)S(1)}, f32[2,16,256]{2,1,0:T(8,128)S(1)}, u32[]{:S(2)}, u32[]{:S(2)}) %collective-permute-start.1) | collective-permute-done | bytes 32800 | tf_op jit(solution)/shard_map/ppermute | solution.py:189
  30.1 1.6 %collective-permute-start.4 = (f32[2,16,256]{2,1,0:T(8,128)S(1)}, f32[2,16,256]{2,1,0:T(8,128)S(1)}, u32[]{:S(2)}, u32[]{:S(2)}) collective-permute-start(f32[2,16,256]{2,1,0:T(8,128)S(1)} %add_add_fusion.refs_0_), channel_id=1, source_target_pairs={{0,9},{1,8},{2,11},{3,10},{4,13},{5,12},{6,15},{7,14},{8,1},{9,0},... | collective-permute-start | bytes 98312 | tf_op jit(solution)/shard_map/ppermute | solution.py:189
  31.7 2.7 %collective-permute-done.4.refs_1_ = f32[2,16,256]{2,1,0:T(8,128)S(1)} collective-permute-done((f32[2,16,256]{2,1,0:T(8,128)S(1)}, f32[2,16,256]{2,1,0:T(8,128)S(1)}, u32[]{:S(2)}, u32[]{:S(2)}) %collective-permute-start.4) | collective-permute-done | bytes 32800 | tf_op jit(solution)/shard_map/ppermute | solution.py:189
  34.4 1.1 %shard_map.39 = f32[30,16,30]{2,1,0:T(8,128)} custom-call(f32[2,16,256]{2,1,0:T(8,128)S(1)} %add_add_fusion.refs_0_, f32[2,16,256]{2,1,0:T(8,128)S(1)} %collective-permute-done.4.refs_1_), custom_call_target="tpu_custom_call" | custom-call | tf_op jit(solution)/shard_map/pallas_call | solution.py:215
  (2 shorter events, 0.0 us)
Async XLA Ops:
  23.5 1.3 %collective-permute-start = (f32[2,16,256]{2,1,0:T(8,128)S(1)}, f32[2,16,256]{2,1,0:T(8,128)S(1)}, u32[]{:S(2)}, u32[]{:S(2)}) collective-permute-start(f32[2,16,256]{2,1,0:T(8,128)S(1)} %shard_map.38), channel_id=1, source_target_pairs={{0,1},{1,0},{2,3},{3,2},{4,5},{5,4},{6,7},{7,6},{8,9},{9,8},{10,11... | collective-permute-start | bytes 98312 | tf_op jit(solution)/shard_map/ppermute | solution.py:189
  24.8 4.2 %collective-permute-start.3 = (f32[2,16,256]{2,1,0:T(8,128)S(1)}, f32[2,16,256]{2,1,0:T(8,128)S(1)}, u32[]{:S(2)}, u32[]{:S(2)}) collective-permute-start(f32[2,16,256]{2,1,0:T(8,128)S(1)} %add.12), channel_id=1, source_target_pairs={{0,7},{1,6},{2,5},{3,4},{4,3},{5,2},{6,1},{7,0},{8,15},{9,14},{10,... | collective-permute-start | bytes 98312 | tf_op jit(solution)/shard_map/ppermute | solution.py:189
  26.3 3.3 %collective-permute-start.2 = (f32[2,16,256]{2,1,0:T(8,128)S(1)}, f32[2,16,256]{2,1,0:T(8,128)S(1)}, u32[]{:S(2)}, u32[]{:S(2)}) collective-permute-start(f32[2,16,256]{2,1,0:T(8,128)S(1)} %add.12), channel_id=1, source_target_pairs={{0,5},{1,4},{2,7},{3,6},{4,1},{5,0},{6,3},{7,2},{8,13},{9,12},{10,... | collective-permute-start | bytes 98312 | tf_op jit(solution)/shard_map/ppermute | solution.py:189
  26.8 3.3 %collective-permute-start.1 = (f32[2,16,256]{2,1,0:T(8,128)S(1)}, f32[2,16,256]{2,1,0:T(8,128)S(1)}, u32[]{:S(2)}, u32[]{:S(2)}) collective-permute-start(f32[2,16,256]{2,1,0:T(8,128)S(1)} %add.12), channel_id=1, source_target_pairs={{0,3},{1,2},{2,1},{3,0},{4,7},{5,6},{6,5},{7,4},{8,11},{9,10},{10,... | collective-permute-start | bytes 98312 | tf_op jit(solution)/shard_map/ppermute | solution.py:189
  30.1 4.3 %collective-permute-start.4 = (f32[2,16,256]{2,1,0:T(8,128)S(1)}, f32[2,16,256]{2,1,0:T(8,128)S(1)}, u32[]{:S(2)}, u32[]{:S(2)}) collective-permute-start(f32[2,16,256]{2,1,0:T(8,128)S(1)} %add_add_fusion.refs_0_), channel_id=1, source_target_pairs={{0,9},{1,8},{2,11},{3,10},{4,13},{5,12},{6,15},{7,14},{8,1},{9,0},... | collective-permute-start | bytes 98312 | tf_op jit(solution)/shard_map/ppermute | solution.py:189

commit v9 on v8

--- a/solution.py
+++ b/solution.py
@@ -1,3 +1,5 @@
+import math
+
 import numpy as np
 import ml_dtypes
 import jax
@@ -63,8 +65,7 @@
 
 
 def value_of(coded, scale):
-    size = (jnp.log2(jnp.abs(coded)) - LOWEST) * scale
-    return jnp.where(coded < 0.0, -size, size)
+    return (jnp.log2(jnp.abs(coded)) - LOWEST) * jnp.where(coded < 0.0, -scale, scale)
 
 
 def transform_kernel(block_hbm, table_hbm, weight_hbm, out_ref, root_ref, block_ref, table_ref, weight_ref, sems):
@@ -77,28 +78,32 @@
     for copy in copies:
         copy.wait()
     table = table_ref[...]
-    extras = []
-    for c in range(components):
-        block = block_ref[c]
-        rows = jnp.dot(table, jnp.concatenate([block] * 2, axis=0), preferred_element_type=jnp.float32)
-        sizes = jnp.abs(rows)
-        top = sizes[:, 0:LANES]
-        for d in range(1, points // LANES):
-            top = jnp.maximum(top, sizes[:, d * LANES : (d + 1) * LANES])
-        halves = jnp.ceil(2.0 * jnp.log2(jnp.maximum(jnp.max(top, axis=0, keepdims=True), SMALLEST)))
-        scale = jnp.exp2(halves * -0.5) * spread(c)
-        scale, halves = (jnp.concatenate([x] * (points // LANES), axis=1) for x in (scale, halves))
-        coded = coded_of(rows, sizes, scale)
-        for d in range(points // LANES):
-            out_ref[d, c * MAIN : (c + 1) * MAIN] = coded[0:MAIN, d * LANES : (d + 1) * LANES].astype(jnp.bfloat16)
-        whole = rows[32:33] * SMALL_SUM
-        high = whole.astype(jnp.bfloat16).astype(jnp.float32)
-        rest = whole - high
-        extras += [high, coded_of(rest, jnp.abs(rest), scale), coded[35:37], halves]
-    extras.append(jnp.zeros((1, points), jnp.float32))
-    extras = jnp.concatenate(extras, axis=0).astype(jnp.bfloat16)
-    for d in range(points // LANES):
-        out_ref[d, components * MAIN :] = extras[:, d * LANES : (d + 1) * LANES]
+    place = lax.broadcasted_iota(jnp.int32, (8, 1), 0)
+    many = math.gcd(points // LANES, 4)
+    wide = many * LANES
+    for p in range(points // wide):
+        extras = []
+        for c in range(components):
+            block = block_ref[c, :, p * wide : (p + 1) * wide]
+            rows = jnp.dot(table, jnp.concatenate([block] * 2, axis=0), preferred_element_type=jnp.float32)
+            sizes = jnp.abs(rows)
+            top = sizes[:, 0:LANES]
+            for d in range(1, many):
+                top = jnp.maximum(top, sizes[:, d * LANES : (d + 1) * LANES])
+            halves = jnp.ceil(2.0 * jnp.log2(jnp.maximum(jnp.max(top, axis=0, keepdims=True), SMALLEST)))
+            scale = jnp.exp2(halves * -0.5) * spread(c)
+            scale, halves = (jnp.concatenate([x] * many, axis=1) for x in (scale, halves))
+            whole = rows[32:33] * SMALL_SUM
+            high = whole.astype(jnp.bfloat16).astype(jnp.float32)
+            rows = jnp.concatenate([rows[0:32], jnp.where(place == 1, whole - high, rows[32:40])], axis=0)
+            coded = coded_of(rows, jnp.abs(rows), scale)
+            for d in range(many):
+                out_ref[p * many + d, c * MAIN : (c + 1) * MAIN] = coded[0:MAIN, d * LANES : (d + 1) * LANES].astype(jnp.bfloat16)
+            extras += [high, coded[33:34], coded[35:37], halves]
+        extras.append(jnp.zeros((1, wide), jnp.float32))
+        extras = jnp.concatenate(extras, axis=0).astype(jnp.bfloat16)
+        for d in range(many):
+            out_ref[p * many + d, components * MAIN :] = extras[:, d * LANES : (d + 1) * LANES]
     root_ref[...] = jnp.sqrt(weight_ref[...])
 
 

time: 35.8 us -> 35.6 us (level)
  no operation moved by 1% of the time
where the time goes in v9:
time: 35.6 us; the launch traced here: 35.5 us
  blocking collectives  20.4 us (57%)
  waiting for transfers between devices  6.15 us (17%)
  starting transfers between devices  4.74 us (13%)
  Pallas kernels  4.12 us (12%)
    all_to_all x1, blocking collectives, local(): lax.all_to_all(rows, 'space', split_axis=0, concat_axis=0, axis_index_gro...  20.4 us
    ppermute x5, waiting for transfers between devices, partners(): lax.ppermute(value, axis, [(i, i ^ step) for i in range(size)])  6.15 us
    ppermute x5, starting transfers between devices, partners(): lax.ppermute(value, axis, [(i, i ^ step) for i in range(size)])  4.74 us
    pallas_call x1, Pallas kernels, transform(): pl.pallas_call(transform_kernel, in_specs=[pl.BlockSpec(memory_space=pltp...  1.75 us
    pallas_call x1, Pallas kernels, local_gram(): pl.pallas_call(lambda *refs: gram_kernel(steps_all, offsets, *refs), out_...  1.22 us
    pallas_call x1, Pallas kernels, finish(): pl.pallas_call(finish_kernel, out_shape=jax.ShapeDtypeStruct((2 * NB, NF,...  1.14 us
  transfers between devices with their start and end apart: 5, of which 5 were waited for; matrix products, arithmetic and copies ran while one was open for 0% of the time, Pallas kernels for 0%

profile of v9, /device:TPU:0, one launch (start us, length us, event | category | flops | bytes accessed | tf_op | source)
XLA Modules:
  0.0 35.5 jit_solution(6364803540009054095)
XLA Ops:
  0.0 1.8 %shard_map.37 = (bf16[16,112,128]{2,1,0:T(8,128)(2,1)S(1)}, f32[1,128]{1,0:T(1,128)S(1)}) custom-call(bf16[3,64,2048]{2,1,0:T(8,128)(2,1)} %bitcast.3, bf16[40,128]{1,0:T(8,128)(2,1)} %constant.2.clone.table_hbm, f32[1,128]{1,0:T(1,128)} %bitcast.4), custom_call_target="tpu_custom_call" | custom-call | tf_op jit(solution)/shard_map/pallas_call | solution.py:165
  1.8 20.4 %all_to_all.5.refs_0_ = bf16[16,112,128]{2,1,0:T(8,128)(2,1)S(1)} all-to-all(bf16[16,112,128]{2,1,0:T(8,128)(2,1)S(1)} %get-tuple-element.7), channel_id=1, replica_groups=mesh['grp'=2,'space'=16] {'space'}, dimensions={0} | all-to-all | bytes 917504 | tf_op jit(solution)/shard_map/all_to_all | solution.py:252
  22.2 1.2 %shard_map.38 = f32[2,16,256]{2,1,0:T(8,128)S(1)} custom-call(bf16[16,112,128]{2,1,0:T(8,128)(2,1)S(1)} %all_to_all.5.refs_0_, f32[1,128]{1,0:T(1,128)S(1)} %get-tuple-element.8.refs_1_), custom_call_target="tpu_custom_call" | custom-call | tf_op jit(solution)/shard_map/pallas_call | solution.py:185
  23.4 0.2 collective-permute-start
  23.6 1.1 %collective-permute-done = f32[2,16,256]{2,1,0:T(8,128)S(1)} collective-permute-done((f32[2,16,256]{2,1,0:T(8,128)S(1)}, f32[2,16,256]{2,1,0:T(8,128)S(1)}, u32[]{:S(2)}, u32[]{:S(2)}) %collective-permute-start) | collective-permute-done | bytes 32800 | tf_op jit(solution)/shard_map/ppermute | solution.py:194
  24.7 1.5 %collective-permute-start.3 = (f32[2,16,256]{2,1,0:T(8,128)S(1)}, f32[2,16,256]{2,1,0:T(8,128)S(1)}, u32[]{:S(2)}, u32[]{:S(2)}) collective-permute-start(f32[2,16,256]{2,1,0:T(8,128)S(1)} %add.12), channel_id=1, source_target_pairs={{0,7},{1,6},{2,5},{3,4},{4,3},{5,2},{6,1},{7,0},{8,15},{9,14},{10,... | collective-permute-start | bytes 98312 | tf_op jit(solution)/shard_map/ppermute | solution.py:194
  26.2 0.5 %collective-permute-start.2 = (f32[2,16,256]{2,1,0:T(8,128)S(1)}, f32[2,16,256]{2,1,0:T(8,128)S(1)}, u32[]{:S(2)}, u32[]{:S(2)}) collective-permute-start(f32[2,16,256]{2,1,0:T(8,128)S(1)} %add.12), channel_id=1, source_target_pairs={{0,5},{1,4},{2,7},{3,6},{4,1},{5,0},{6,3},{7,2},{8,13},{9,12},{10,... | collective-permute-start | bytes 98312 | tf_op jit(solution)/shard_map/ppermute | solution.py:194
  26.7 1.0 %collective-permute-start.1 = (f32[2,16,256]{2,1,0:T(8,128)S(1)}, f32[2,16,256]{2,1,0:T(8,128)S(1)}, u32[]{:S(2)}, u32[]{:S(2)}) collective-permute-start(f32[2,16,256]{2,1,0:T(8,128)S(1)} %add.12), channel_id=1, source_target_pairs={{0,3},{1,2},{2,1},{3,0},{4,7},{5,6},{6,5},{7,4},{8,11},{9,10},{10,... | collective-permute-start | bytes 98312 | tf_op jit(solution)/shard_map/ppermute | solution.py:194
  27.7 1.3 %collective-permute-done.3 = f32[2,16,256]{2,1,0:T(8,128)S(1)} collective-permute-done((f32[2,16,256]{2,1,0:T(8,128)S(1)}, f32[2,16,256]{2,1,0:T(8,128)S(1)}, u32[]{:S(2)}, u32[]{:S(2)}) %collective-permute-start.3) | collective-permute-done | bytes 32800 | tf_op jit(solution)/shard_map/ppermute | solution.py:194
  28.9 0.6 %collective-permute-done.2 = f32[2,16,256]{2,1,0:T(8,128)S(1)} collective-permute-done((f32[2,16,256]{2,1,0:T(8,128)S(1)}, f32[2,16,256]{2,1,0:T(8,128)S(1)}, u32[]{:S(2)}, u32[]{:S(2)}) %collective-permute-start.2) | collective-permute-done | bytes 32800 | tf_op jit(solution)/shard_map/ppermute | solution.py:194
  29.5 0.5 %collective-permute-done.1 = f32[2,16,256]{2,1,0:T(8,128)S(1)} collective-permute-done((f32[2,16,256]{2,1,0:T(8,128)S(1)}, f32[2,16,256]{2,1,0:T(8,128)S(1)}, u32[]{:S(2)}, u32[]{:S(2)}) %collective-permute-start.1) | collective-permute-done | bytes 32800 | tf_op jit(solution)/shard_map/ppermute | solution.py:194
  30.0 1.6 %collective-permute-start.4 = (f32[2,16,256]{2,1,0:T(8,128)S(1)}, f32[2,16,256]{2,1,0:T(8,128)S(1)}, u32[]{:S(2)}, u32[]{:S(2)}) collective-permute-start(f32[2,16,256]{2,1,0:T(8,128)S(1)} %add_add_fusion.refs_0_), channel_id=1, source_target_pairs={{0,9},{1,8},{2,11},{3,10},{4,13},{5,12},{6,15},{7,14},{8,1},{9,0},... | collective-permute-start | bytes 98312 | tf_op jit(solution)/shard_map/ppermute | solution.py:194
  31.6 2.7 %collective-permute-done.4.refs_1_ = f32[2,16,256]{2,1,0:T(8,128)S(1)} collective-permute-done((f32[2,16,256]{2,1,0:T(8,128)S(1)}, f32[2,16,256]{2,1,0:T(8,128)S(1)}, u32[]{:S(2)}, u32[]{:S(2)}) %collective-permute-start.4) | collective-permute-done | bytes 32800 | tf_op jit(solution)/shard_map/ppermute | solution.py:194
  34.3 1.1 %shard_map.39 = f32[30,16,30]{2,1,0:T(8,128)} custom-call(f32[2,16,256]{2,1,0:T(8,128)S(1)} %add_add_fusion.refs_0_, f32[2,16,256]{2,1,0:T(8,128)S(1)} %collective-permute-done.4.refs_1_), custom_call_target="tpu_custom_call" | custom-call | tf_op jit(solution)/shard_map/pallas_call | solution.py:220
  (2 shorter events, 0.0 us)
Async XLA Ops:
  23.4 1.3 %collective-permute-start = (f32[2,16,256]{2,1,0:T(8,128)S(1)}, f32[2,16,256]{2,1,0:T(8,128)S(1)}, u32[]{:S(2)}, u32[]{:S(2)}) collective-permute-start(f32[2,16,256]{2,1,0:T(8,128)S(1)} %shard_map.38), channel_id=1, source_target_pairs={{0,1},{1,0},{2,3},{3,2},{4,5},{5,4},{6,7},{7,6},{8,9},{9,8},{10,11... | collective-permute-start | bytes 98312 | tf_op jit(solution)/shard_map/ppermute | solution.py:194
  24.7 4.2 %collective-permute-start.3 = (f32[2,16,256]{2,1,0:T(8,128)S(1)}, f32[2,16,256]{2,1,0:T(8,128)S(1)}, u32[]{:S(2)}, u32[]{:S(2)}) collective-permute-start(f32[2,16,256]{2,1,0:T(8,128)S(1)} %add.12), channel_id=1, source_target_pairs={{0,7},{1,6},{2,5},{3,4},{4,3},{5,2},{6,1},{7,0},{8,15},{9,14},{10,... | collective-permute-start | bytes 98312 | tf_op jit(solution)/shard_map/ppermute | solution.py:194
  26.2 3.3 %collective-permute-start.2 = (f32[2,16,256]{2,1,0:T(8,128)S(1)}, f32[2,16,256]{2,1,0:T(8,128)S(1)}, u32[]{:S(2)}, u32[]{:S(2)}) collective-permute-start(f32[2,16,256]{2,1,0:T(8,128)S(1)} %add.12), channel_id=1, source_target_pairs={{0,5},{1,4},{2,7},{3,6},{4,1},{5,0},{6,3},{7,2},{8,13},{9,12},{10,... | collective-permute-start | bytes 98312 | tf_op jit(solution)/shard_map/ppermute | solution.py:194
  26.7 3.3 %collective-permute-start.1 = (f32[2,16,256]{2,1,0:T(8,128)S(1)}, f32[2,16,256]{2,1,0:T(8,128)S(1)}, u32[]{:S(2)}, u32[]{:S(2)}) collective-permute-start(f32[2,16,256]{2,1,0:T(8,128)S(1)} %add.12), channel_id=1, source_target_pairs={{0,3},{1,2},{2,1},{3,0},{4,7},{5,6},{6,5},{7,4},{8,11},{9,10},{10,... | collective-permute-start | bytes 98312 | tf_op jit(solution)/shard_map/ppermute | solution.py:194
  30.0 4.3 %collective-permute-start.4 = (f32[2,16,256]{2,1,0:T(8,128)S(1)}, f32[2,16,256]{2,1,0:T(8,128)S(1)}, u32[]{:S(2)}, u32[]{:S(2)}) collective-permute-start(f32[2,16,256]{2,1,0:T(8,128)S(1)} %add_add_fusion.refs_0_), channel_id=1, source_target_pairs={{0,9},{1,8},{2,11},{3,10},{4,13},{5,12},{6,15},{7,14},{8,1},{9,0},... | collective-permute-start | bytes 98312 | tf_op jit(solution)/shard_map/ppermute | solution.py:194

commit v10 on v7

--- a/solution.py
+++ b/solution.py
@@ -17,8 +17,6 @@
 EXTRA = 5
 ROWS = 40
 SMALLEST = 2.0**-60
-SMALL_SUM = 1024.0
-LOWEST, STEEP = -14.0, 29.9
 VMEM = 48 * 1024 * 1024
 
 
@@ -30,7 +28,7 @@
     table = np.zeros((ROWS, HALF))
     table[0:NF] = re0[1 : NF + 1]
     table[NF : 2 * NF] = im0[1 : NF + 1]
-    table[32] = 1.0 / SMALL_SUM
+    table[32] = 1.0
     table[35] = re0[NF + 1]
     table[36] = im0[NF + 1]
     return table, (offset_re.tolist(), offset_im.tolist())
@@ -67,25 +65,19 @@
     for copy in copies:
         copy.wait()
     table = table_ref[...]
+    top = jnp.max(jnp.abs(block_ref[...].astype(jnp.float32)), axis=(0, 1, 2), keepdims=True)[0]
+    power = jnp.floor(jnp.log2(jnp.maximum(top, SMALLEST)))
     extras = []
     for c in range(components):
         block = block_ref[c]
         rows = jnp.dot(table, jnp.concatenate([block] * 2, axis=0), preferred_element_type=jnp.float32)
-        sizes = jnp.abs(rows)
-        top = sizes[:, 0:LANES]
-        for d in range(1, points // LANES):
-            top = jnp.maximum(top, sizes[:, d * LANES : (d + 1) * LANES])
-        eighths = jnp.ceil(8.0 * jnp.log2(jnp.maximum(jnp.max(top, axis=0, keepdims=True), SMALLEST)))
-        scale = jnp.exp2(eighths * -0.125) * spread(c)
-        scale, eighths = (jnp.concatenate([x] * (points // LANES), axis=1) for x in (scale, eighths))
-        coded = jnp.exp2(sizes * (scale * STEEP) + LOWEST)
-        coded = jnp.where(rows < 0.0, -coded, coded)
+        scale = jnp.concatenate([jnp.exp2(7.0 - power) * spread(c)] * (points // LANES), axis=1)
+        rows = rows * scale
         for d in range(points // LANES):
-            out_ref[d, c * MAIN : (c + 1) * MAIN] = coded[0:MAIN, d * LANES : (d + 1) * LANES]
-        whole = rows[32:33] * (scale * SMALL_SUM)
-        shifted = whole * 8193.0
-        high = shifted - (shifted - whole)
-        extras += [high, whole - high, coded[35:37], eighths]
+            out_ref[d, c * MAIN : (c + 1) * MAIN] = rows[0:MAIN, d * LANES : (d + 1) * LANES]
+        shifted = rows[32:33] * 8193.0
+        high = shifted - (shifted - rows[32:33])
+        extras += [high, rows[32:33] - high, rows[35:37], jnp.broadcast_to(power, (1, points))]
     extras.append(jnp.zeros((1, points), jnp.float32))
     extras = jnp.concatenate(extras, axis=0)
     for d in range(points // LANES):
@@ -102,15 +94,15 @@
     last = lax.broadcasted_iota(jnp.int32, (NH, LANES), 0) == NB
     for c in range(components):
         further = rows[extra + c * EXTRA : extra + (c + 1) * EXTRA]
-        scale = jnp.exp2(further[4] * 0.125) * (1.0 / spread(c))
+        scale = jnp.exp2(further[4] - 7.0) * (1.0 / spread(c))
         sums = (further[0] + further[1]) * scale
         delta = (sums * (1.0 / HALF) - jnp.sum(sums, axis=0, keepdims=True) * (1.0 / steps_all)) * root
-        scale = scale * (root * (1.0 / STEEP))
+        scale = scale * root
 
         def value(i, k):
             coded = rows[c * MAIN + i * NF + k - 1] if k <= NF else further[2 + i]
-            size = (jnp.log2(jnp.abs(coded)) - LOWEST) * scale
-            return jnp.where(coded < 0.0, -size, size) + (offsets[i][k] * delta if k % 2 else 0.0)
+            part = coded * scale
+            return part + offsets[i][k] * delta if k % 2 else part
 
         for i in range(2):
             before, here = (delta * float(HALF), jnp.zeros_like(delta))[i], value(i, 1)

time: 35.8 us -> 35.4 us (0.989)
  Pallas kernels: 4.14 us -> 3.71 us
where the time goes in v10:
time: 35.4 us; the launch traced here: 35.2 us
  blocking collectives  20.4 us (58%)
  waiting for transfers between devices  6.15 us (17%)
  starting transfers between devices  4.74 us (13%)
  Pallas kernels  3.71 us (10%)
    all_to_all x1, blocking collectives, local(): lax.all_to_all(rows.astype(jnp.float16), 'space', split_axis=0, concat_ax...  20.4 us
    ppermute x5, waiting for transfers between devices, partners(): lax.ppermute(value, axis, [(i, i ^ step) for i in range(size)])  6.15 us
    ppermute x5, starting transfers between devices, partners(): lax.ppermute(value, axis, [(i, i ^ step) for i in range(size)])  4.74 us
    pallas_call x1, Pallas kernels, transform(): pl.pallas_call(transform_kernel, in_specs=[pl.BlockSpec(memory_space=pltp...  1.53 us
    pallas_call x1, Pallas kernels, finish(): pl.pallas_call(finish_kernel, out_shape=jax.ShapeDtypeStruct((2 * NB, NF,...  1.14 us
    pallas_call x1, Pallas kernels, local_gram(): pl.pallas_call(lambda *refs: gram_kernel(steps_all, offsets, *refs), out_...  1.04 us
  transfers between devices with their start and end apart: 5, of which 5 were waited for; matrix products, arithmetic and copies ran while one was open for 0% of the time, Pallas kernels for 0%

profile of v10, /device:TPU:0, one launch (start us, length us, event | category | flops | bytes accessed | tf_op | source)
XLA Modules:
  0.0 35.2 jit_solution(848831396297746150)
XLA Ops:
  0.0 1.5 %shard_map.37 = (f32[16,112,128]{2,1,0:T(8,128)S(1)}, f32[1,128]{1,0:T(1,128)S(1)}) custom-call(bf16[3,64,2048]{2,1,0:T(8,128)(2,1)} %bitcast.3, bf16[40,128]{1,0:T(8,128)(2,1)} %constant.2.clone.table_hbm, f32[1,128]{1,0:T(1,128)} %bitcast.4), custom_call_target="tpu_custom_call" | custom-call | tf_op jit(solution)/shard_map/pallas_call | solution.py:144
  1.5 0.1 convert_element_type.6
  1.6 20.4 %all_to_all.5 = f16[16,112,128]{2,1,0:T(8,128)(2,1)S(1)} all-to-all(f16[16,112,128]{2,1,0:T(8,128)(2,1)S(1)} %convert_element_type.6), channel_id=1, replica_groups=mesh['grp'=2,'space'=16] {'space'}, dimensions={0} | all-to-all | bytes 917504 | tf_op jit(solution)/shard_map/all_to_all | solution.py:231
  22.0 0.1 convert_element_type.7.refs_0_
  22.1 1.0 %shard_map.38 = f32[2,16,256]{2,1,0:T(8,128)S(1)} custom-call(f32[16,112,128]{2,1,0:T(8,128)S(1)} %convert_element_type.7.refs_0_, f32[1,128]{1,0:T(1,128)S(1)} %get-tuple-element.8.refs_1_), custom_call_target="tpu_custom_call" | custom-call | tf_op jit(solution)/shard_map/pallas_call | solution.py:164
  23.1 0.2 collective-permute-start
  23.3 1.1 %collective-permute-done = f32[2,16,256]{2,1,0:T(8,128)S(1)} collective-permute-done((f32[2,16,256]{2,1,0:T(8,128)S(1)}, f32[2,16,256]{2,1,0:T(8,128)S(1)}, u32[]{:S(2)}, u32[]{:S(2)}) %collective-permute-start) | collective-permute-done | bytes 32800 | tf_op jit(solution)/shard_map/ppermute | solution.py:173
  24.4 1.5 %collective-permute-start.3 = (f32[2,16,256]{2,1,0:T(8,128)S(1)}, f32[2,16,256]{2,1,0:T(8,128)S(1)}, u32[]{:S(2)}, u32[]{:S(2)}) collective-permute-start(f32[2,16,256]{2,1,0:T(8,128)S(1)} %add.12), channel_id=1, source_target_pairs={{0,7},{1,6},{2,5},{3,4},{4,3},{5,2},{6,1},{7,0},{8,15},{9,14},{10,... | collective-permute-start | bytes 98312 | tf_op jit(solution)/shard_map/ppermute | solution.py:173
  25.9 0.5 %collective-permute-start.2 = (f32[2,16,256]{2,1,0:T(8,128)S(1)}, f32[2,16,256]{2,1,0:T(8,128)S(1)}, u32[]{:S(2)}, u32[]{:S(2)}) collective-permute-start(f32[2,16,256]{2,1,0:T(8,128)S(1)} %add.12), channel_id=1, source_target_pairs={{0,5},{1,4},{2,7},{3,6},{4,1},{5,0},{6,3},{7,2},{8,13},{9,12},{10,... | collective-permute-start | bytes 98312 | tf_op jit(solution)/shard_map/ppermute | solution.py:173
  26.4 1.0 %collective-permute-start.1 = (f32[2,16,256]{2,1,0:T(8,128)S(1)}, f32[2,16,256]{2,1,0:T(8,128)S(1)}, u32[]{:S(2)}, u32[]{:S(2)}) collective-permute-start(f32[2,16,256]{2,1,0:T(8,128)S(1)} %add.12), channel_id=1, source_target_pairs={{0,3},{1,2},{2,1},{3,0},{4,7},{5,6},{6,5},{7,4},{8,11},{9,10},{10,... | collective-permute-start | bytes 98312 | tf_op jit(solution)/shard_map/ppermute | solution.py:173
  27.4 1.3 %collective-permute-done.3 = f32[2,16,256]{2,1,0:T(8,128)S(1)} collective-permute-done((f32[2,16,256]{2,1,0:T(8,128)S(1)}, f32[2,16,256]{2,1,0:T(8,128)S(1)}, u32[]{:S(2)}, u32[]{:S(2)}) %collective-permute-start.3) | collective-permute-done | bytes 32800 | tf_op jit(solution)/shard_map/ppermute | solution.py:173
  28.7 0.6 %collective-permute-done.2 = f32[2,16,256]{2,1,0:T(8,128)S(1)} collective-permute-done((f32[2,16,256]{2,1,0:T(8,128)S(1)}, f32[2,16,256]{2,1,0:T(8,128)S(1)}, u32[]{:S(2)}, u32[]{:S(2)}) %collective-permute-start.2) | collective-permute-done | bytes 32800 | tf_op jit(solution)/shard_map/ppermute | solution.py:173
  29.2 0.5 %collective-permute-done.1 = f32[2,16,256]{2,1,0:T(8,128)S(1)} collective-permute-done((f32[2,16,256]{2,1,0:T(8,128)S(1)}, f32[2,16,256]{2,1,0:T(8,128)S(1)}, u32[]{:S(2)}, u32[]{:S(2)}) %collective-permute-start.1) | collective-permute-done | bytes 32800 | tf_op jit(solution)/shard_map/ppermute | solution.py:173
  29.7 1.6 %collective-permute-start.4 = (f32[2,16,256]{2,1,0:T(8,128)S(1)}, f32[2,16,256]{2,1,0:T(8,128)S(1)}, u32[]{:S(2)}, u32[]{:S(2)}) collective-permute-start(f32[2,16,256]{2,1,0:T(8,128)S(1)} %add_add_fusion.refs_0_), channel_id=1, source_target_pairs={{0,9},{1,8},{2,11},{3,10},{4,13},{5,12},{6,15},{7,14},{8,1},{9,0},... | collective-permute-start | bytes 98312 | tf_op jit(solution)/shard_map/ppermute | solution.py:173
  31.3 2.7 %collective-permute-done.4.refs_1_ = f32[2,16,256]{2,1,0:T(8,128)S(1)} collective-permute-done((f32[2,16,256]{2,1,0:T(8,128)S(1)}, f32[2,16,256]{2,1,0:T(8,128)S(1)}, u32[]{:S(2)}, u32[]{:S(2)}) %collective-permute-start.4) | collective-permute-done | bytes 32800 | tf_op jit(solution)/shard_map/ppermute | solution.py:173
  34.0 1.1 %shard_map.39 = f32[30,16,30]{2,1,0:T(8,128)} custom-call(f32[2,16,256]{2,1,0:T(8,128)S(1)} %add_add_fusion.refs_0_, f32[2,16,256]{2,1,0:T(8,128)S(1)} %collective-permute-done.4.refs_1_), custom_call_target="tpu_custom_call" | custom-call | tf_op jit(solution)/shard_map/pallas_call | solution.py:199
  (2 shorter events, 0.0 us)
Async XLA Ops:
  23.1 1.3 %collective-permute-start = (f32[2,16,256]{2,1,0:T(8,128)S(1)}, f32[2,16,256]{2,1,0:T(8,128)S(1)}, u32[]{:S(2)}, u32[]{:S(2)}) collective-permute-start(f32[2,16,256]{2,1,0:T(8,128)S(1)} %shard_map.38), channel_id=1, source_target_pairs={{0,1},{1,0},{2,3},{3,2},{4,5},{5,4},{6,7},{7,6},{8,9},{9,8},{10,11... | collective-permute-start | bytes 98312 | tf_op jit(solution)/shard_map/ppermute | solution.py:173
  24.4 4.2 %collective-permute-start.3 = (f32[2,16,256]{2,1,0:T(8,128)S(1)}, f32[2,16,256]{2,1,0:T(8,128)S(1)}, u32[]{:S(2)}, u32[]{:S(2)}) collective-permute-start(f32[2,16,256]{2,1,0:T(8,128)S(1)} %add.12), channel_id=1, source_target_pairs={{0,7},{1,6},{2,5},{3,4},{4,3},{5,2},{6,1},{7,0},{8,15},{9,14},{10,... | collective-permute-start | bytes 98312 | tf_op jit(solution)/shard_map/ppermute | solution.py:173
  25.9 3.3 %collective-permute-start.2 = (f32[2,16,256]{2,1,0:T(8,128)S(1)}, f32[2,16,256]{2,1,0:T(8,128)S(1)}, u32[]{:S(2)}, u32[]{:S(2)}) collective-permute-start(f32[2,16,256]{2,1,0:T(8,128)S(1)} %add.12), channel_id=1, source_target_pairs={{0,5},{1,4},{2,7},{3,6},{4,1},{5,0},{6,3},{7,2},{8,13},{9,12},{10,... | collective-permute-start | bytes 98312 | tf_op jit(solution)/shard_map/ppermute | solution.py:173
  26.4 3.3 %collective-permute-start.1 = (f32[2,16,256]{2,1,0:T(8,128)S(1)}, f32[2,16,256]{2,1,0:T(8,128)S(1)}, u32[]{:S(2)}, u32[]{:S(2)}) collective-permute-start(f32[2,16,256]{2,1,0:T(8,128)S(1)} %add.12), channel_id=1, source_target_pairs={{0,3},{1,2},{2,1},{3,0},{4,7},{5,6},{6,5},{7,4},{8,11},{9,10},{10,... | collective-permute-start | bytes 98312 | tf_op jit(solution)/shard_map/ppermute | solution.py:173
  29.7 4.3 %collective-permute-start.4 = (f32[2,16,256]{2,1,0:T(8,128)S(1)}, f32[2,16,256]{2,1,0:T(8,128)S(1)}, u32[]{:S(2)}, u32[]{:S(2)}) collective-permute-start(f32[2,16,256]{2,1,0:T(8,128)S(1)} %add_add_fusion.refs_0_), channel_id=1, source_target_pairs={{0,9},{1,8},{2,11},{3,10},{4,13},{5,12},{6,15},{7,14},{8,1},{9,0},... | collective-permute-start | bytes 98312 | tf_op jit(solution)/shard_map/ppermute | solution.py:173

commit v11 on v9

--- a/solution.py
+++ b/solution.py
@@ -15,6 +15,7 @@
 HALF = NFFT // 2
 NH = NB + 1
 LANES = 128
+ORDER = (11, 10, 5, 4, 12, 15, 2, 14, 9, 13, 7, 1, 0, 6, 8, 3)
 MAIN = 2 * NF
 EXTRA = 5
 ROWS = 40
@@ -79,6 +80,7 @@
         copy.wait()
     table = table_ref[...]
     place = lax.broadcasted_iota(jnp.int32, (8, 1), 0)
+    place_of = [ORDER.index(h) for h in range(points // LANES)]
     many = math.gcd(points // LANES, 4)
     wide = many * LANES
     for p in range(points // wide):
@@ -98,12 +100,12 @@
             rows = jnp.concatenate([rows[0:32], jnp.where(place == 1, whole - high, rows[32:40])], axis=0)
             coded = coded_of(rows, jnp.abs(rows), scale)
             for d in range(many):
-                out_ref[p * many + d, c * MAIN : (c + 1) * MAIN] = coded[0:MAIN, d * LANES : (d + 1) * LANES].astype(jnp.bfloat16)
+                out_ref[place_of[p * many + d], c * MAIN : (c + 1) * MAIN] = coded[0:MAIN, d * LANES : (d + 1) * LANES].astype(jnp.bfloat16)
             extras += [high, coded[33:34], coded[35:37], halves]
         extras.append(jnp.zeros((1, wide), jnp.float32))
         extras = jnp.concatenate(extras, axis=0).astype(jnp.bfloat16)
         for d in range(many):
-            out_ref[p * many + d, components * MAIN :] = extras[:, d * LANES : (d + 1) * LANES]
+            out_ref[place_of[p * many + d], components * MAIN :] = extras[:, d * LANES : (d + 1) * LANES]
     root_ref[...] = jnp.sqrt(weight_ref[...])
 
 
@@ -111,7 +113,8 @@
     components = (rows_ref.shape[1] - 1) // (MAIN + EXTRA)
     extra = components * MAIN
     group = NF // 2
-    rows = jnp.transpose(rows_ref[...].astype(jnp.float32), (1, 0, 2))
+    rows = jnp.stack([rows_ref[ORDER.index(h)] for h in range(NH)])
+    rows = jnp.transpose(rows.astype(jnp.float32), (1, 0, 2))
     root = root_ref[...]
     last = lax.broadcasted_iota(jnp.int32, (NH, LANES), 0) == NB
     for c in range(components):
@@ -241,13 +244,12 @@
         steps, components, points = snapshots.shape
         share = HALF // steps
         block = jnp.transpose(snapshots, (1, 0, 2))
-        across = None
+        across = [[h * share + i for h in ORDER] for i in range(share)]
         if share > 1:
             block = block.reshape(components, steps, NH, share, -1)
             teams = [[h * share + i for i in range(share)] for h in range(NH)]
             block = lax.all_to_all(block, "space", split_axis=3, concat_axis=1, axis_index_groups=teams, tiled=True)
             block = block.reshape(components, HALF, -1)
-            across = [[h * share + i for h in range(NH)] for i in range(share)]
         rows, root = transform(block, weights)
         rows = lax.all_to_all(rows, "space", split_axis=0, concat_axis=0, axis_index_groups=across, tiled=True)
         gram = local_gram(rows, root, n_space * steps)

time: 35.6 us -> 33.4 us (0.938)
  blocking collectives: 20.4 us -> 18.3 us
  waiting for transfers between devices: 6.15 us -> 5.52 us
  starting transfers between devices: 4.74 us -> 5.21 us
    all_to_all x1, blocking collectives: 20.4 us -> 18.3 us  [local(): lax.all_to_all(rows, 'space', split_axis=0, concat_axis=0, axis_index_gro...]
    ppermute x5, waiting for transfers between devices: 6.15 us -> 5.52 us  [partners(): lax.ppermute(value, axis, [(i, i ^ step) for i in range(size)])]
    ppermute x5, starting transfers between devices: 4.74 us -> 5.21 us  [partners(): lax.ppermute(value, axis, [(i, i ^ step) for i in range(size)])]
  transfers between devices with their start and end apart: 5 -> 5, of which waited for: 5 -> 4; matrix products, arithmetic and copies ran while one was open for 0% -> 0% of each run, Pallas kernels for 0% -> 0%
where the time goes in v11:
time: 33.4 us; the launch traced here: 33.2 us
  blocking collectives  18.3 us (55%)
  waiting for transfers between devices  5.52 us (17%)
  starting transfers between devices  5.21 us (16%)
  Pallas kernels  4.12 us (12%)
    all_to_all x1, blocking collectives, local(): lax.all_to_all(rows, 'space', split_axis=0, concat_axis=0, axis_index_gro...  18.3 us
    ppermute x5, waiting for transfers between devices, partners(): lax.ppermute(value, axis, [(i, i ^ step) for i in range(size)])  5.52 us
    ppermute x5, starting transfers between devices, partners(): lax.ppermute(value, axis, [(i, i ^ step) for i in range(size)])  5.21 us
    pallas_call x1, Pallas kernels, transform(): pl.pallas_call(transform_kernel, in_specs=[pl.BlockSpec(memory_space=pltp...  1.75 us
    pallas_call x1, Pallas kernels, local_gram(): pl.pallas_call(lambda *refs: gram_kernel(steps_all, offsets, *refs), out_...  1.22 us
    pallas_call x1, Pallas kernels, finish(): pl.pallas_call(finish_kernel, out_shape=jax.ShapeDtypeStruct((2 * NB, NF,...  1.14 us
  transfers between devices with their start and end apart: 5, of which 4 were waited for; matrix products, arithmetic and copies ran while one was open for 0% of the time, Pallas kernels for 0%

profile of v11, /device:TPU:0, one launch (start us, length us, event | category | flops | bytes accessed | tf_op | source)
XLA Modules:
  0.0 33.2 jit_solution(12818001259668164639)
XLA Ops:
  0.0 1.8 %shard_map.37 = (bf16[16,112,128]{2,1,0:T(8,128)(2,1)S(1)}, f32[1,128]{1,0:T(1,128)S(1)}) custom-call(bf16[3,64,2048]{2,1,0:T(8,128)(2,1)} %bitcast.3, bf16[40,128]{1,0:T(8,128)(2,1)} %constant.2.clone.table_hbm, f32[1,128]{1,0:T(1,128)} %bitcast.4), custom_call_target="tpu_custom_call" | custom-call | tf_op jit(solution)/shard_map/pallas_call | solution.py:168
  1.8 18.3 %all_to_all.5.refs_0_ = bf16[16,112,128]{2,1,0:T(8,128)(2,1)S(1)} all-to-all(bf16[16,112,128]{2,1,0:T(8,128)(2,1)S(1)} %get-tuple-element.7), channel_id=1, replica_groups={{11,10,5,4,12,15,2,14,9,13,7,1,0,6,8,3},{27,26,21,20,28,31,18,30,25,29,..., dimensions={0} | all-to-all | bytes 917504 | tf_op jit(solution)/shard_map/all_to_all | solution.py:254
  20.1 1.2 %shard_map.38 = f32[2,16,256]{2,1,0:T(8,128)S(1)} custom-call(bf16[16,112,128]{2,1,0:T(8,128)(2,1)S(1)} %all_to_all.5.refs_0_, f32[1,128]{1,0:T(1,128)S(1)} %get-tuple-element.8.refs_1_), custom_call_target="tpu_custom_call" | custom-call | tf_op jit(solution)/shard_map/pallas_call | solution.py:188
  21.3 0.2 collective-permute-start
  21.5 1.1 %collective-permute-done = f32[2,16,256]{2,1,0:T(8,128)S(1)} collective-permute-done((f32[2,16,256]{2,1,0:T(8,128)S(1)}, f32[2,16,256]{2,1,0:T(8,128)S(1)}, u32[]{:S(2)}, u32[]{:S(2)}) %collective-permute-start) | collective-permute-done | bytes 32800 | tf_op jit(solution)/shard_map/ppermute | solution.py:197
  22.6 1.8 %collective-permute-start.3 = (f32[2,16,256]{2,1,0:T(8,128)S(1)}, f32[2,16,256]{2,1,0:T(8,128)S(1)}, u32[]{:S(2)}, u32[]{:S(2)}) collective-permute-start(f32[2,16,256]{2,1,0:T(8,128)S(1)} %add.12), channel_id=1, source_target_pairs={{0,7},{1,6},{2,5},{3,4},{4,3},{5,2},{6,1},{7,0},{8,15},{9,14},{10,... | collective-permute-start | bytes 98312 | tf_op jit(solution)/shard_map/ppermute | solution.py:197
  24.4 0.0 collective-permute-start.2
  24.4 1.2 %collective-permute-start.1 = (f32[2,16,256]{2,1,0:T(8,128)S(1)}, f32[2,16,256]{2,1,0:T(8,128)S(1)}, u32[]{:S(2)}, u32[]{:S(2)}) collective-permute-start(f32[2,16,256]{2,1,0:T(8,128)S(1)} %add.12), channel_id=1, source_target_pairs={{0,3},{1,2},{2,1},{3,0},{4,7},{5,6},{6,5},{7,4},{8,11},{9,10},{10,... | collective-permute-start | bytes 98312 | tf_op jit(solution)/shard_map/ppermute | solution.py:197
  25.6 1.3 %collective-permute-done.3 = f32[2,16,256]{2,1,0:T(8,128)S(1)} collective-permute-done((f32[2,16,256]{2,1,0:T(8,128)S(1)}, f32[2,16,256]{2,1,0:T(8,128)S(1)}, u32[]{:S(2)}, u32[]{:S(2)}) %collective-permute-start.3) | collective-permute-done | bytes 32800 | tf_op jit(solution)/shard_map/ppermute | solution.py:197
  26.8 0.9 %collective-permute-done.2 = f32[2,16,256]{2,1,0:T(8,128)S(1)} collective-permute-done((f32[2,16,256]{2,1,0:T(8,128)S(1)}, f32[2,16,256]{2,1,0:T(8,128)S(1)}, u32[]{:S(2)}, u32[]{:S(2)}) %collective-permute-start.2) | collective-permute-done | bytes 32800 | tf_op jit(solution)/shard_map/ppermute | solution.py:197
  27.7 0.0 collective-permute-done.1
  27.8 2.1 %collective-permute-start.4 = (f32[2,16,256]{2,1,0:T(8,128)S(1)}, f32[2,16,256]{2,1,0:T(8,128)S(1)}, u32[]{:S(2)}, u32[]{:S(2)}) collective-permute-start(f32[2,16,256]{2,1,0:T(8,128)S(1)} %add_add_fusion.refs_0_), channel_id=1, source_target_pairs={{0,9},{1,8},{2,11},{3,10},{4,13},{5,12},{6,15},{7,14},{8,1},{9,0},... | collective-permute-start | bytes 98312 | tf_op jit(solution)/shard_map/ppermute | solution.py:197
  29.8 2.2 %collective-permute-done.4.refs_1_ = f32[2,16,256]{2,1,0:T(8,128)S(1)} collective-permute-done((f32[2,16,256]{2,1,0:T(8,128)S(1)}, f32[2,16,256]{2,1,0:T(8,128)S(1)}, u32[]{:S(2)}, u32[]{:S(2)}) %collective-permute-start.4) | collective-permute-done | bytes 32800 | tf_op jit(solution)/shard_map/ppermute | solution.py:197
  32.1 1.1 %shard_map.39 = f32[30,16,30]{2,1,0:T(8,128)} custom-call(f32[2,16,256]{2,1,0:T(8,128)S(1)} %add_add_fusion.refs_0_, f32[2,16,256]{2,1,0:T(8,128)S(1)} %collective-permute-done.4.refs_1_), custom_call_target="tpu_custom_call" | custom-call | tf_op jit(solution)/shard_map/pallas_call | solution.py:223
  (2 shorter events, 0.0 us)
Async XLA Ops:
  21.3 1.3 %collective-permute-start = (f32[2,16,256]{2,1,0:T(8,128)S(1)}, f32[2,16,256]{2,1,0:T(8,128)S(1)}, u32[]{:S(2)}, u32[]{:S(2)}) collective-permute-start(f32[2,16,256]{2,1,0:T(8,128)S(1)} %shard_map.38), channel_id=1, source_target_pairs={{0,1},{1,0},{2,3},{3,2},{4,5},{5,4},{6,7},{7,6},{8,9},{9,8},{10,11... | collective-permute-start | bytes 98312 | tf_op jit(solution)/shard_map/ppermute | solution.py:197
  22.6 4.2 %collective-permute-start.3 = (f32[2,16,256]{2,1,0:T(8,128)S(1)}, f32[2,16,256]{2,1,0:T(8,128)S(1)}, u32[]{:S(2)}, u32[]{:S(2)}) collective-permute-start(f32[2,16,256]{2,1,0:T(8,128)S(1)} %add.12), channel_id=1, source_target_pairs={{0,7},{1,6},{2,5},{3,4},{4,3},{5,2},{6,1},{7,0},{8,15},{9,14},{10,... | collective-permute-start | bytes 98312 | tf_op jit(solution)/shard_map/ppermute | solution.py:197
  24.4 3.3 %collective-permute-start.2 = (f32[2,16,256]{2,1,0:T(8,128)S(1)}, f32[2,16,256]{2,1,0:T(8,128)S(1)}, u32[]{:S(2)}, u32[]{:S(2)}) collective-permute-start(f32[2,16,256]{2,1,0:T(8,128)S(1)} %add.12), channel_id=1, source_target_pairs={{0,5},{1,4},{2,7},{3,6},{4,1},{5,0},{6,3},{7,2},{8,13},{9,12},{10,... | collective-permute-start | bytes 98312 | tf_op jit(solution)/shard_map/ppermute | solution.py:197
  24.4 3.3 %collective-permute-start.1 = (f32[2,16,256]{2,1,0:T(8,128)S(1)}, f32[2,16,256]{2,1,0:T(8,128)S(1)}, u32[]{:S(2)}, u32[]{:S(2)}) collective-permute-start(f32[2,16,256]{2,1,0:T(8,128)S(1)} %add.12), channel_id=1, source_target_pairs={{0,3},{1,2},{2,1},{3,0},{4,7},{5,6},{6,5},{7,4},{8,11},{9,10},{10,... | collective-permute-start | bytes 98312 | tf_op jit(solution)/shard_map/ppermute | solution.py:197
  27.8 4.3 %collective-permute-start.4 = (f32[2,16,256]{2,1,0:T(8,128)S(1)}, f32[2,16,256]{2,1,0:T(8,128)S(1)}, u32[]{:S(2)}, u32[]{:S(2)}) collective-permute-start(f32[2,16,256]{2,1,0:T(8,128)S(1)} %add_add_fusion.refs_0_), channel_id=1, source_target_pairs={{0,9},{1,8},{2,11},{3,10},{4,13},{5,12},{6,15},{7,14},{8,1},{9,0},... | collective-permute-start | bytes 98312 | tf_op jit(solution)/shard_map/ppermute | solution.py:197

commit v12 on v11

--- a/solution.py
+++ b/solution.py
@@ -15,7 +15,7 @@
 HALF = NFFT // 2
 NH = NB + 1
 LANES = 128
-ORDER = (11, 10, 5, 4, 12, 15, 2, 14, 9, 13, 7, 1, 0, 6, 8, 3)
+ORDER = (11, 10, 7, 6, 15, 12, 2, 14, 9, 0, 1, 5, 13, 4, 8, 3)
 MAIN = 2 * NF
 EXTRA = 5
 ROWS = 40

time: 33.4 us -> 33.2 us (level)
  no operation moved by 1% of the time
where the time goes in v12:
time: 33.2 us; the launch traced here: 33 us
  blocking collectives  18.2 us (55%)
  waiting for transfers between devices  5.71 us (17%)
  starting transfers between devices  4.94 us (15%)
  Pallas kernels  4.11 us (12%)
    all_to_all x1, blocking collectives, local(): lax.all_to_all(rows, 'space', split_axis=0, concat_axis=0, axis_index_gro...  18.2 us
    ppermute x5, waiting for transfers between devices, partners(): lax.ppermute(value, axis, [(i, i ^ step) for i in range(size)])  5.71 us
    ppermute x5, starting transfers between devices, partners(): lax.ppermute(value, axis, [(i, i ^ step) for i in range(size)])  4.94 us
    pallas_call x1, Pallas kernels, transform(): pl.pallas_call(transform_kernel, in_specs=[pl.BlockSpec(memory_space=pltp...  1.75 us
    pallas_call x1, Pallas kernels, local_gram(): pl.pallas_call(lambda *refs: gram_kernel(steps_all, offsets, *refs), out_...  1.22 us
    pallas_call x1, Pallas kernels, finish(): pl.pallas_call(finish_kernel, out_shape=jax.ShapeDtypeStruct((2 * NB, NF,...  1.14 us
  transfers between devices with their start and end apart: 5, of which 4 were waited for; matrix products, arithmetic and copies ran while one was open for 0% of the time, Pallas kernels for 0%

profile of v12, /device:TPU:0, one launch (start us, length us, event | category | flops | bytes accessed | tf_op | source)
XLA Modules:
  0.0 33.0 jit_solution(15969006910604960407)
XLA Ops:
  0.0 1.8 %shard_map.37 = (bf16[16,112,128]{2,1,0:T(8,128)(2,1)S(1)}, f32[1,128]{1,0:T(1,128)S(1)}) custom-call(bf16[3,64,2048]{2,1,0:T(8,128)(2,1)} %bitcast.3, bf16[40,128]{1,0:T(8,128)(2,1)} %constant.2.clone.table_hbm, f32[1,128]{1,0:T(1,128)} %bitcast.4), custom_call_target="tpu_custom_call" | custom-call | tf_op jit(solution)/shard_map/pallas_call | solution.py:168
  1.8 18.2 %all_to_all.5.refs_0_ = bf16[16,112,128]{2,1,0:T(8,128)(2,1)S(1)} all-to-all(bf16[16,112,128]{2,1,0:T(8,128)(2,1)S(1)} %get-tuple-element.7), channel_id=1, replica_groups={{11,10,7,6,15,12,2,14,9,0,1,5,13,4,8,3},{27,26,23,22,31,28,18,30,25,16,..., dimensions={0} | all-to-all | bytes 917504 | tf_op jit(solution)/shard_map/all_to_all | solution.py:254
  20.0 1.2 %shard_map.38 = f32[2,16,256]{2,1,0:T(8,128)S(1)} custom-call(bf16[16,112,128]{2,1,0:T(8,128)(2,1)S(1)} %all_to_all.5.refs_0_, f32[1,128]{1,0:T(1,128)S(1)} %get-tuple-element.8.refs_1_), custom_call_target="tpu_custom_call" | custom-call | tf_op jit(solution)/shard_map/pallas_call | solution.py:188
  21.2 0.2 collective-permute-start
  21.4 1.1 %collective-permute-done = f32[2,16,256]{2,1,0:T(8,128)S(1)} collective-permute-done((f32[2,16,256]{2,1,0:T(8,128)S(1)}, f32[2,16,256]{2,1,0:T(8,128)S(1)}, u32[]{:S(2)}, u32[]{:S(2)}) %collective-permute-start) | collective-permute-done | bytes 32800 | tf_op jit(solution)/shard_map/ppermute | solution.py:197
  22.5 0.7 %collective-permute-start.3 = (f32[2,16,256]{2,1,0:T(8,128)S(1)}, f32[2,16,256]{2,1,0:T(8,128)S(1)}, u32[]{:S(2)}, u32[]{:S(2)}) collective-permute-start(f32[2,16,256]{2,1,0:T(8,128)S(1)} %add.12), channel_id=1, source_target_pairs={{0,7},{1,6},{2,5},{3,4},{4,3},{5,2},{6,1},{7,0},{8,15},{9,14},{10,... | collective-permute-start | bytes 98312 | tf_op jit(solution)/shard_map/ppermute | solution.py:197
  23.2 0.8 %collective-permute-start.2 = (f32[2,16,256]{2,1,0:T(8,128)S(1)}, f32[2,16,256]{2,1,0:T(8,128)S(1)}, u32[]{:S(2)}, u32[]{:S(2)}) collective-permute-start(f32[2,16,256]{2,1,0:T(8,128)S(1)} %add.12), channel_id=1, source_target_pairs={{0,5},{1,4},{2,7},{3,6},{4,1},{5,0},{6,3},{7,2},{8,13},{9,12},{10,... | collective-permute-start | bytes 98312 | tf_op jit(solution)/shard_map/ppermute | solution.py:197
  24.0 1.4 %collective-permute-start.1 = (f32[2,16,256]{2,1,0:T(8,128)S(1)}, f32[2,16,256]{2,1,0:T(8,128)S(1)}, u32[]{:S(2)}, u32[]{:S(2)}) collective-permute-start(f32[2,16,256]{2,1,0:T(8,128)S(1)} %add.12), channel_id=1, source_target_pairs={{0,3},{1,2},{2,1},{3,0},{4,7},{5,6},{6,5},{7,4},{8,11},{9,10},{10,... | collective-permute-start | bytes 98312 | tf_op jit(solution)/shard_map/ppermute | solution.py:197
  25.5 1.3 %collective-permute-done.3 = f32[2,16,256]{2,1,0:T(8,128)S(1)} collective-permute-done((f32[2,16,256]{2,1,0:T(8,128)S(1)}, f32[2,16,256]{2,1,0:T(8,128)S(1)}, u32[]{:S(2)}, u32[]{:S(2)}) %collective-permute-start.3) | collective-permute-done | bytes 32800 | tf_op jit(solution)/shard_map/ppermute | solution.py:197
  26.7 0.0 collective-permute-done.2
  26.7 0.8 %collective-permute-done.1 = f32[2,16,256]{2,1,0:T(8,128)S(1)} collective-permute-done((f32[2,16,256]{2,1,0:T(8,128)S(1)}, f32[2,16,256]{2,1,0:T(8,128)S(1)}, u32[]{:S(2)}, u32[]{:S(2)}) %collective-permute-start.1) | collective-permute-done | bytes 32800 | tf_op jit(solution)/shard_map/ppermute | solution.py:197
  27.5 1.8 %collective-permute-start.4 = (f32[2,16,256]{2,1,0:T(8,128)S(1)}, f32[2,16,256]{2,1,0:T(8,128)S(1)}, u32[]{:S(2)}, u32[]{:S(2)}) collective-permute-start(f32[2,16,256]{2,1,0:T(8,128)S(1)} %add_add_fusion.refs_0_), channel_id=1, source_target_pairs={{0,9},{1,8},{2,11},{3,10},{4,13},{5,12},{6,15},{7,14},{8,1},{9,0},... | collective-permute-start | bytes 98312 | tf_op jit(solution)/shard_map/ppermute | solution.py:197
  29.3 2.6 %collective-permute-done.4.refs_1_ = f32[2,16,256]{2,1,0:T(8,128)S(1)} collective-permute-done((f32[2,16,256]{2,1,0:T(8,128)S(1)}, f32[2,16,256]{2,1,0:T(8,128)S(1)}, u32[]{:S(2)}, u32[]{:S(2)}) %collective-permute-start.4) | collective-permute-done | bytes 32800 | tf_op jit(solution)/shard_map/ppermute | solution.py:197
  31.9 1.1 %shard_map.39 = f32[30,16,30]{2,1,0:T(8,128)} custom-call(f32[2,16,256]{2,1,0:T(8,128)S(1)} %add_add_fusion.refs_0_, f32[2,16,256]{2,1,0:T(8,128)S(1)} %collective-permute-done.4.refs_1_), custom_call_target="tpu_custom_call" | custom-call | tf_op jit(solution)/shard_map/pallas_call | solution.py:223
  (2 shorter events, 0.0 us)
Async XLA Ops:
  21.2 1.3 %collective-permute-start = (f32[2,16,256]{2,1,0:T(8,128)S(1)}, f32[2,16,256]{2,1,0:T(8,128)S(1)}, u32[]{:S(2)}, u32[]{:S(2)}) collective-permute-start(f32[2,16,256]{2,1,0:T(8,128)S(1)} %shard_map.38), channel_id=1, source_target_pairs={{0,1},{1,0},{2,3},{3,2},{4,5},{5,4},{6,7},{7,6},{8,9},{9,8},{10,11... | collective-permute-start | bytes 98312 | tf_op jit(solution)/shard_map/ppermute | solution.py:197
  22.5 4.2 %collective-permute-start.3 = (f32[2,16,256]{2,1,0:T(8,128)S(1)}, f32[2,16,256]{2,1,0:T(8,128)S(1)}, u32[]{:S(2)}, u32[]{:S(2)}) collective-permute-start(f32[2,16,256]{2,1,0:T(8,128)S(1)} %add.12), channel_id=1, source_target_pairs={{0,7},{1,6},{2,5},{3,4},{4,3},{5,2},{6,1},{7,0},{8,15},{9,14},{10,... | collective-permute-start | bytes 98312 | tf_op jit(solution)/shard_map/ppermute | solution.py:197
  23.2 3.5 %collective-permute-start.2 = (f32[2,16,256]{2,1,0:T(8,128)S(1)}, f32[2,16,256]{2,1,0:T(8,128)S(1)}, u32[]{:S(2)}, u32[]{:S(2)}) collective-permute-start(f32[2,16,256]{2,1,0:T(8,128)S(1)} %add.12), channel_id=1, source_target_pairs={{0,5},{1,4},{2,7},{3,6},{4,1},{5,0},{6,3},{7,2},{8,13},{9,12},{10,... | collective-permute-start | bytes 98312 | tf_op jit(solution)/shard_map/ppermute | solution.py:197
  24.0 3.5 %collective-permute-start.1 = (f32[2,16,256]{2,1,0:T(8,128)S(1)}, f32[2,16,256]{2,1,0:T(8,128)S(1)}, u32[]{:S(2)}, u32[]{:S(2)}) collective-permute-start(f32[2,16,256]{2,1,0:T(8,128)S(1)} %add.12), channel_id=1, source_target_pairs={{0,3},{1,2},{2,1},{3,0},{4,7},{5,6},{6,5},{7,4},{8,11},{9,10},{10,... | collective-permute-start | bytes 98312 | tf_op jit(solution)/shard_map/ppermute | solution.py:197
  27.5 4.4 %collective-permute-start.4 = (f32[2,16,256]{2,1,0:T(8,128)S(1)}, f32[2,16,256]{2,1,0:T(8,128)S(1)}, u32[]{:S(2)}, u32[]{:S(2)}) collective-permute-start(f32[2,16,256]{2,1,0:T(8,128)S(1)} %add_add_fusion.refs_0_), channel_id=1, source_target_pairs={{0,9},{1,8},{2,11},{3,10},{4,13},{5,12},{6,15},{7,14},{8,1},{9,0},... | collective-permute-start | bytes 98312 | tf_op jit(solution)/shard_map/ppermute | solution.py:197

commit v13 on v12

--- a/solution.py
+++ b/solution.py
@@ -15,7 +15,7 @@
 HALF = NFFT // 2
 NH = NB + 1
 LANES = 128
-ORDER = (11, 10, 7, 6, 15, 12, 2, 14, 9, 0, 1, 5, 13, 4, 8, 3)
+ORDER = (11, 10, 7, 6, 15, 12, 3, 2, 14, 9, 0, 1, 5, 13, 4, 8)
 MAIN = 2 * NF
 EXTRA = 5
 ROWS = 40
@@ -234,6 +234,7 @@
         wide = step == 2 and 4 * step <= size
         rounds.append([c + (step > 1) for c in ([step, 2 * step, 3 * step] if wide else [step])])
         step *= 4 if wide else 2
+    rounds.sort(key=len)
     for steps in rounds[:-1]:
         value = sum(partners(value, axis, size, steps), value)
     return [value] + partners(value, axis, size, rounds[-1])

time: 33.2 us -> 33.6 us (1.012); the launches traced: 33 us -> 33 us
  starting transfers between devices: 4.94 us -> 4.18 us
  waiting for transfers between devices: 5.71 us -> 6.47 us
    ppermute x5, waiting for transfers between devices: 5.71 us -> 6.47 us  [partners(): lax.ppermute(value, axis, [(i, i ^ step) for i in range(size)])]
    ppermute x5, starting transfers between devices: 4.94 us -> 4.18 us  [partners(): lax.ppermute(value, axis, [(i, i ^ step) for i in range(size)])]
  transfers between devices with their start and end apart: 5 -> 5, of which waited for: 4 -> 5; matrix products, arithmetic and copies ran while one was open for 0% -> 0% of each run, Pallas kernels for 0% -> 0%
where the time goes in v13:
time: 33.6 us; the launch traced here: 33 us
  blocking collectives  18.2 us (54%)
  waiting for transfers between devices  6.47 us (19%)
  starting transfers between devices  4.18 us (12%)
  Pallas kernels  4.12 us (12%)
    all_to_all x1, blocking collectives, local(): lax.all_to_all(rows, 'space', split_axis=0, concat_axis=0, axis_index_gro...  18.2 us
    ppermute x5, waiting for transfers between devices, partners(): lax.ppermute(value, axis, [(i, i ^ step) for i in range(size)])  6.47 us
    ppermute x5, starting transfers between devices, partners(): lax.ppermute(value, axis, [(i, i ^ step) for i in range(size)])  4.18 us
    pallas_call x1, Pallas kernels, transform(): pl.pallas_call(transform_kernel, in_specs=[pl.BlockSpec(memory_space=pltp...  1.75 us
    pallas_call x1, Pallas kernels, local_gram(): pl.pallas_call(lambda *refs: gram_kernel(steps_all, offsets, *refs), out_...  1.22 us
    pallas_call x1, Pallas kernels, finish(): pl.pallas_call(finish_kernel, out_shape=jax.ShapeDtypeStruct((2 * NB, NF,...  1.14 us
  transfers between devices with their start and end apart: 5, of which 5 were waited for; matrix products, arithmetic and copies ran while one was open for 0% of the time, Pallas kernels for 0%

profile of v13, /device:TPU:0, one launch (start us, length us, event | category | flops | bytes accessed | tf_op | source)
XLA Modules:
  0.0 33.0 jit_solution(3850022821599310951)
XLA Ops:
  0.0 1.8 %shard_map.37 = (bf16[16,112,128]{2,1,0:T(8,128)(2,1)S(1)}, f32[1,128]{1,0:T(1,128)S(1)}) custom-call(bf16[3,64,2048]{2,1,0:T(8,128)(2,1)} %bitcast.3, bf16[40,128]{1,0:T(8,128)(2,1)} %constant.2.clone.table_hbm, f32[1,128]{1,0:T(1,128)} %bitcast.4), custom_call_target="tpu_custom_call" | custom-call | tf_op jit(solution)/shard_map/pallas_call | solution.py:168
  1.8 18.2 %all_to_all.5.refs_0_ = bf16[16,112,128]{2,1,0:T(8,128)(2,1)S(1)} all-to-all(bf16[16,112,128]{2,1,0:T(8,128)(2,1)S(1)} %get-tuple-element.7), channel_id=1, replica_groups={{11,10,7,6,15,12,3,2,14,9,0,1,5,13,4,8},{27,26,23,22,31,28,19,18,30,25,..., dimensions={0} | all-to-all | bytes 917504 | tf_op jit(solution)/shard_map/all_to_all | solution.py:255
  20.0 1.2 %shard_map.38 = f32[2,16,256]{2,1,0:T(8,128)S(1)} custom-call(bf16[16,112,128]{2,1,0:T(8,128)(2,1)S(1)} %all_to_all.5.refs_0_, f32[1,128]{1,0:T(1,128)S(1)} %get-tuple-element.8.refs_1_), custom_call_target="tpu_custom_call" | custom-call | tf_op jit(solution)/shard_map/pallas_call | solution.py:188
  21.2 0.2 collective-permute-start
  21.4 1.1 %collective-permute-done = f32[2,16,256]{2,1,0:T(8,128)S(1)} collective-permute-done((f32[2,16,256]{2,1,0:T(8,128)S(1)}, f32[2,16,256]{2,1,0:T(8,128)S(1)}, u32[]{:S(2)}, u32[]{:S(2)}) %collective-permute-start) | collective-permute-done | bytes 32800 | tf_op jit(solution)/shard_map/ppermute | solution.py:197
  22.5 1.0 %collective-permute-start.1 = (f32[2,16,256]{2,1,0:T(8,128)S(1)}, f32[2,16,256]{2,1,0:T(8,128)S(1)}, u32[]{:S(2)}, u32[]{:S(2)}) collective-permute-start(f32[2,16,256]{2,1,0:T(8,128)S(1)} %add.6), channel_id=1, source_target_pairs={{0,9},{1,8},{2,11},{3,10},{4,13},{5,12},{6,15},{7,14},{8,1},{9,0},... | collective-permute-start | bytes 98312 | tf_op jit(solution)/shard_map/ppermute | solution.py:197
  23.5 3.2 %collective-permute-done.1 = f32[2,16,256]{2,1,0:T(8,128)S(1)} collective-permute-done((f32[2,16,256]{2,1,0:T(8,128)S(1)}, f32[2,16,256]{2,1,0:T(8,128)S(1)}, u32[]{:S(2)}, u32[]{:S(2)}) %collective-permute-start.1) | collective-permute-done | bytes 32800 | tf_op jit(solution)/shard_map/ppermute | solution.py:197
  26.7 1.0 %collective-permute-start.4 = (f32[2,16,256]{2,1,0:T(8,128)S(1)}, f32[2,16,256]{2,1,0:T(8,128)S(1)}, u32[]{:S(2)}, u32[]{:S(2)}) collective-permute-start(f32[2,16,256]{2,1,0:T(8,128)S(1)} %add.7.refs_0_), channel_id=1, source_target_pairs={{0,7},{1,6},{2,5},{3,4},{4,3},{5,2},{6,1},{7,0},{8,15},{9,14},{10,... | collective-permute-start | bytes 98312 | tf_op jit(solution)/shard_map/ppermute | solution.py:197
  27.8 0.8 %collective-permute-start.3 = (f32[2,16,256]{2,1,0:T(8,128)S(1)}, f32[2,16,256]{2,1,0:T(8,128)S(1)}, u32[]{:S(2)}, u32[]{:S(2)}) collective-permute-start(f32[2,16,256]{2,1,0:T(8,128)S(1)} %add.7.refs_0_), channel_id=1, source_target_pairs={{0,5},{1,4},{2,7},{3,6},{4,1},{5,0},{6,3},{7,2},{8,13},{9,12},{10,... | collective-permute-start | bytes 98312 | tf_op jit(solution)/shard_map/ppermute | solution.py:197
  28.5 1.2 %collective-permute-start.2 = (f32[2,16,256]{2,1,0:T(8,128)S(1)}, f32[2,16,256]{2,1,0:T(8,128)S(1)}, u32[]{:S(2)}, u32[]{:S(2)}) collective-permute-start(f32[2,16,256]{2,1,0:T(8,128)S(1)} %add.7.refs_0_), channel_id=1, source_target_pairs={{0,3},{1,2},{2,1},{3,0},{4,7},{5,6},{6,5},{7,4},{8,11},{9,10},{10,... | collective-permute-start | bytes 98312 | tf_op jit(solution)/shard_map/ppermute | solution.py:197
  29.7 1.2 %collective-permute-done.4.refs_3_ = f32[2,16,256]{2,1,0:T(8,128)S(1)} collective-permute-done((f32[2,16,256]{2,1,0:T(8,128)S(1)}, f32[2,16,256]{2,1,0:T(8,128)S(1)}, u32[]{:S(2)}, u32[]{:S(2)}) %collective-permute-start.4) | collective-permute-done | bytes 32800 | tf_op jit(solution)/shard_map/ppermute | solution.py:197
  31.0 0.4 %collective-permute-done.3.refs_2_ = f32[2,16,256]{2,1,0:T(8,128)S(1)} collective-permute-done((f32[2,16,256]{2,1,0:T(8,128)S(1)}, f32[2,16,256]{2,1,0:T(8,128)S(1)}, u32[]{:S(2)}, u32[]{:S(2)}) %collective-permute-start.3) | collective-permute-done | bytes 32800 | tf_op jit(solution)/shard_map/ppermute | solution.py:197
  31.4 0.5 %collective-permute-done.2.refs_1_ = f32[2,16,256]{2,1,0:T(8,128)S(1)} collective-permute-done((f32[2,16,256]{2,1,0:T(8,128)S(1)}, f32[2,16,256]{2,1,0:T(8,128)S(1)}, u32[]{:S(2)}, u32[]{:S(2)}) %collective-permute-start.2) | collective-permute-done | bytes 32800 | tf_op jit(solution)/shard_map/ppermute | solution.py:197
  31.9 1.1 %shard_map.39 = f32[30,16,30]{2,1,0:T(8,128)} custom-call(f32[2,16,256]{2,1,0:T(8,128)S(1)} %add.7.refs_0_, f32[2,16,256]{2,1,0:T(8,128)S(1)} %collective-permute-done.2.refs_1_, f32[2,16,256]{2,1,0:T(8,128)S(1)} %collective-permute-done.3.refs_2_, f32[2,16,256]{2,1,0:T(8,128)S(1)} %collective-permute-done.4.refs_3_), custom_call_target="tpu_custom_call" | custom-call | tf_op jit(solution)/shard_map/pallas_call | solution.py:223
  (2 shorter events, 0.0 us)
Async XLA Ops:
  21.2 1.3 %collective-permute-start = (f32[2,16,256]{2,1,0:T(8,128)S(1)}, f32[2,16,256]{2,1,0:T(8,128)S(1)}, u32[]{:S(2)}, u32[]{:S(2)}) collective-permute-start(f32[2,16,256]{2,1,0:T(8,128)S(1)} %shard_map.38), channel_id=1, source_target_pairs={{0,1},{1,0},{2,3},{3,2},{4,5},{5,4},{6,7},{7,6},{8,9},{9,8},{10,11... | collective-permute-start | bytes 98312 | tf_op jit(solution)/shard_map/ppermute | solution.py:197
  22.5 4.2 %collective-permute-start.1 = (f32[2,16,256]{2,1,0:T(8,128)S(1)}, f32[2,16,256]{2,1,0:T(8,128)S(1)}, u32[]{:S(2)}, u32[]{:S(2)}) collective-permute-start(f32[2,16,256]{2,1,0:T(8,128)S(1)} %add.6), channel_id=1, source_target_pairs={{0,9},{1,8},{2,11},{3,10},{4,13},{5,12},{6,15},{7,14},{8,1},{9,0},... | collective-permute-start | bytes 98312 | tf_op jit(solution)/shard_map/ppermute | solution.py:197
  26.7 4.2 %collective-permute-start.4 = (f32[2,16,256]{2,1,0:T(8,128)S(1)}, f32[2,16,256]{2,1,0:T(8,128)S(1)}, u32[]{:S(2)}, u32[]{:S(2)}) collective-permute-start(f32[2,16,256]{2,1,0:T(8,128)S(1)} %add.7.refs_0_), channel_id=1, source_target_pairs={{0,7},{1,6},{2,5},{3,4},{4,3},{5,2},{6,1},{7,0},{8,15},{9,14},{10,... | collective-permute-start | bytes 98312 | tf_op jit(solution)/shard_map/ppermute | solution.py:197
  27.8 3.6 %collective-permute-start.3 = (f32[2,16,256]{2,1,0:T(8,128)S(1)}, f32[2,16,256]{2,1,0:T(8,128)S(1)}, u32[]{:S(2)}, u32[]{:S(2)}) collective-permute-start(f32[2,16,256]{2,1,0:T(8,128)S(1)} %add.7.refs_0_), channel_id=1, source_target_pairs={{0,5},{1,4},{2,7},{3,6},{4,1},{5,0},{6,3},{7,2},{8,13},{9,12},{10,... | collective-permute-start | bytes 98312 | tf_op jit(solution)/shard_map/ppermute | solution.py:197
  28.5 3.3 %collective-permute-start.2 = (f32[2,16,256]{2,1,0:T(8,128)S(1)}, f32[2,16,256]{2,1,0:T(8,128)S(1)}, u32[]{:S(2)}, u32[]{:S(2)}) collective-permute-start(f32[2,16,256]{2,1,0:T(8,128)S(1)} %add.7.refs_0_), channel_id=1, source_target_pairs={{0,3},{1,2},{2,1},{3,0},{4,7},{5,6},{6,5},{7,4},{8,11},{9,10},{10,... | collective-permute-start | bytes 98312 | tf_op jit(solution)/shard_map/ppermute | solution.py:197
